TPU v7x, 32 devices: a whole 2x2x4 slice. The times are simulated.
32 devices in a mesh: section: 4 (over z), shard: 8 (over y, x, core).
Axes of the slice: x: 2, y: 2, z: 4, core: 2. Of those that a mesh axis runs over, the one named last changes fastest.
Arguments:
- tokens: bfloat16 [4, 16, 8192], P(None, 'shard'), may hold values from -6 to 6
- lengths: int32 [4], replicated, may hold values from 1 to 16, 40 in all
- norm_gain: float32 [4, 8192], P('section'), may hold values from 0.25 to 1.75
- gate_tiles: bfloat16 [4, 128, 28, 128, 128], P('section', 'shard'), may hold values from -0.09375 to 0.09375
- up_tiles: bfloat16 [4, 128, 28, 128, 128], P('section', 'shard'), may hold values from -0.09375 to 0.09375
- in_index: int32 [4, 128, 28], P('section', 'shard'), may hold values from -1 to 63, as said below
- down_tiles: bfloat16 [4, 128, 28, 128, 128], P('section', 'shard'), may hold values from -0.0625 to 0.0625
- out_index: int32 [4, 128, 28], P('section', 'shard'), may hold values from -1 to 63, as said below
Outputs:
- hidden_states: bfloat16 [4, 4, 16, 8192], P('section', None, 'shard')
Inputs may be any that keep to these rules, and one draw needn't show every extreme that they name: `in_index`: each list of 28 slots holds distinct block numbers first and -1 in the slots after them; at least 21 slots of every list hold a block number, and in each layer some list holds 28. `out_index`: each list of 28 slots holds distinct block numbers first and -1 in the slots after them; at least 21 slots of every list hold a block number, and in each layer some list holds 28.
All inputs are finite; a program needn't handle non-finite values.
Results may differ from a plain program's by a relative error of at most 0.035.
Values may be sent and summed in bfloat16 or wider, within the bound.
No kernel may reach another device: no remote copies, remote signals or barrier semaphores. Data moves between devices by JAX's collectives and lax.ppermute only.
A program may use at most 192 MiB of HBM per device.

v0:
```python
import jax
import jax.numpy as jnp
from jax import lax
from jax.sharding import PartitionSpec as P

norm_eps = 1e-05


def shifted(value, axis, by):
    size = lax.axis_size(axis)
    pairs = [(i, i + by) for i in range(size) if 0 <= i + by < size]
    return lax.ppermute(value, axis, pairs)


def body(tokens, lengths, norm_gain, gate_tiles, up_tiles, in_index, down_tiles, out_index):
    micro_count, own_count, model_width = tokens.shape
    gain_row = norm_gain[0]
    gate_local = gate_tiles[0]
    up_local = up_tiles[0]
    down_local = down_tiles[0]
    in_local = in_index[0]
    out_local = out_index[0]
    block_size = gate_local.shape[-1]
    block_total = model_width // block_size
    local_blocks = gate_local.shape[0]
    section_id = lax.axis_index("section")
    section_total = lax.axis_size("section")
    shard_id = lax.axis_index("shard")
    in_valid = (in_local >= 0).astype(jnp.bfloat16)
    in_clamped = jnp.maximum(in_local, 0)
    onehot = (
        out_local[:, :, None] == jnp.arange(block_total, dtype=jnp.int32)[None, None, :]
    ).astype(jnp.bfloat16)
    dense_down = jnp.einsum(
        "hkb,hkcf->hcbf", onehot, down_local, preferred_element_type=jnp.bfloat16
    )
    dense_down = dense_down.reshape(local_blocks * block_size, model_width)
    pieces = 1
    unit_rows = own_count // pieces
    unit_count = micro_count * pieces
    turn_count = unit_count + section_total - 1

    def expand(rows_piece):
        row_count = rows_piece.shape[0]
        column_blocks = rows_piece.reshape(row_count, block_total, block_size)
        picked = jnp.take(column_blocks, in_clamped, axis=1) * in_valid[None, :, :, None]
        gate_val = jnp.einsum(
            "nhkc,hkcf->nhf", picked, gate_local, preferred_element_type=jnp.float32
        )
        up_val = jnp.einsum("nhkc,hkcf->nhf", picked, up_local, preferred_element_type=jnp.float32)
        return (
            (jax.nn.silu(gate_val) * up_val)
            .astype(jnp.bfloat16)
            .reshape(row_count, local_blocks * block_size)
        )

    def turn_step(turn, state_pair):
        incoming, stored = state_pair
        unit_id = turn - section_id
        active = (unit_id >= 0) & (unit_id < unit_count)
        unit_clamped = jnp.clip(unit_id, 0, unit_count - 1)
        micro_id = unit_clamped // pieces
        offset = unit_clamped % pieces * unit_rows
        own_rows = lax.dynamic_slice(tokens, (micro_id, offset, 0), (1, unit_rows, model_width))[0]
        arrived = jnp.where(section_id == 0, own_rows, incoming)
        widened = arrived.astype(jnp.float32)
        scale_row = lax.rsqrt(jnp.mean(widened * widened, axis=-1, keepdims=True) + norm_eps)
        normed = (widened * scale_row * gain_row[None, :]).astype(jnp.bfloat16)
        hidden = expand(lax.all_gather(normed, "shard", axis=0, tiled=True))
        summed = lax.psum_scatter(
            jnp.dot(hidden, dense_down, preferred_element_type=jnp.float32).astype(jnp.bfloat16),
            "shard",
            scatter_dimension=0,
            tiled=True,
        ).astype(jnp.float32)
        row_ids = shard_id * own_count + offset + jnp.arange(unit_rows, dtype=jnp.int32)
        keep_row = row_ids < lengths[micro_id]
        result_rows = jnp.where(keep_row[:, None], widened + summed, jnp.float32(0.0)).astype(
            jnp.bfloat16
        )
        updated = lax.dynamic_update_slice(stored, result_rows[None], (micro_id, offset, 0))
        stored = jnp.where(active, updated, stored)
        incoming = shifted(result_rows, "section", 1)
        return (incoming, stored)

    initial = (
        jnp.zeros((unit_rows, model_width), jnp.bfloat16),
        jnp.zeros((micro_count, own_count, model_width), jnp.bfloat16),
    )
    _, stored = lax.fori_loop(0, turn_count, turn_step, initial)
    return stored[None]


def solution(mesh):
    placed = (
        P(None, "shard", None),
        P(),
        P("section", None),
        P("section", "shard", None, None, None),
        P("section", "shard", None, None, None),
        P("section", "shard", None),
        P("section", "shard", None, None, None),
        P("section", "shard", None),
    )
    return jax.shard_map(
        body,
        mesh=mesh,
        in_specs=placed,
        out_specs=P("section", None, "shard", None),
        check_vma=False,
    )
```

profile of v0, /device:TPU:24, one launch (start us, length us, event | category | flops | bytes accessed | tf_op | source)
XLA Modules:
  0.0 761.8 jit_solution(634545095158423982)
XLA Ops:
  6.5 21.1 %fusion.34 = bf16[16,64,128,128]{3,1,2,0:T(8,128)(2,1)} fusion(bf16[16,28,128,128]{3,2,1,0:T(8,128)(2,1)} %bitcast.110, s32[16,28]{1,0:T(8,128)} %bitcast.112), kind=kOutput, calls=%fused_computation.39 | convolution fusion | flops 939552768 | bytes 48236288 | tf_op jit(solution)/shard_map/hkb,hkcf->hcbf/dot_general | solution.py:34
  27.7 36.3 %copy.31 = bf16[256,8,64,128]{3,1,2,0:T(8,128)(2,1)} copy(bf16[256,8,64,128]{3,2,1,0:T(8,128)(2,1)} %bitcast.107) | data formatting | bytes 67108864
  64.1 690.2 %while.17 = (s32[]{:T(128)}, bf16[2,8192]{1,0:T(2,128)(2,1)S(1)}, bf16[4,2,8192]{2,1,0:T(2,128)(2,1)S(1)}, s32[]{:T(128)}, s32[]{:T(128)}, /*index=5*/s32[4]{0:T...) while((s32[]{:T(128)}, bf16[2,8192]{1,0:T(2,128)(2,1)S(1)}, ...), condition=%wide.region_3.4_spmd, body=%wide.region_0.3_spmd.sunk | while | flops 1010996160 | bytes 133058840 | solution.py:90
  65.5 9.3 %all-gather.2 = bf16[8,2,8192]{2,1,0:T(2,128)(2,1)S(1)} all-gather(bf16[1,2,8192]{2,1,0:T(2,128)(2,1)S(1)} %fusion.62), channel_id=1, replica_groups=mesh['section'=4,'shard'=8] {'shard'}, dimensions={0}, use_global_device_ids=true | all-gather | bytes 294912 | tf_op jit(solution)/shard_map/while/body/eval_jaxpr/all_gather | solution.py:69
  77.3 6.5 fusion.63
  89.4 13.6 %convolution_convert_fusion.2 = bf16[16,8192]{1,0:T(8,128)(2,1)} fusion(bf16[2048,8192]{1,0:T(8,128)(2,1)} %get-tuple-element.504, bf16[16,2,8,128]{3,2,1,0:T(8,128)(2,1)S(1)} %fusion.64), kind=kOutput, calls=%fused_computation.1.clone.1 | convolution fusion | flops 537001984 | bytes 33882112 | tf_op jit(solution)/shard_map/while/body/eval_jaxpr/dot_general | solution.py:71
  105.3 51.4 %all-reduce.5.cloned.1.call-done = bf16[16,8192]{1,0:T(8,128)(2,1)} async-done(((bf16[16,8192]{1,0:T(8,128)(2,1)}), bf16[16,8192]{1,0:T(8,128)(2,1)}) %all-reduce.5.cloned.1.call-update) | async-done | bytes 262160 | tf_op jit(solution)/shard_map/while
  159.1 4.5 collective-permute-done
  164.7 8.6 %all-gather.2 = bf16[8,2,8192]{2,1,0:T(2,128)(2,1)S(1)} all-gather(bf16[1,2,8192]{2,1,0:T(2,128)(2,1)S(1)} %fusion.62), channel_id=1, replica_groups=mesh['section'=4,'shard'=8] {'shard'}, dimensions={0}, use_global_device_ids=true | all-gather | bytes 294912 | tf_op jit(solution)/shard_map/while/body/eval_jaxpr/all_gather | solution.py:69
  175.8 6.5 fusion.63
  187.9 13.6 %convolution_convert_fusion.2 = bf16[16,8192]{1,0:T(8,128)(2,1)} fusion(bf16[2048,8192]{1,0:T(8,128)(2,1)} %get-tuple-element.504, bf16[16,2,8,128]{3,2,1,0:T(8,128)(2,1)S(1)} %fusion.64), kind=kOutput, calls=%fused_computation.1.clone.1 | convolution fusion | flops 537001984 | bytes 33882112 | tf_op jit(solution)/shard_map/while/body/eval_jaxpr/dot_general | solution.py:71
  203.8 51.4 %all-reduce.5.cloned.1.call-done = bf16[16,8192]{1,0:T(8,128)(2,1)} async-done(((bf16[16,8192]{1,0:T(8,128)(2,1)}), bf16[16,8192]{1,0:T(8,128)(2,1)}) %all-reduce.5.cloned.1.call-update) | async-done | bytes 262160 | tf_op jit(solution)/shard_map/while
  263.1 8.6 %all-gather.2 = bf16[8,2,8192]{2,1,0:T(2,128)(2,1)S(1)} all-gather(bf16[1,2,8192]{2,1,0:T(2,128)(2,1)S(1)} %fusion.62), channel_id=1, replica_groups=mesh['section'=4,'shard'=8] {'shard'}, dimensions={0}, use_global_device_ids=true | all-gather | bytes 294912 | tf_op jit(solution)/shard_map/while/body/eval_jaxpr/all_gather | solution.py:69
  274.2 6.5 fusion.63
  286.3 13.6 %convolution_convert_fusion.2 = bf16[16,8192]{1,0:T(8,128)(2,1)} fusion(bf16[2048,8192]{1,0:T(8,128)(2,1)} %get-tuple-element.504, bf16[16,2,8,128]{3,2,1,0:T(8,128)(2,1)S(1)} %fusion.64), kind=kOutput, calls=%fused_computation.1.clone.1 | convolution fusion | flops 537001984 | bytes 33882112 | tf_op jit(solution)/shard_map/while/body/eval_jaxpr/dot_general | solution.py:71
  302.2 51.4 %all-reduce.5.cloned.1.call-done = bf16[16,8192]{1,0:T(8,128)(2,1)} async-done(((bf16[16,8192]{1,0:T(8,128)(2,1)}), bf16[16,8192]{1,0:T(8,128)(2,1)}) %all-reduce.5.cloned.1.call-update) | async-done | bytes 262160 | tf_op jit(solution)/shard_map/while
  361.6 8.6 %all-gather.2 = bf16[8,2,8192]{2,1,0:T(2,128)(2,1)S(1)} all-gather(bf16[1,2,8192]{2,1,0:T(2,128)(2,1)S(1)} %fusion.62), channel_id=1, replica_groups=mesh['section'=4,'shard'=8] {'shard'}, dimensions={0}, use_global_device_ids=true | all-gather | bytes 294912 | tf_op jit(solution)/shard_map/while/body/eval_jaxpr/all_gather | solution.py:69
  372.7 6.5 fusion.63
  384.8 13.6 %convolution_convert_fusion.2 = bf16[16,8192]{1,0:T(8,128)(2,1)} fusion(bf16[2048,8192]{1,0:T(8,128)(2,1)} %get-tuple-element.504, bf16[16,2,8,128]{3,2,1,0:T(8,128)(2,1)S(1)} %fusion.64), kind=kOutput, calls=%fused_computation.1.clone.1 | convolution fusion | flops 537001984 | bytes 33882112 | tf_op jit(solution)/shard_map/while/body/eval_jaxpr/dot_general | solution.py:71
  400.7 51.4 %all-reduce.5.cloned.1.call-done = bf16[16,8192]{1,0:T(8,128)(2,1)} async-done(((bf16[16,8192]{1,0:T(8,128)(2,1)}), bf16[16,8192]{1,0:T(8,128)(2,1)}) %all-reduce.5.cloned.1.call-update) | async-done | bytes 262160 | tf_op jit(solution)/shard_map/while
  460.0 8.6 %all-gather.2 = bf16[8,2,8192]{2,1,0:T(2,128)(2,1)S(1)} all-gather(bf16[1,2,8192]{2,1,0:T(2,128)(2,1)S(1)} %fusion.62), channel_id=1, replica_groups=mesh['section'=4,'shard'=8] {'shard'}, dimensions={0}, use_global_device_ids=true | all-gather | bytes 294912 | tf_op jit(solution)/shard_map/while/body/eval_jaxpr/all_gather | solution.py:69
  471.2 6.5 fusion.63
  483.3 13.6 %convolution_convert_fusion.2 = bf16[16,8192]{1,0:T(8,128)(2,1)} fusion(bf16[2048,8192]{1,0:T(8,128)(2,1)} %get-tuple-element.504, bf16[16,2,8,128]{3,2,1,0:T(8,128)(2,1)S(1)} %fusion.64), kind=kOutput, calls=%fused_computation.1.clone.1 | convolution fusion | flops 537001984 | bytes 33882112 | tf_op jit(solution)/shard_map/while/body/eval_jaxpr/dot_general | solution.py:71
  499.2 51.4 %all-reduce.5.cloned.1.call-done = bf16[16,8192]{1,0:T(8,128)(2,1)} async-done(((bf16[16,8192]{1,0:T(8,128)(2,1)}), bf16[16,8192]{1,0:T(8,128)(2,1)}) %all-reduce.5.cloned.1.call-update) | async-done | bytes 262160 | tf_op jit(solution)/shard_map/while
  558.5 8.6 %all-gather.2 = bf16[8,2,8192]{2,1,0:T(2,128)(2,1)S(1)} all-gather(bf16[1,2,8192]{2,1,0:T(2,128)(2,1)S(1)} %fusion.62), channel_id=1, replica_groups=mesh['section'=4,'shard'=8] {'shard'}, dimensions={0}, use_global_device_ids=true | all-gather | bytes 294912 | tf_op jit(solution)/shard_map/while/body/eval_jaxpr/all_gather | solution.py:69
  569.6 6.5 fusion.63
  581.7 13.6 %convolution_convert_fusion.2 = bf16[16,8192]{1,0:T(8,128)(2,1)} fusion(bf16[2048,8192]{1,0:T(8,128)(2,1)} %get-tuple-element.504, bf16[16,2,8,128]{3,2,1,0:T(8,128)(2,1)S(1)} %fusion.64), kind=kOutput, calls=%fused_computation.1.clone.1 | convolution fusion | flops 537001984 | bytes 33882112 | tf_op jit(solution)/shard_map/while/body/eval_jaxpr/dot_general | solution.py:71
  597.6 51.4 %all-reduce.5.cloned.1.call-done = bf16[16,8192]{1,0:T(8,128)(2,1)} async-done(((bf16[16,8192]{1,0:T(8,128)(2,1)}), bf16[16,8192]{1,0:T(8,128)(2,1)}) %all-reduce.5.cloned.1.call-update) | async-done | bytes 262160 | tf_op jit(solution)/shard_map/while
  657.0 8.6 %all-gather.2 = bf16[8,2,8192]{2,1,0:T(2,128)(2,1)S(1)} all-gather(bf16[1,2,8192]{2,1,0:T(2,128)(2,1)S(1)} %fusion.62), channel_id=1, replica_groups=mesh['section'=4,'shard'=8] {'shard'}, dimensions={0}, use_global_device_ids=true | all-gather | bytes 294912 | tf_op jit(solution)/shard_map/while/body/eval_jaxpr/all_gather | solution.py:69
  668.1 6.5 fusion.63
  680.2 13.6 %convolution_convert_fusion.2 = bf16[16,8192]{1,0:T(8,128)(2,1)} fusion(bf16[2048,8192]{1,0:T(8,128)(2,1)} %get-tuple-element.504, bf16[16,2,8,128]{3,2,1,0:T(8,128)(2,1)S(1)} %fusion.64), kind=kOutput, calls=%fused_computation.1.clone.1 | convolution fusion | flops 537001984 | bytes 33882112 | tf_op jit(solution)/shard_map/while/body/eval_jaxpr/dot_general | solution.py:71
  696.1 51.4 %all-reduce.5.cloned.1.call-done = bf16[16,8192]{1,0:T(8,128)(2,1)} async-done(((bf16[16,8192]{1,0:T(8,128)(2,1)}), bf16[16,8192]{1,0:T(8,128)(2,1)}) %all-reduce.5.cloned.1.call-update) | async-done | bytes 262160 | tf_op jit(solution)/shard_map/while
  (160 shorter events, 119.7 us)
Async XLA Ops:
  27.7 36.3 %copy-start.2 = (s32[1,16,28]{2,1,0:T(8,128)S(1)}, s32[1,16,28]{2,1,0:T(8,128)}, u32[]{:S(2)}) copy-start(s32[1,16,28]{2,1,0:T(8,128)} %param.15) | copy-start | bytes 5380
  27.7 36.4 %copy-start = (f32[1,8192]{1,0:T(1,128)S(1)}, f32[1,8192]{1,0:T(1,128)}, u32[]{:S(2)}) copy-start(f32[1,8192]{1,0:T(1,128)} %param.12) | copy-start | bytes 98308
  27.7 36.4 %copy-start.4 = (s32[4]{0:T(128)S(1)}, s32[4]{0:T(128)}, u32[]{:S(2)}) copy-start(s32[4]{0:T(128)} %param.11) | copy-start | bytes 52
  27.7 36.5 %copy-start.5 = (u32[32]{0:T(128)S(1)}, u32[32]{0:T(128)}, u32[]{:S(2)}) copy-start(u32[32]{0:T(128)} %constant.219) | copy-start | bytes 388
  64.3 92.4 %all-reduce.5.cloned.1.call-start = ((), (), s32[]{:S(2)}) async-start(), calls=%async_computation | async-start | bytes 524288 | tf_op jit(solution)/shard_map/while
  77.3 9.4 %copy-start.3 = (bf16[16,28,128,128]{3,2,1,0:T(8,128)(2,1)S(1)}, bf16[16,28,128,128]{3,2,1,0:T(8,128)(2,1)}, u32[]{:S(2)}) copy-start(bf16[16,28,128,128]{3,2,1,0:T(8,128)(2,1)} %get-tuple-element.503) | copy-start | bytes 44040196 | tf_op jit(solution)/shard_map/while
  157.8 5.8 collective-permute-start
  163.6 91.6 %all-reduce.5.cloned.1.call-start = ((), (), s32[]{:S(2)}) async-start(), calls=%async_computation | async-start | bytes 524288 | tf_op jit(solution)/shard_map/while
  175.8 9.4 %copy-start.3 = (bf16[16,28,128,128]{3,2,1,0:T(8,128)(2,1)S(1)}, bf16[16,28,128,128]{3,2,1,0:T(8,128)(2,1)}, u32[]{:S(2)}) copy-start(bf16[16,28,128,128]{3,2,1,0:T(8,128)(2,1)} %get-tuple-element.503) | copy-start | bytes 44040196 | tf_op jit(solution)/shard_map/while
  256.2 5.8 collective-permute-start
  262.0 91.6 %all-reduce.5.cloned.1.call-start = ((), (), s32[]{:S(2)}) async-start(), calls=%async_computation | async-start | bytes 524288 | tf_op jit(solution)/shard_map/while
  274.2 9.4 %copy-start.3 = (bf16[16,28,128,128]{3,2,1,0:T(8,128)(2,1)S(1)}, bf16[16,28,128,128]{3,2,1,0:T(8,128)(2,1)}, u32[]{:S(2)}) copy-start(bf16[16,28,128,128]{3,2,1,0:T(8,128)(2,1)} %get-tuple-element.503) | copy-start | bytes 44040196 | tf_op jit(solution)/shard_map/while
  354.7 5.8 collective-permute-start
  360.5 91.6 %all-reduce.5.cloned.1.call-start = ((), (), s32[]{:S(2)}) async-start(), calls=%async_computation | async-start | bytes 524288 | tf_op jit(solution)/shard_map/while
  372.7 9.4 %copy-start.3 = (bf16[16,28,128,128]{3,2,1,0:T(8,128)(2,1)S(1)}, bf16[16,28,128,128]{3,2,1,0:T(8,128)(2,1)}, u32[]{:S(2)}) copy-start(bf16[16,28,128,128]{3,2,1,0:T(8,128)(2,1)} %get-tuple-element.503) | copy-start | bytes 44040196 | tf_op jit(solution)/shard_map/while
  453.1 5.8 collective-permute-start
  459.0 91.6 %all-reduce.5.cloned.1.call-start = ((), (), s32[]{:S(2)}) async-start(), calls=%async_computation | async-start | bytes 524288 | tf_op jit(solution)/shard_map/while
  471.1 9.4 %copy-start.3 = (bf16[16,28,128,128]{3,2,1,0:T(8,128)(2,1)S(1)}, bf16[16,28,128,128]{3,2,1,0:T(8,128)(2,1)}, u32[]{:S(2)}) copy-start(bf16[16,28,128,128]{3,2,1,0:T(8,128)(2,1)} %get-tuple-element.503) | copy-start | bytes 44040196 | tf_op jit(solution)/shard_map/while
  551.6 5.8 collective-permute-start
  557.4 91.6 %all-reduce.5.cloned.1.call-start = ((), (), s32[]{:S(2)}) async-start(), calls=%async_computation | async-start | bytes 524288 | tf_op jit(solution)/shard_map/while
  569.6 9.4 %copy-start.3 = (bf16[16,28,128,128]{3,2,1,0:T(8,128)(2,1)S(1)}, bf16[16,28,128,128]{3,2,1,0:T(8,128)(2,1)}, u32[]{:S(2)}) copy-start(bf16[16,28,128,128]{3,2,1,0:T(8,128)(2,1)} %get-tuple-element.503) | copy-start | bytes 44040196 | tf_op jit(solution)/shard_map/while
  650.1 5.8 collective-permute-start
  655.9 91.6 %all-reduce.5.cloned.1.call-start = ((), (), s32[]{:S(2)}) async-start(), calls=%async_computation | async-start | bytes 524288 | tf_op jit(solution)/shard_map/while
  668.1 9.4 %copy-start.3 = (bf16[16,28,128,128]{3,2,1,0:T(8,128)(2,1)S(1)}, bf16[16,28,128,128]{3,2,1,0:T(8,128)(2,1)}, u32[]{:S(2)}) copy-start(bf16[16,28,128,128]{3,2,1,0:T(8,128)(2,1)} %get-tuple-element.503) | copy-start | bytes 44040196 | tf_op jit(solution)/shard_map/while
  748.5 5.8 collective-permute-start
  754.3 0.7 copy-start.1
Sparse Core Ops, SparseCore 0:
  103.1 53.5 all-reduce.4
  201.6 53.5 all-reduce.4
  300.0 53.5 all-reduce.4
  398.5 53.5 all-reduce.4
  497.0 53.5 all-reduce.4
  595.4 53.5 all-reduce.4
  693.9 53.5 all-reduce.4
where the time goes:
time: 764 us; the launch traced here: 762 us
  waiting for transfers between devices  392 us (51%)
  matrix products  181 us (24%)
  local copies, waits for them, and re-layouts  81.8 us (11%)
  blocking collectives  61.1 us (8%)
  other arithmetic  18.7 us (2%)
  between operations  13.5 us (2%)
  starting transfers between devices  9.07 us (1%)
    while x14, waiting for transfers between devices  360 us
    dot_general x7, matrix products, turn_step(): jnp.dot(hidden, dense_down, preferred_element_type=jnp.float32)  94.9 us
    all_gather x7, blocking collectives, turn_step(): hidden = expand(lax.all_gather(normed, 'shard', axis=0, tiled=True))  61.1 us
    dot_general x7, matrix products, expand(): jnp.einsum('nhkc,hkcf->nhf', picked, gate_local, preferred_element_type=j...  45.8 us
    unnamed x11, local copies, waits for them, and re-layouts  37 us
    ppermute x7, waiting for transfers between devices, shifted(): return lax.ppermute(value, axis, pairs)  31.5 us
    while x21, local copies, waits for them, and re-layouts  23.6 us
    dot_general x1, matrix products, body(): jnp.einsum('hkb,hkcf->hcbf', onehot, down_local, preferred_element_type=j...  21.1 us
  transfers between devices with their start and end apart: 14, of which 14 were waited for; matrix products, arithmetic and copies ran while one was open for 2% of the time, Pallas kernels for 0%

commit v1 on v0

v1 whole, which is shorter than its diff:
```python
import functools

import jax
import jax.numpy as jnp
from jax import lax
from jax.experimental import pallas as pl
from jax.experimental.pallas import tpu as pltpu
from jax.sharding import PartitionSpec as P

norm_eps = 1e-05
f32 = jnp.float32
bf16 = jnp.bfloat16
MIB = 2**20
VMEM_SPEC = pl.BlockSpec(memory_space=pltpu.VMEM)
SMEM_SPEC = pl.BlockSpec(memory_space=pltpu.SMEM)
ANY_SPEC = pl.BlockSpec(memory_space=pl.ANY)


def live_total(tokens_shape, shard_total):
    micro_count, own_count, _ = tokens_shape
    return micro_count * own_count * shard_total * 5 // 8


def xor_shard(value, mask):
    size = lax.axis_size("shard")
    return lax.ppermute(value, "shard", [(i, i ^ mask) for i in range(size)])


def spread(value):
    size = lax.axis_size("shard")
    same_core = [value] + [xor_shard(value, mask) for mask in range(2, size, 2)]
    other_core = [xor_shard(part, 1) for part in same_core]
    return [part for pair in zip(same_core, other_core) for part in pair]


def vmem_limit(rows):
    return (12 if rows <= 64 else 32) * MIB


def in_vmem(value):
    return pltpu.with_memory_space_constraint(value, pltpu.VMEM)


def load_kernel(info_ref, gate_ref, up_ref, down_ref, held_ref, sems):
    blocks = gate_ref.shape[0]

    def copies(h):
        return [
            pltpu.make_async_copy(ref.at[h], held_ref.at[i, h], sems.at[i, h])
            for i, ref in enumerate((gate_ref, up_ref, down_ref))
        ]

    @pl.loop(0, blocks)
    def _(h):
        for copy in copies(h):
            copy.start()

    @pl.loop(0, blocks)
    def _(h):
        for copy in copies(h):
            copy.wait()


def load_weights(info, gate, up, down, rows):
    shape = (3,) + gate.shape
    size = gate.size * 3
    return pl.pallas_call(
        load_kernel,
        out_shape=pltpu.VMEM(shape, bf16),
        in_specs=[SMEM_SPEC] + [ANY_SPEC] * 3,
        out_specs=VMEM_SPEC,
        scratch_shapes=[pltpu.SemaphoreType.DMA((3, gate.shape[0]))],
        compiler_params=pltpu.CompilerParams(vmem_limit_bytes=vmem_limit(rows) + 0 * MIB),
        cost_estimate=pl.CostEstimate(flops=0, bytes_accessed=size * 2, transcendentals=0),
        name="load_weights",
    )(info, gate, up, down)


def row_starts(lengths_ref, micro_count):
    starts = [jnp.int32(0)]
    for m in range(micro_count):
        starts.append(starts[-1] + lengths_ref[m])
    return starts


def layer_kernel(first, rows, unroll, shard_total, micro_count, own_count, *refs):
    info_ref, lengths_ref, in_ref, out_ref, gain_ref, held_ref = refs[:6]
    rest = list(refs[6:])
    shard_id = info_ref[0]
    blocks, slots, block = held_ref.shape[1], held_ref.shape[2], held_ref.shape[4]
    block_total = gain_ref.shape[0]
    chunk_blocks = block_total // shard_total
    chunks = [rest.pop(0) for _ in range(shard_total)]
    even_ref, odd_ref = rest.pop(0), rest.pop(0)
    own_ref = rest.pop(0) if first else None
    normed, hidden, total = rest

    squares = jnp.zeros((rows, block), f32)
    if first:
        starts = row_starts(lengths_ref, micro_count)
        group = micro_count * own_count
        place = lax.broadcasted_iota(jnp.int32, (rows, group), 0)
        local = lax.broadcasted_iota(jnp.int32, (rows, group), 1)
        picks = []
        for j in range(shard_total):
            device = shard_id ^ j
            target = jnp.full((rows, group), -1, jnp.int32)
            for m in range(micro_count):
                for q in range(own_count):
                    row = device * own_count + q
                    to = jnp.where(row < lengths_ref[m], starts[m] + row, -1)
                    target = jnp.where(local == m * own_count + q, to, target)
            picks.append((target == place).astype(f32))
        pick = jnp.concatenate(picks, axis=1).astype(bf16)
        for c in range(shard_total):
            columns = pl.ds(c * chunk_blocks * block, chunk_blocks * block)
            spans = jnp.concatenate([ref[:, columns].astype(f32) for ref in chunks], axis=0)
            raw = jnp.dot(pick, spans.astype(bf16), preferred_element_type=f32)
            for i in range(chunk_blocks):
                piece = raw[:, i * block : (i + 1) * block]
                squares += piece * piece
                normed[c * chunk_blocks + i] = piece.astype(bf16)
        for i in range(chunk_blocks):
            own_ref[:, i * block : (i + 1) * block] = normed[shard_id * chunk_blocks + i]
    else:
        for j in range(shard_total):
            base = (shard_id ^ j) * chunk_blocks
            for i in range(chunk_blocks):
                piece = chunks[j][:, i * block : (i + 1) * block]
                normed[base + i] = piece
                wide = piece.astype(f32)
                squares += wide * wide
    mean = jnp.sum(squares, axis=1, keepdims=True) / (block_total * block)
    scale = lax.rsqrt(mean + norm_eps)
    for b in range(block_total):
        normed[b] = (normed[b].astype(f32) * scale * gain_ref[b : b + 1, :]).astype(bf16)
    normed[block_total] = jnp.zeros((rows, block), bf16)
    total[...] = jnp.zeros_like(total)

    def at(ref, h, k):
        index = ref[h, k]
        return jnp.where(index < 0, block_total, index)

    @pl.loop(0, blocks // unroll)
    def _(step):
        for q in range(unroll):
            h = step * unroll + q
            picked = jnp.concatenate([normed[at(in_ref, h, k)] for k in range(slots)], axis=1)
            gate = jnp.dot(
                picked, held_ref[0, h].reshape(slots * block, block), preferred_element_type=f32
            )
            up = jnp.dot(
                picked, held_ref[1, h].reshape(slots * block, block), preferred_element_type=f32
            )
            hidden[h] = (gate / (1.0 + jnp.exp(-gate)) * up).astype(bf16)

    @pl.loop(0, blocks // unroll)
    def _(step):
        for q in range(unroll):
            h = step * unroll + q
            rows_in = hidden[h]
            for k in range(0, slots, 2):
                pair = jnp.concatenate([held_ref[2, h, k], held_ref[2, h, k + 1]], axis=1)
                product = jnp.dot(rows_in, pair, preferred_element_type=f32)
                for p in range(2):
                    total[at(out_ref, h, k + p)] += product[:, p * block : (p + 1) * block]

    for j in range(shard_total):
        base = (shard_id ^ j) * chunk_blocks
        target = (odd_ref if j % 2 else even_ref).at[j // 2]
        for i in range(chunk_blocks):
            target[:, i * block : (i + 1) * block] = total[base + i].astype(bf16)


def layer_step(first, rows, info, lengths, in_index, out_index, gain, held, chunks, micro_count, own_count):
    shard_total = len(chunks)
    _, blocks, slots, block, _ = held.shape
    block_total = gain.shape[0]
    width = block_total * block // shard_total
    unroll = 2 if blocks % 2 == 0 else 1
    outs = [pltpu.VMEM((shard_total // 2, rows, width), bf16)] * 2
    if first:
        outs.append(pltpu.VMEM((rows, width), bf16))
    return pl.pallas_call(
        functools.partial(layer_kernel, first, rows, unroll, shard_total, micro_count, own_count),
        out_shape=outs,
        in_specs=[SMEM_SPEC] * 4 + [VMEM_SPEC] * (2 + shard_total),
        out_specs=[VMEM_SPEC] * len(outs),
        scratch_shapes=[
            pltpu.VMEM((block_total + 1, rows, block), bf16),
            pltpu.VMEM((blocks, rows, block), bf16),
            pltpu.VMEM((block_total + 1, rows, block), f32),
        ],
        compiler_params=pltpu.CompilerParams(vmem_limit_bytes=vmem_limit(rows)),
        cost_estimate=pl.CostEstimate(
            flops=2 * rows * held.size, bytes_accessed=0, transcendentals=0
        ),
        name="layer_first" if first else "layer",
    )(info, lengths, in_index, out_index, gain, held, *map(in_vmem, chunks))


def pair_kernel(held_ref, even_ref, came_ref, own_ref, *send_refs):
    own_ref[...] = even_ref[0].astype(f32) + came_ref[0].astype(f32)
    for i, ref in enumerate(send_refs):
        ref[...] = (even_ref[i + 1].astype(f32) + came_ref[i + 1].astype(f32)).astype(bf16)


def pair_sum(held, even, came):
    parts, rows, width = even.shape
    return pl.pallas_call(
        pair_kernel,
        out_shape=[pltpu.VMEM((rows, width), f32)] + [pltpu.VMEM((rows, width), bf16)] * (parts - 1),
        in_specs=[VMEM_SPEC] * 3,
        out_specs=[VMEM_SPEC] * parts,
        compiler_params=pltpu.CompilerParams(vmem_limit_bytes=vmem_limit(rows)),
        name="pair_sum",
    )(held, in_vmem(even), in_vmem(came))


def finish_kernel(turn, info_ref, held_ref, x_ref, own_ref, *refs):
    fresh_ref, kept_out_ref = refs[-2:]
    sum_value = own_ref[...]
    for ref in refs[:-3]:
        sum_value = sum_value + ref[...].astype(f32)
    fresh = (x_ref[...].astype(f32) + sum_value).astype(bf16)
    fresh_ref[...] = fresh
    kept_ref = refs[-3]
    kept_out_ref[...] = jnp.where(info_ref[1] == turn, fresh, kept_ref[...])


def finish_sum(turn, info, held, x_own, own, came, kept):
    rows, width = x_own.shape
    return pl.pallas_call(
        functools.partial(finish_kernel, turn),
        out_shape=[pltpu.VMEM((rows, width), bf16)] * 2,
        in_specs=[SMEM_SPEC] + [VMEM_SPEC] * (4 + len(came)),
        out_specs=[VMEM_SPEC] * 2,
        compiler_params=pltpu.CompilerParams(vmem_limit_bytes=vmem_limit(rows)),
        name="finish_sum",
    )(info, held, *map(in_vmem, (x_own, own, *came, kept)))


def result_kernel(info_ref, lengths_ref, *refs):
    chunks, out_ref = refs[:-1], refs[-1]
    micro_count, own_count, _ = out_ref.shape
    shard_id = info_ref[0]
    rows, width = chunks[0].shape
    starts = row_starts(lengths_ref, micro_count)
    group = micro_count * own_count
    place = lax.broadcasted_iota(jnp.int32, (group, rows), 1)
    local = lax.broadcasted_iota(jnp.int32, (group, rows), 0)
    target = jnp.full((group, rows), -1, jnp.int32)
    for m in range(micro_count):
        for q in range(own_count):
            row = shard_id * own_count + q
            to = jnp.where(row < lengths_ref[m], starts[m] + row, -1)
            target = jnp.where(local == m * own_count + q, to, target)
    pick = (target == place).astype(f32).astype(bf16)
    for j, ref in enumerate(chunks):
        columns = pl.ds(pl.multiple_of((shard_id ^ j) * width, width), width)
        value = jnp.dot(pick, ref[...], preferred_element_type=f32)
        for m in range(micro_count):
            out_ref[m, :, columns] = value[m * own_count : (m + 1) * own_count].astype(bf16)


def result_rows(info, lengths, chunks, shape):
    rows = chunks[0].shape[0]
    return pl.pallas_call(
        result_kernel,
        out_shape=jax.ShapeDtypeStruct(shape, bf16),
        in_specs=[SMEM_SPEC] * 2 + [VMEM_SPEC] * len(chunks),
        out_specs=VMEM_SPEC,
        compiler_params=pltpu.CompilerParams(vmem_limit_bytes=vmem_limit(rows)),
        name="result_rows",
    )(info, lengths, *map(in_vmem, chunks))


def body(tokens, lengths, norm_gain, gate_tiles, up_tiles, in_index, down_tiles, out_index):
    micro_count, own_count, model_width = tokens.shape
    block = gate_tiles.shape[-1]
    section_id = lax.axis_index("section")
    section_total = lax.axis_size("section")
    shard_total = lax.axis_size("shard")
    rows = live_total(tokens.shape, shard_total)
    info = jnp.stack([lax.axis_index("shard"), section_id])
    gain = norm_gain.reshape(model_width // block, block)
    held = load_weights(info, gate_tiles[0], up_tiles[0], down_tiles[0], rows)
    held = in_vmem(held)
    chunks = spread(tokens.reshape(micro_count * own_count, model_width))
    for turn in range(section_total):
        first = turn == 0
        parts = layer_step(
            first, rows, info, lengths, in_index[0], out_index[0], gain, held, chunks, micro_count, own_count
        )
        x_own = parts[2] if first else chunks[0]
        sums = pair_sum(held, parts[0], xor_shard(parts[1], 1))
        came = [xor_shard(part, 2 * i + 2) for i, part in enumerate(sums[1:])]
        kept = x_own if first else kept
        fresh, kept = finish_sum(turn, info, held, x_own, sums[0], came, kept)
        if turn + 1 < section_total:
            moved = lax.ppermute(
                fresh, "section", [(i, i + 1) for i in range(section_total - 1)]
            )
            chunks = spread(moved)
    return result_rows(info, lengths, spread(kept), tokens.shape)[None]


def solution(mesh):
    placed = (
        P(None, "shard", None),
        P(),
        P("section", None),
        P("section", "shard", None, None, None),
        P("section", "shard", None, None, None),
        P("section", "shard", None),
        P("section", "shard", None, None, None),
        P("section", "shard", None),
    )
    return jax.shard_map(
        body,
        mesh=mesh,
        in_specs=placed,
        out_specs=P("section", None, "shard", None),
        check_vma=False,
    )
```

time: 764 us -> 166 us (0.22)
  waiting for transfers between devices: 392 us -> 61.1 us
  matrix products: 181 us -> 0 us
  local copies, waits for them, and re-layouts: 81.8 us -> 0.96 us
  Pallas kernels: 0 us -> 65 us
  blocking collectives: 61.1 us -> 0 us
  starting transfers between devices: 9.07 us -> 36.9 us
  other arithmetic: 18.7 us -> 0.65 us
  between operations: 13.5 us -> 0.2 us
    while x14 -> x0, waiting for transfers between devices: 360 us -> none
    dot_general x22 -> x0, matrix products: 181 us -> none  [the longest x7 94.9 us: turn_step(): jnp.dot(hidden, dense_down, preferred_element_type=jnp.float32)]
    pallas_call x0 -> x14, Pallas kernels: none -> 65 us  [the longest x4 44.9 us: layer_step(): pl.pallas_call(functools.partial(layer_kernel, first, rows, unroll, shard...]
    all_gather x7 -> x0, blocking collectives: 61.1 us -> none  [turn_step(): hidden = expand(lax.all_gather(normed, 'shard', axis=0, tiled=True))]
    unnamed x11 -> x4, local copies, waits for them, and re-layouts: 37 us -> 0.01 us
    ppermute x7 -> x54, waiting for transfers between devices: 31.5 us -> 61.1 us  [the longest x51 46.2 us: xor_shard(): return lax.ppermute(value, 'shard', [(i, i ^ mask) for i in range(size)])]
    ppermute x7 -> x54, starting transfers between devices: 9.02 us -> 36.9 us  [the longest x51 32.9 us: xor_shard(): return lax.ppermute(value, 'shard', [(i, i ^ mask) for i in range(size)])]
    while x21 -> x0, local copies, waits for them, and re-layouts: 23.6 us -> none
  transfers between devices with their start and end apart: 14 -> 54, of which waited for: 14 -> 40; matrix products, arithmetic and copies ran while one was open for 2% -> 0% of each run, Pallas kernels for 0% -> 9%
where the time goes in v1:
time: 166 us; the launch traced here: 165 us
  Pallas kernels  65 us (39%)
  waiting for transfers between devices  61.1 us (37%)
  starting transfers between devices  36.9 us (22%)
    ppermute x51, waiting for transfers between devices, xor_shard(): return lax.ppermute(value, 'shard', [(i, i ^ mask) for i in range(size)])  46.2 us
    pallas_call x4, Pallas kernels, layer_step(): pl.pallas_call(functools.partial(layer_kernel, first, rows, unroll, shard...  44.9 us
    ppermute x51, starting transfers between devices, xor_shard(): return lax.ppermute(value, 'shard', [(i, i ^ mask) for i in range(size)])  32.9 us
    ppermute x3, waiting for transfers between devices, body(): lax.ppermute(fresh, 'section', [(i, i + 1) for i in range(section_total -...  14.9 us
    pallas_call x1, Pallas kernels, load_weights(): pl.pallas_call(load_kernel, out_shape=pltpu.VMEM(shape, bf16), in_specs=[...  14.8 us
    ppermute x3, starting transfers between devices, body(): lax.ppermute(fresh, 'section', [(i, i + 1) for i in range(section_total -...  4.06 us
    pallas_call x4, Pallas kernels, finish_sum(): pl.pallas_call(functools.partial(finish_kernel, turn), out_shape=[pltpu.V...  3.65 us
  transfers between devices with their start and end apart: 54, of which 40 were waited for; matrix products, arithmetic and copies ran while one was open for 0% of the time, Pallas kernels for 9%

profile of v1, /device:TPU:24, one launch (start us, length us, event | category | flops | bytes accessed | tf_op | source)
XLA Modules:
  0.0 164.9 jit_solution(17753308878886680676)
XLA Ops:
  1.0 2.5 %collective-permute-start.5 = (bf16[8,8192]{1,0:T(8,128)(2,1)S(1)}, bf16[8,8192]{1,0:T(8,128)(2,1)S(1)}, u32[]{:S(2)}, u32[]{:S(2)}) collective-permute-start(bf16[8,8192]{1,0:T(8,128)(2,1)S(1)} %reshape.7.refs_6_), channel_id=1, source_target_pairs={{0,6},{1,7},{2,4},{3,5},{4,2},{5,3},{6,0},{7,1},{8,14},{9,15},{10,... | collective-permute-start | bytes 393224 | tf_op jit(solution)/shard_map/ppermute | solution.py:26
  4.5 3.0 %collective-permute-done.5.refs_12_ = bf16[8,8192]{1,0:T(8,128)(2,1)S(1)} collective-permute-done((bf16[8,8192]{1,0:T(8,128)(2,1)S(1)}, bf16[8,8192]{1,0:T(8,128)(2,1)S(1)}, u32[]{:S(2)}, u32[]{:S(2)}) %collective-permute-start.5) | collective-permute-done | bytes 131104 | tf_op jit(solution)/shard_map/ppermute | solution.py:26
  7.5 2.5 %collective-permute-done.3.refs_10_ = bf16[8,8192]{1,0:T(8,128)(2,1)S(1)} collective-permute-done((bf16[8,8192]{1,0:T(8,128)(2,1)S(1)}, bf16[8,8192]{1,0:T(8,128)(2,1)S(1)}, u32[]{:S(2)}, u32[]{:S(2)}) %collective-permute-start.3) | collective-permute-done | bytes 131104 | tf_op jit(solution)/shard_map/ppermute | solution.py:26
  11.1 14.8 %load_weights.1.refs_5_.held_ref = bf16[3,16,28,128,128]{4,3,2,1,0:T(8,128)(2,1)S(1)} custom-call(s32[2]{0:T(128)} %pad_add_fusion.info_ref.refs_0_, bf16[16,28,128,128]{3,2,1,0:T(8,128)(2,1)} %bitcast.9, bf16[16,28,128,128]{3,2,1,0:T(8,128)(2,1)} %bitcast.10, bf16[16,28,128,128]{3,2,1,0:T(8,128)(2,1)} %bitcast.11), custom_call_target="tpu_custom_call" | custom-call | bytes 44040192 | tf_op jit(solution)/shard_map/load_weights/pallas_call | solution.py:67
  25.9 11.4 %layer_first.1 = (bf16[4,40,1024]{2,1,0:T(8,128)(2,1)S(1)}, bf16[4,40,1024]{2,1,0:T(8,128)(2,1)S(1)}, bf16[40,1024]{1,0:T(8,128)(2,1)S(1)}) custom-call(s32[2]{0:T(128)} %pad_add_fusion.info_ref.refs_0_, s32[4]{0:T(128)} %lengths_ref.1, s32[16,28]{1,0:T(8,128)} %bitcast.16, s32[16,28]{1,0:T(8,128)} %bitcast.20, f32[64,128]{1,0:T(8,128)} %bitcast.12, ...), custom_call_target="tpu_custom_call" | custom-call | flops 1761607680 | tf_op jit(solution)/shard_map/layer_first/pallas_call | solution.py:184
  37.5 1.6 collective-permute-done.7.came_ref
  39.1 1.6 collective-permute-start.8
  43.7 3.2 %collective-permute-done.9.refs_1_ = bf16[40,1024]{1,0:T(8,128)(2,1)S(1)} collective-permute-done((bf16[40,1024]{1,0:T(8,128)(2,1)S(1)}, bf16[40,1024]{1,0:T(8,128)(2,1)S(1)}, u32[]{:S(2)}, u32[]{:S(2)}) %collective-permute-start.9) | collective-permute-done | bytes 81952 | tf_op jit(solution)/shard_map/ppermute | solution.py:26
  48.9 5.0 %collective-permute-done.11.refs_6_.x_ref = bf16[40,1024]{1,0:T(8,128)(2,1)S(1)} collective-permute-done((bf16[40,1024]{1,0:T(8,128)(2,1)S(1)}, bf16[40,1024]{1,0:T(8,128)(2,1)S(1)}, u32[]{:S(2)}, u32[]{:S(2)}) %collective-permute-start.11) | collective-permute-done | bytes 81952 | tf_op jit(solution)/shard_map/ppermute | solution.py:301
  54.0 1.5 collective-permute-start.17
  57.5 1.9 %collective-permute-done.17.refs_12_ = bf16[40,1024]{1,0:T(8,128)(2,1)S(1)} collective-permute-done((bf16[40,1024]{1,0:T(8,128)(2,1)S(1)}, bf16[40,1024]{1,0:T(8,128)(2,1)S(1)}, u32[]{:S(2)}, u32[]{:S(2)}) %collective-permute-start.17) | collective-permute-done | bytes 81952 | tf_op jit(solution)/shard_map/ppermute | solution.py:26
  62.3 11.1 %layer.3 = (bf16[4,40,1024]{2,1,0:T(8,128)(2,1)S(1)}, bf16[4,40,1024]{2,1,0:T(8,128)(2,1)S(1)}) custom-call(s32[2]{0:T(128)} %pad_add_fusion.info_ref.refs_0_, s32[4]{0:T(128)} %lengths_ref.1, s32[16,28]{1,0:T(8,128)} %bitcast.17, s32[16,28]{1,0:T(8,128)} %bitcast.21, f32[64,128]{1,0:T(8,128)} %bitcast.13, ...), custom_call_target="tpu_custom_call" | custom-call | flops 1761607680 | tf_op jit(solution)/shard_map/layer/pallas_call | solution.py:184
  73.7 1.5 collective-permute-done.19.came_ref
  77.3 1.5 collective-permute-start.22
  79.8 1.7 %collective-permute-done.21.refs_1_ = bf16[40,1024]{1,0:T(8,128)(2,1)S(1)} collective-permute-done((bf16[40,1024]{1,0:T(8,128)(2,1)S(1)}, bf16[40,1024]{1,0:T(8,128)(2,1)S(1)}, u32[]{:S(2)}, u32[]{:S(2)}) %collective-permute-start.21) | collective-permute-done | bytes 81952 | tf_op jit(solution)/shard_map/ppermute | solution.py:26
  84.7 5.0 %collective-permute-done.23.refs_6_.x_ref = bf16[40,1024]{1,0:T(8,128)(2,1)S(1)} collective-permute-done((bf16[40,1024]{1,0:T(8,128)(2,1)S(1)}, bf16[40,1024]{1,0:T(8,128)(2,1)S(1)}, u32[]{:S(2)}, u32[]{:S(2)}) %collective-permute-start.23) | collective-permute-done | bytes 81952 | tf_op jit(solution)/shard_map/ppermute | solution.py:301
  89.7 1.5 collective-permute-start.29
  93.2 1.9 %collective-permute-done.29.refs_12_ = bf16[40,1024]{1,0:T(8,128)(2,1)S(1)} collective-permute-done((bf16[40,1024]{1,0:T(8,128)(2,1)S(1)}, bf16[40,1024]{1,0:T(8,128)(2,1)S(1)}, u32[]{:S(2)}, u32[]{:S(2)}) %collective-permute-start.29) | collective-permute-done | bytes 81952 | tf_op jit(solution)/shard_map/ppermute | solution.py:26
  97.8 11.1 %layer.4 = (bf16[4,40,1024]{2,1,0:T(8,128)(2,1)S(1)}, bf16[4,40,1024]{2,1,0:T(8,128)(2,1)S(1)}) custom-call(s32[2]{0:T(128)} %pad_add_fusion.info_ref.refs_0_, s32[4]{0:T(128)} %lengths_ref.1, s32[16,28]{1,0:T(8,128)} %bitcast.18, s32[16,28]{1,0:T(8,128)} %bitcast.22, f32[64,128]{1,0:T(8,128)} %bitcast.14, ...), custom_call_target="tpu_custom_call" | custom-call | flops 1761607680 | tf_op jit(solution)/shard_map/layer/pallas_call | solution.py:184
  109.1 1.5 collective-permute-done.31.came_ref
  112.8 1.5 collective-permute-start.34
  115.3 2.0 %collective-permute-done.33.refs_1_ = bf16[40,1024]{1,0:T(8,128)(2,1)S(1)} collective-permute-done((bf16[40,1024]{1,0:T(8,128)(2,1)S(1)}, bf16[40,1024]{1,0:T(8,128)(2,1)S(1)}, u32[]{:S(2)}, u32[]{:S(2)}) %collective-permute-start.33) | collective-permute-done | bytes 81952 | tf_op jit(solution)/shard_map/ppermute | solution.py:26
  120.3 4.9 %collective-permute-done.35.refs_6_.x_ref = bf16[40,1024]{1,0:T(8,128)(2,1)S(1)} collective-permute-done((bf16[40,1024]{1,0:T(8,128)(2,1)S(1)}, bf16[40,1024]{1,0:T(8,128)(2,1)S(1)}, u32[]{:S(2)}, u32[]{:S(2)}) %collective-permute-start.35) | collective-permute-done | bytes 81952 | tf_op jit(solution)/shard_map/ppermute | solution.py:301
  125.2 1.5 collective-permute-start.41
  128.7 1.9 %collective-permute-done.41.refs_12_ = bf16[40,1024]{1,0:T(8,128)(2,1)S(1)} collective-permute-done((bf16[40,1024]{1,0:T(8,128)(2,1)S(1)}, bf16[40,1024]{1,0:T(8,128)(2,1)S(1)}, u32[]{:S(2)}, u32[]{:S(2)}) %collective-permute-start.41) | collective-permute-done | bytes 81952 | tf_op jit(solution)/shard_map/ppermute | solution.py:26
  133.6 11.1 %layer.5 = (bf16[4,40,1024]{2,1,0:T(8,128)(2,1)S(1)}, bf16[4,40,1024]{2,1,0:T(8,128)(2,1)S(1)}) custom-call(s32[2]{0:T(128)} %pad_add_fusion.info_ref.refs_0_, s32[4]{0:T(128)} %lengths_ref.1, s32[16,28]{1,0:T(8,128)} %bitcast.19, s32[16,28]{1,0:T(8,128)} %bitcast.23, f32[64,128]{1,0:T(8,128)} %bitcast.15, ...), custom_call_target="tpu_custom_call" | custom-call | flops 1761607680 | tf_op jit(solution)/shard_map/layer/pallas_call | solution.py:184
  144.9 1.5 collective-permute-done.43.came_ref
  148.6 1.5 collective-permute-start.46
  151.0 1.7 %collective-permute-done.45.refs_1_ = bf16[40,1024]{1,0:T(8,128)(2,1)S(1)} collective-permute-done((bf16[40,1024]{1,0:T(8,128)(2,1)S(1)}, bf16[40,1024]{1,0:T(8,128)(2,1)S(1)}, u32[]{:S(2)}, u32[]{:S(2)}) %collective-permute-start.45) | collective-permute-done | bytes 81952 | tf_op jit(solution)/shard_map/ppermute | solution.py:26
  153.9 1.5 finish_sum.7
  155.4 1.5 collective-permute-start.52
  158.9 1.9 %collective-permute-done.52.refs_6_ = bf16[40,1024]{1,0:T(8,128)(2,1)S(1)} collective-permute-done((bf16[40,1024]{1,0:T(8,128)(2,1)S(1)}, bf16[40,1024]{1,0:T(8,128)(2,1)S(1)}, u32[]{:S(2)}, u32[]{:S(2)}) %collective-permute-start.52) | collective-permute-done | bytes 81952 | tf_op jit(solution)/shard_map/ppermute | solution.py:26
  (96 shorter events, 46.6 us)
Async XLA Ops:
  1.0 6.5 %collective-permute-start.5 = (bf16[8,8192]{1,0:T(8,128)(2,1)S(1)}, bf16[8,8192]{1,0:T(8,128)(2,1)S(1)}, u32[]{:S(2)}, u32[]{:S(2)}) collective-permute-start(bf16[8,8192]{1,0:T(8,128)(2,1)S(1)} %reshape.7.refs_6_), channel_id=1, source_target_pairs={{0,6},{1,7},{2,4},{3,5},{4,2},{5,3},{6,0},{7,1},{8,14},{9,15},{10,... | collective-permute-start | bytes 393224 | tf_op jit(solution)/shard_map/ppermute | solution.py:26
  3.5 6.5 %collective-permute-start.3 = (bf16[8,8192]{1,0:T(8,128)(2,1)S(1)}, bf16[8,8192]{1,0:T(8,128)(2,1)S(1)}, u32[]{:S(2)}, u32[]{:S(2)}) collective-permute-start(bf16[8,8192]{1,0:T(8,128)(2,1)S(1)} %reshape.7.refs_6_), channel_id=1, source_target_pairs={{0,4},{1,5},{2,6},{3,7},{4,0},{5,1},{6,2},{7,3},{8,12},{9,13},{10,... | collective-permute-start | bytes 393224 | tf_op jit(solution)/shard_map/ppermute | solution.py:26
  4.0 6.0 %collective-permute-start.1 = (bf16[8,8192]{1,0:T(8,128)(2,1)S(1)}, bf16[8,8192]{1,0:T(8,128)(2,1)S(1)}, u32[]{:S(2)}, u32[]{:S(2)}) collective-permute-start(bf16[8,8192]{1,0:T(8,128)(2,1)S(1)} %reshape.7.refs_6_), channel_id=1, source_target_pairs={{0,2},{1,3},{2,0},{3,1},{4,6},{5,7},{6,4},{7,5},{8,10},{9,11},{10,... | collective-permute-start | bytes 393224 | tf_op jit(solution)/shard_map/ppermute | solution.py:26
  4.5 21.4 %collective-permute-start = (bf16[8,8192]{1,0:T(8,128)(2,1)S(1)}, bf16[8,8192]{1,0:T(8,128)(2,1)S(1)}, u32[]{:S(2)}, u32[]{:S(2)}) collective-permute-start(bf16[8,8192]{1,0:T(8,128)(2,1)S(1)} %reshape.7.refs_6_), channel_id=1, source_target_pairs={{0,1},{1,0},{2,3},{3,2},{4,5},{5,4},{6,7},{7,6},{8,9},{9,8},{10,11... | collective-permute-start | bytes 393224 | tf_op jit(solution)/shard_map/ppermute | solution.py:26
  7.5 18.4 %collective-permute-start.6 = (bf16[8,8192]{1,0:T(8,128)(2,1)S(1)}, bf16[8,8192]{1,0:T(8,128)(2,1)S(1)}, u32[]{:S(2)}, u32[]{:S(2)}) collective-permute-start(bf16[8,8192]{1,0:T(8,128)(2,1)S(1)} %collective-permute-done.5.refs_12_), channel_id=1, source_target_pairs={{0,1},{1,0},{2,3},{3,2},{4,5},{5,4},{6,7},{7,6},{8,9},{9,8},{10,11... | collective-permute-start | bytes 393224 | tf_op jit(solution)/shard_map/ppermute | solution.py:26
  10.0 16.0 %collective-permute-start.4 = (bf16[8,8192]{1,0:T(8,128)(2,1)S(1)}, bf16[8,8192]{1,0:T(8,128)(2,1)S(1)}, u32[]{:S(2)}, u32[]{:S(2)}) collective-permute-start(bf16[8,8192]{1,0:T(8,128)(2,1)S(1)} %collective-permute-done.3.refs_10_), channel_id=1, source_target_pairs={{0,1},{1,0},{2,3},{3,2},{4,5},{5,4},{6,7},{7,6},{8,9},{9,8},{10,11... | collective-permute-start | bytes 393224 | tf_op jit(solution)/shard_map/ppermute | solution.py:26
  10.0 15.9 %collective-permute-start.2 = (bf16[8,8192]{1,0:T(8,128)(2,1)S(1)}, bf16[8,8192]{1,0:T(8,128)(2,1)S(1)}, u32[]{:S(2)}, u32[]{:S(2)}) collective-permute-start(bf16[8,8192]{1,0:T(8,128)(2,1)S(1)} %collective-permute-done.1.refs_8_), channel_id=1, source_target_pairs={{0,1},{1,0},{2,3},{3,2},{4,5},{5,4},{6,7},{7,6},{8,9},{9,8},{10,11... | collective-permute-start | bytes 393224 | tf_op jit(solution)/shard_map/ppermute | solution.py:26
  39.1 4.6 %collective-permute-start.8 = (bf16[40,1024]{1,0:T(8,128)(2,1)S(1)}, bf16[40,1024]{1,0:T(8,128)(2,1)S(1)}, u32[]{:S(2)}, u32[]{:S(2)}) collective-permute-start(bf16[40,1024]{1,0:T(8,128)(2,1)S(1)} %get-tuple-element.41), channel_id=1, source_target_pairs={{0,2},{1,3},{2,0},{3,1},{4,6},{5,7},{6,4},{7,5},{8,10},{9,11},{10,... | collective-permute-start | bytes 245768 | tf_op jit(solution)/shard_map/ppermute | solution.py:26
  40.7 6.2 %collective-permute-start.9 = (bf16[40,1024]{1,0:T(8,128)(2,1)S(1)}, bf16[40,1024]{1,0:T(8,128)(2,1)S(1)}, u32[]{:S(2)}, u32[]{:S(2)}) collective-permute-start(bf16[40,1024]{1,0:T(8,128)(2,1)S(1)} %get-tuple-element.42), channel_id=1, source_target_pairs={{0,4},{1,5},{2,6},{3,7},{4,0},{5,1},{6,2},{7,3},{8,12},{9,13},{10,... | collective-permute-start | bytes 245768 | tf_op jit(solution)/shard_map/ppermute | solution.py:26
  41.5 5.4 %collective-permute-start.10 = (bf16[40,1024]{1,0:T(8,128)(2,1)S(1)}, bf16[40,1024]{1,0:T(8,128)(2,1)S(1)}, u32[]{:S(2)}, u32[]{:S(2)}) collective-permute-start(bf16[40,1024]{1,0:T(8,128)(2,1)S(1)} %get-tuple-element.43), channel_id=1, source_target_pairs={{0,6},{1,7},{2,4},{3,5},{4,2},{5,3},{6,0},{7,1},{8,14},{9,15},{10,... | collective-permute-start | bytes 245768 | tf_op jit(solution)/shard_map/ppermute | solution.py:26
  47.6 6.3 %collective-permute-start.11 = (bf16[40,1024]{1,0:T(8,128)(2,1)S(1)}, bf16[40,1024]{1,0:T(8,128)(2,1)S(1)}, u32[]{:S(2)}, u32[]{:S(2)}) collective-permute-start(bf16[40,1024]{1,0:T(8,128)(2,1)S(1)} %get-tuple-element.44), channel_id=1, source_target_pairs={{0,8},{8,16},{16,24},{1,9},{9,17},{17,25},{2,10},{10,18},{18,26},{... | collective-permute-start | bytes 245768 | tf_op jit(solution)/shard_map/ppermute | solution.py:301
  54.0 5.4 %collective-permute-start.17 = (bf16[40,1024]{1,0:T(8,128)(2,1)S(1)}, bf16[40,1024]{1,0:T(8,128)(2,1)S(1)}, u32[]{:S(2)}, u32[]{:S(2)}) collective-permute-start(bf16[40,1024]{1,0:T(8,128)(2,1)S(1)} %collective-permute-done.11.refs_6_.x_ref), channel_id=1, source_target_pairs={{0,6},{1,7},{2,4},{3,5},{4,2},{5,3},{6,0},{7,1},{8,14},{9,15},{10,... | collective-permute-start | bytes 245768 | tf_op jit(solution)/shard_map/ppermute | solution.py:26
  55.4 4.7 %collective-permute-start.15 = (bf16[40,1024]{1,0:T(8,128)(2,1)S(1)}, bf16[40,1024]{1,0:T(8,128)(2,1)S(1)}, u32[]{:S(2)}, u32[]{:S(2)}) collective-permute-start(bf16[40,1024]{1,0:T(8,128)(2,1)S(1)} %collective-permute-done.11.refs_6_.x_ref), channel_id=1, source_target_pairs={{0,4},{1,5},{2,6},{3,7},{4,0},{5,1},{6,2},{7,3},{8,12},{9,13},{10,... | collective-permute-start | bytes 245768 | tf_op jit(solution)/shard_map/ppermute | solution.py:26
  75.3 4.6 %collective-permute-start.20 = (bf16[40,1024]{1,0:T(8,128)(2,1)S(1)}, bf16[40,1024]{1,0:T(8,128)(2,1)S(1)}, u32[]{:S(2)}, u32[]{:S(2)}) collective-permute-start(bf16[40,1024]{1,0:T(8,128)(2,1)S(1)} %get-tuple-element.48), channel_id=1, source_target_pairs={{0,2},{1,3},{2,0},{3,1},{4,6},{5,7},{6,4},{7,5},{8,10},{9,11},{10,... | collective-permute-start | bytes 245768 | tf_op jit(solution)/shard_map/ppermute | solution.py:26
  76.2 5.3 %collective-permute-start.21 = (bf16[40,1024]{1,0:T(8,128)(2,1)S(1)}, bf16[40,1024]{1,0:T(8,128)(2,1)S(1)}, u32[]{:S(2)}, u32[]{:S(2)}) collective-permute-start(bf16[40,1024]{1,0:T(8,128)(2,1)S(1)} %get-tuple-element.49), channel_id=1, source_target_pairs={{0,4},{1,5},{2,6},{3,7},{4,0},{5,1},{6,2},{7,3},{8,12},{9,13},{10,... | collective-permute-start | bytes 245768 | tf_op jit(solution)/shard_map/ppermute | solution.py:26
  77.3 5.3 %collective-permute-start.22 = (bf16[40,1024]{1,0:T(8,128)(2,1)S(1)}, bf16[40,1024]{1,0:T(8,128)(2,1)S(1)}, u32[]{:S(2)}, u32[]{:S(2)}) collective-permute-start(bf16[40,1024]{1,0:T(8,128)(2,1)S(1)} %get-tuple-element.50), channel_id=1, source_target_pairs={{0,6},{1,7},{2,4},{3,5},{4,2},{5,3},{6,0},{7,1},{8,14},{9,15},{10,... | collective-permute-start | bytes 245768 | tf_op jit(solution)/shard_map/ppermute | solution.py:26
  83.4 6.3 %collective-permute-start.23 = (bf16[40,1024]{1,0:T(8,128)(2,1)S(1)}, bf16[40,1024]{1,0:T(8,128)(2,1)S(1)}, u32[]{:S(2)}, u32[]{:S(2)}) collective-permute-start(bf16[40,1024]{1,0:T(8,128)(2,1)S(1)} %get-tuple-element.52), channel_id=1, source_target_pairs={{0,8},{8,16},{16,24},{1,9},{9,17},{17,25},{2,10},{10,18},{18,26},{... | collective-permute-start | bytes 245768 | tf_op jit(solution)/shard_map/ppermute | solution.py:301
  89.7 5.4 %collective-permute-start.29 = (bf16[40,1024]{1,0:T(8,128)(2,1)S(1)}, bf16[40,1024]{1,0:T(8,128)(2,1)S(1)}, u32[]{:S(2)}, u32[]{:S(2)}) collective-permute-start(bf16[40,1024]{1,0:T(8,128)(2,1)S(1)} %collective-permute-done.23.refs_6_.x_ref), channel_id=1, source_target_pairs={{0,6},{1,7},{2,4},{3,5},{4,2},{5,3},{6,0},{7,1},{8,14},{9,15},{10,... | collective-permute-start | bytes 245768 | tf_op jit(solution)/shard_map/ppermute | solution.py:26
  91.2 4.7 %collective-permute-start.27 = (bf16[40,1024]{1,0:T(8,128)(2,1)S(1)}, bf16[40,1024]{1,0:T(8,128)(2,1)S(1)}, u32[]{:S(2)}, u32[]{:S(2)}) collective-permute-start(bf16[40,1024]{1,0:T(8,128)(2,1)S(1)} %collective-permute-done.23.refs_6_.x_ref), channel_id=1, source_target_pairs={{0,4},{1,5},{2,6},{3,7},{4,0},{5,1},{6,2},{7,3},{8,12},{9,13},{10,... | collective-permute-start | bytes 245768 | tf_op jit(solution)/shard_map/ppermute | solution.py:26
  92.1 4.4 %collective-permute-start.25 = (bf16[40,1024]{1,0:T(8,128)(2,1)S(1)}, bf16[40,1024]{1,0:T(8,128)(2,1)S(1)}, u32[]{:S(2)}, u32[]{:S(2)}) collective-permute-start(bf16[40,1024]{1,0:T(8,128)(2,1)S(1)} %collective-permute-done.23.refs_6_.x_ref), channel_id=1, source_target_pairs={{0,2},{1,3},{2,0},{3,1},{4,6},{5,7},{6,4},{7,5},{8,10},{9,11},{10,... | collective-permute-start | bytes 245768 | tf_op jit(solution)/shard_map/ppermute | solution.py:26
  110.7 4.6 %collective-permute-start.32 = (bf16[40,1024]{1,0:T(8,128)(2,1)S(1)}, bf16[40,1024]{1,0:T(8,128)(2,1)S(1)}, u32[]{:S(2)}, u32[]{:S(2)}) collective-permute-start(bf16[40,1024]{1,0:T(8,128)(2,1)S(1)} %get-tuple-element.56), channel_id=1, source_target_pairs={{0,2},{1,3},{2,0},{3,1},{4,6},{5,7},{6,4},{7,5},{8,10},{9,11},{10,... | collective-permute-start | bytes 245768 | tf_op jit(solution)/shard_map/ppermute | solution.py:26
  111.9 5.3 %collective-permute-start.33 = (bf16[40,1024]{1,0:T(8,128)(2,1)S(1)}, bf16[40,1024]{1,0:T(8,128)(2,1)S(1)}, u32[]{:S(2)}, u32[]{:S(2)}) collective-permute-start(bf16[40,1024]{1,0:T(8,128)(2,1)S(1)} %get-tuple-element.57), channel_id=1, source_target_pairs={{0,4},{1,5},{2,6},{3,7},{4,0},{5,1},{6,2},{7,3},{8,12},{9,13},{10,... | collective-permute-start | bytes 245768 | tf_op jit(solution)/shard_map/ppermute | solution.py:26
  112.8 5.3 %collective-permute-start.34 = (bf16[40,1024]{1,0:T(8,128)(2,1)S(1)}, bf16[40,1024]{1,0:T(8,128)(2,1)S(1)}, u32[]{:S(2)}, u32[]{:S(2)}) collective-permute-start(bf16[40,1024]{1,0:T(8,128)(2,1)S(1)} %get-tuple-element.58), channel_id=1, source_target_pairs={{0,6},{1,7},{2,4},{3,5},{4,2},{5,3},{6,0},{7,1},{8,14},{9,15},{10,... | collective-permute-start | bytes 245768 | tf_op jit(solution)/shard_map/ppermute | solution.py:26
  118.9 6.3 %collective-permute-start.35 = (bf16[40,1024]{1,0:T(8,128)(2,1)S(1)}, bf16[40,1024]{1,0:T(8,128)(2,1)S(1)}, u32[]{:S(2)}, u32[]{:S(2)}) collective-permute-start(bf16[40,1024]{1,0:T(8,128)(2,1)S(1)} %get-tuple-element.60), channel_id=1, source_target_pairs={{0,8},{8,16},{16,24},{1,9},{9,17},{17,25},{2,10},{10,18},{18,26},{... | collective-permute-start | bytes 245768 | tf_op jit(solution)/shard_map/ppermute | solution.py:301
  125.2 5.4 %collective-permute-start.41 = (bf16[40,1024]{1,0:T(8,128)(2,1)S(1)}, bf16[40,1024]{1,0:T(8,128)(2,1)S(1)}, u32[]{:S(2)}, u32[]{:S(2)}) collective-permute-start(bf16[40,1024]{1,0:T(8,128)(2,1)S(1)} %collective-permute-done.35.refs_6_.x_ref), channel_id=1, source_target_pairs={{0,6},{1,7},{2,4},{3,5},{4,2},{5,3},{6,0},{7,1},{8,14},{9,15},{10,... | collective-permute-start | bytes 245768 | tf_op jit(solution)/shard_map/ppermute | solution.py:26
  126.7 4.7 %collective-permute-start.39 = (bf16[40,1024]{1,0:T(8,128)(2,1)S(1)}, bf16[40,1024]{1,0:T(8,128)(2,1)S(1)}, u32[]{:S(2)}, u32[]{:S(2)}) collective-permute-start(bf16[40,1024]{1,0:T(8,128)(2,1)S(1)} %collective-permute-done.35.refs_6_.x_ref), channel_id=1, source_target_pairs={{0,4},{1,5},{2,6},{3,7},{4,0},{5,1},{6,2},{7,3},{8,12},{9,13},{10,... | collective-permute-start | bytes 245768 | tf_op jit(solution)/shard_map/ppermute | solution.py:26
  127.8 4.4 %collective-permute-start.37 = (bf16[40,1024]{1,0:T(8,128)(2,1)S(1)}, bf16[40,1024]{1,0:T(8,128)(2,1)S(1)}, u32[]{:S(2)}, u32[]{:S(2)}) collective-permute-start(bf16[40,1024]{1,0:T(8,128)(2,1)S(1)} %collective-permute-done.35.refs_6_.x_ref), channel_id=1, source_target_pairs={{0,2},{1,3},{2,0},{3,1},{4,6},{5,7},{6,4},{7,5},{8,10},{9,11},{10,... | collective-permute-start | bytes 245768 | tf_op jit(solution)/shard_map/ppermute | solution.py:26
  146.5 4.6 %collective-permute-start.44 = (bf16[40,1024]{1,0:T(8,128)(2,1)S(1)}, bf16[40,1024]{1,0:T(8,128)(2,1)S(1)}, u32[]{:S(2)}, u32[]{:S(2)}) collective-permute-start(bf16[40,1024]{1,0:T(8,128)(2,1)S(1)} %get-tuple-element.64), channel_id=1, source_target_pairs={{0,2},{1,3},{2,0},{3,1},{4,6},{5,7},{6,4},{7,5},{8,10},{9,11},{10,... | collective-permute-start | bytes 245768 | tf_op jit(solution)/shard_map/ppermute | solution.py:26
  147.4 5.3 %collective-permute-start.45 = (bf16[40,1024]{1,0:T(8,128)(2,1)S(1)}, bf16[40,1024]{1,0:T(8,128)(2,1)S(1)}, u32[]{:S(2)}, u32[]{:S(2)}) collective-permute-start(bf16[40,1024]{1,0:T(8,128)(2,1)S(1)} %get-tuple-element.65), channel_id=1, source_target_pairs={{0,4},{1,5},{2,6},{3,7},{4,0},{5,1},{6,2},{7,3},{8,12},{9,13},{10,... | collective-permute-start | bytes 245768 | tf_op jit(solution)/shard_map/ppermute | solution.py:26
  148.6 5.3 %collective-permute-start.46 = (bf16[40,1024]{1,0:T(8,128)(2,1)S(1)}, bf16[40,1024]{1,0:T(8,128)(2,1)S(1)}, u32[]{:S(2)}, u32[]{:S(2)}) collective-permute-start(bf16[40,1024]{1,0:T(8,128)(2,1)S(1)} %get-tuple-element.66), channel_id=1, source_target_pairs={{0,6},{1,7},{2,4},{3,5},{4,2},{5,3},{6,0},{7,1},{8,14},{9,15},{10,... | collective-permute-start | bytes 245768 | tf_op jit(solution)/shard_map/ppermute | solution.py:26
  155.4 5.4 %collective-permute-start.52 = (bf16[40,1024]{1,0:T(8,128)(2,1)S(1)}, bf16[40,1024]{1,0:T(8,128)(2,1)S(1)}, u32[]{:S(2)}, u32[]{:S(2)}) collective-permute-start(bf16[40,1024]{1,0:T(8,128)(2,1)S(1)} %get-tuple-element.68.refs_0_), channel_id=1, source_target_pairs={{0,6},{1,7},{2,4},{3,5},{4,2},{5,3},{6,0},{7,1},{8,14},{9,15},{10,... | collective-permute-start | bytes 245768 | tf_op jit(solution)/shard_map/ppermute | solution.py:26
  156.9 4.7 %collective-permute-start.50 = (bf16[40,1024]{1,0:T(8,128)(2,1)S(1)}, bf16[40,1024]{1,0:T(8,128)(2,1)S(1)}, u32[]{:S(2)}, u32[]{:S(2)}) collective-permute-start(bf16[40,1024]{1,0:T(8,128)(2,1)S(1)} %get-tuple-element.68.refs_0_), channel_id=1, source_target_pairs={{0,4},{1,5},{2,6},{3,7},{4,0},{5,1},{6,2},{7,3},{8,12},{9,13},{10,... | collective-permute-start | bytes 245768 | tf_op jit(solution)/shard_map/ppermute | solution.py:26
  (24 other events, 65.0 us)

commit v2 on v1

--- a/solution.py
+++ b/solution.py
@@ -11,6 +11,7 @@
 f32 = jnp.float32
 bf16 = jnp.bfloat16
 MIB = 2**20
+UNROLL = 4
 VMEM_SPEC = pl.BlockSpec(memory_space=pltpu.VMEM)
 SMEM_SPEC = pl.BlockSpec(memory_space=pltpu.SMEM)
 ANY_SPEC = pl.BlockSpec(memory_space=pl.ANY)
@@ -26,11 +27,27 @@
     return lax.ppermute(value, "shard", [(i, i ^ mask) for i in range(size)])
 
 
-def spread(value):
+def same_core(value):
     size = lax.axis_size("shard")
-    same_core = [value] + [xor_shard(value, mask) for mask in range(2, size, 2)]
-    other_core = [xor_shard(part, 1) for part in same_core]
-    return [part for pair in zip(same_core, other_core) for part in pair]
+    return [value] + [xor_shard(value, mask) for mask in range(2, size, 2)]
+
+
+def next_section(value, turn):
+    size = lax.axis_size("shard")
+    start = turn * size
+    return [
+        lax.ppermute(
+            value,
+            ("section", "shard"),
+            [(start + i, start + size + (i ^ mask)) for i in range(size)],
+        )
+        for mask in range(0, size, 2)
+    ]
+
+
+def both_cores(parts):
+    other_core = [xor_shard(part, 1) for part in parts]
+    return [part for pair in zip(parts, other_core) for part in pair]
 
 
 def vmem_limit(rows):
@@ -41,13 +58,13 @@
     return pltpu.with_memory_space_constraint(value, pltpu.VMEM)
 
 
-def load_kernel(info_ref, gate_ref, up_ref, down_ref, held_ref, sems):
+def load_kernel(info_ref, gate_ref, up_ref, held_ref, sems):
     blocks = gate_ref.shape[0]
 
     def copies(h):
         return [
             pltpu.make_async_copy(ref.at[h], held_ref.at[i, h], sems.at[i, h])
-            for i, ref in enumerate((gate_ref, up_ref, down_ref))
+            for i, ref in enumerate((gate_ref, up_ref))
         ]
 
     @pl.loop(0, blocks)
@@ -61,19 +78,36 @@
             copy.wait()
 
 
-def load_weights(info, gate, up, down, rows):
+def load_weights(info, gate, up, rows):
     shape = (3,) + gate.shape
-    size = gate.size * 3
+    size = gate.size * 2
     return pl.pallas_call(
         load_kernel,
         out_shape=pltpu.VMEM(shape, bf16),
-        in_specs=[SMEM_SPEC] + [ANY_SPEC] * 3,
+        in_specs=[SMEM_SPEC] + [ANY_SPEC] * 2,
         out_specs=VMEM_SPEC,
-        scratch_shapes=[pltpu.SemaphoreType.DMA((3, gate.shape[0]))],
-        compiler_params=pltpu.CompilerParams(vmem_limit_bytes=vmem_limit(rows) + 0 * MIB),
+        scratch_shapes=[pltpu.SemaphoreType.DMA((2, gate.shape[0]))],
+        compiler_params=pltpu.CompilerParams(vmem_limit_bytes=vmem_limit(rows)),
         cost_estimate=pl.CostEstimate(flops=0, bytes_accessed=size * 2, transcendentals=0),
         name="load_weights",
-    )(info, gate, up, down)
+    )(info, gate, up)
+
+
+def relay_kernel(held_ref, *refs):
+    half = len(refs) // 2
+    for source, target in zip(refs[:half], refs[half:]):
+        target[...] = source[...]
+
+
+def relay(held, parts, rows):
+    return pl.pallas_call(
+        relay_kernel,
+        out_shape=[pltpu.VMEM(part.shape, part.dtype) for part in parts],
+        in_specs=[VMEM_SPEC] * (1 + len(parts)),
+        out_specs=[VMEM_SPEC] * len(parts),
+        compiler_params=pltpu.CompilerParams(vmem_limit_bytes=vmem_limit(rows)),
+        name="relay",
+    )(held, *map(in_vmem, parts))
 
 
 def row_starts(lengths_ref, micro_count):
@@ -86,13 +120,25 @@
 def layer_kernel(first, rows, unroll, shard_total, micro_count, own_count, *refs):
     info_ref, lengths_ref, in_ref, out_ref, gain_ref, held_ref = refs[:6]
     rest = list(refs[6:])
+    down_ref = rest.pop(0) if first else None
     shard_id = info_ref[0]
     blocks, slots, block = held_ref.shape[1], held_ref.shape[2], held_ref.shape[4]
     block_total = gain_ref.shape[0]
     chunk_blocks = block_total // shard_total
     chunks = [rest.pop(0) for _ in range(shard_total)]
     even_ref, odd_ref = rest.pop(0), rest.pop(0)
-    own_ref = rest.pop(0) if first else None
+    if first:
+        own_ref, filled_ref = rest.pop(0), rest.pop(0)
+        sems = rest.pop()
+
+        def copy_down(h):
+            return pltpu.make_async_copy(down_ref.at[h], filled_ref.at[2, h], sems.at[h])
+
+        @pl.loop(0, blocks)
+        def _(h):
+            copy_down(h).start()
+    else:
+        filled_ref = held_ref
     normed, hidden, total = rest
 
     squares = jnp.zeros((rows, block), f32)
@@ -158,9 +204,11 @@
     def _(step):
         for q in range(unroll):
             h = step * unroll + q
+            if first:
+                copy_down(h).wait()
             rows_in = hidden[h]
             for k in range(0, slots, 2):
-                pair = jnp.concatenate([held_ref[2, h, k], held_ref[2, h, k + 1]], axis=1)
+                pair = jnp.concatenate([filled_ref[2, h, k], filled_ref[2, h, k + 1]], axis=1)
                 product = jnp.dot(rows_in, pair, preferred_element_type=f32)
                 for p in range(2):
                     total[at(out_ref, h, k + p)] += product[:, p * block : (p + 1) * block]
@@ -172,31 +220,37 @@
             target[:, i * block : (i + 1) * block] = total[base + i].astype(bf16)
 
 
-def layer_step(first, rows, info, lengths, in_index, out_index, gain, held, chunks, micro_count, own_count):
+def layer_step(first, rows, info, lengths, in_index, out_index, gain, held, down, chunks, micro_count, own_count):
     shard_total = len(chunks)
     _, blocks, slots, block, _ = held.shape
     block_total = gain.shape[0]
     width = block_total * block // shard_total
-    unroll = 2 if blocks % 2 == 0 else 1
+    unroll = max(u for u in (1, 2, UNROLL) if blocks % u == 0)
     outs = [pltpu.VMEM((shard_total // 2, rows, width), bf16)] * 2
     if first:
         outs.append(pltpu.VMEM((rows, width), bf16))
+        outs.append(pltpu.VMEM(held.shape, bf16))
     return pl.pallas_call(
         functools.partial(layer_kernel, first, rows, unroll, shard_total, micro_count, own_count),
         out_shape=outs,
-        in_specs=[SMEM_SPEC] * 4 + [VMEM_SPEC] * (2 + shard_total),
+        in_specs=[SMEM_SPEC] * 4
+        + [VMEM_SPEC] * 2
+        + [ANY_SPEC] * first
+        + [VMEM_SPEC] * shard_total,
         out_specs=[VMEM_SPEC] * len(outs),
         scratch_shapes=[
             pltpu.VMEM((block_total + 1, rows, block), bf16),
             pltpu.VMEM((blocks, rows, block), bf16),
             pltpu.VMEM((block_total + 1, rows, block), f32),
-        ],
+        ]
+        + ([pltpu.SemaphoreType.DMA((blocks,))] if first else []),
         compiler_params=pltpu.CompilerParams(vmem_limit_bytes=vmem_limit(rows)),
         cost_estimate=pl.CostEstimate(
             flops=2 * rows * held.size, bytes_accessed=0, transcendentals=0
         ),
+        input_output_aliases={5: 3} if first else {},
         name="layer_first" if first else "layer",
-    )(info, lengths, in_index, out_index, gain, held, *map(in_vmem, chunks))
+    )(info, lengths, in_index, out_index, gain, held, *([down] if first else []), *map(in_vmem, chunks))
 
 
 def pair_kernel(held_ref, even_ref, came_ref, own_ref, *send_refs):
@@ -284,25 +338,25 @@
     rows = live_total(tokens.shape, shard_total)
     info = jnp.stack([lax.axis_index("shard"), section_id])
     gain = norm_gain.reshape(model_width // block, block)
-    held = load_weights(info, gate_tiles[0], up_tiles[0], down_tiles[0], rows)
-    held = in_vmem(held)
-    chunks = spread(tokens.reshape(micro_count * own_count, model_width))
+    held = in_vmem(load_weights(info, gate_tiles[0], up_tiles[0], rows))
+    own_tokens = tokens.reshape(micro_count * own_count, model_width)
+    came = same_core(own_tokens)[1:]
+    chunks = both_cores([own_tokens, *relay(held, came, rows)])
     for turn in range(section_total):
         first = turn == 0
         parts = layer_step(
-            first, rows, info, lengths, in_index[0], out_index[0], gain, held, chunks, micro_count, own_count
+            first, rows, info, lengths, in_index[0], out_index[0], gain, held, down_tiles[0], chunks, micro_count, own_count
         )
-        x_own = parts[2] if first else chunks[0]
+        if first:
+            x_own, kept, held = parts[2], parts[2], in_vmem(parts[3])
+        else:
+            x_own = chunks[0]
         sums = pair_sum(held, parts[0], xor_shard(parts[1], 1))
         came = [xor_shard(part, 2 * i + 2) for i, part in enumerate(sums[1:])]
-        kept = x_own if first else kept
         fresh, kept = finish_sum(turn, info, held, x_own, sums[0], came, kept)
         if turn + 1 < section_total:
-            moved = lax.ppermute(
-                fresh, "section", [(i, i + 1) for i in range(section_total - 1)]
-            )
-            chunks = spread(moved)
-    return result_rows(info, lengths, spread(kept), tokens.shape)[None]
+            chunks = both_cores(next_section(fresh, turn))
+    return result_rows(info, lengths, both_cores(same_core(kept)), tokens.shape)[None]
 
 
 def solution(mesh):

time: 166 us -> 145 us (0.87)
  waiting for transfers between devices: 61.1 us -> 47 us
  Pallas kernels: 65 us -> 58.5 us
    ppermute x51 -> x42, waiting for transfers between devices: 46.2 us -> 30.7 us  [xor_shard(): return lax.ppermute(value, 'shard', [(i, i ^ mask) for i in range(size)])]
    ppermute x51 -> x42, starting transfers between devices: 32.9 us -> 26 us  [xor_shard(): return lax.ppermute(value, 'shard', [(i, i ^ mask) for i in range(size)])]
    ppermute x3 -> x12, starting transfers between devices: 4.06 us -> 10.7 us  [next_section(): lax.ppermute(value, ('section', 'shard'), [(start + i, start + size + (i...]
    pallas_call x1, Pallas kernels: 14.8 us -> 10.3 us  [load_weights(): pl.pallas_call(load_kernel, out_shape=pltpu.VMEM(shape, bf16), in_specs=[...]
    pallas_call x4, Pallas kernels: 44.9 us -> 42.7 us  [layer_step(): pl.pallas_call(functools.partial(layer_kernel, first, rows, unroll, shard...]
    ppermute x3 -> x12, waiting for transfers between devices: 14.9 us -> 16.3 us  [next_section(): lax.ppermute(value, ('section', 'shard'), [(start + i, start + size + (i...]
  transfers between devices with their start and end apart: 54 -> 54, of which waited for: 40 -> 38; matrix products, arithmetic and copies ran while one was open for 0% -> 0% of each run, Pallas kernels for 9% -> 7%
where the time goes in v2:
time: 145 us; the launch traced here: 144 us
  Pallas kernels  58.5 us (40%)
  waiting for transfers between devices  47 us (32%)
  starting transfers between devices  36.7 us (25%)
    pallas_call x4, Pallas kernels, layer_step(): pl.pallas_call(functools.partial(layer_kernel, first, rows, unroll, shard...  42.7 us
    ppermute x42, waiting for transfers between devices, xor_shard(): return lax.ppermute(value, 'shard', [(i, i ^ mask) for i in range(size)])  30.7 us
    ppermute x42, starting transfers between devices, xor_shard(): return lax.ppermute(value, 'shard', [(i, i ^ mask) for i in range(size)])  26 us
    ppermute x12, waiting for transfers between devices, next_section(): lax.ppermute(value, ('section', 'shard'), [(start + i, start + size + (i...  16.3 us
    ppermute x12, starting transfers between devices, next_section(): lax.ppermute(value, ('section', 'shard'), [(start + i, start + size + (i...  10.7 us
    pallas_call x1, Pallas kernels, load_weights(): pl.pallas_call(load_kernel, out_shape=pltpu.VMEM(shape, bf16), in_specs=[...  10.3 us
    pallas_call x4, Pallas kernels, finish_sum(): pl.pallas_call(functools.partial(finish_kernel, turn), out_shape=[pltpu.V...  3.65 us
  transfers between devices with their start and end apart: 54, of which 38 were waited for; matrix products, arithmetic and copies ran while one was open for 0% of the time, Pallas kernels for 7%

profile of v2, /device:TPU:24, one launch (start us, length us, event | category | flops | bytes accessed | tf_op | source)
XLA Modules:
  0.0 144.1 jit_solution(16227676961535457259)
XLA Ops:
  1.0 2.5 %collective-permute-start.3 = (bf16[8,8192]{1,0:T(8,128)(2,1)S(1)}, bf16[8,8192]{1,0:T(8,128)(2,1)S(1)}, u32[]{:S(2)}, u32[]{:S(2)}) collective-permute-start(bf16[8,8192]{1,0:T(8,128)(2,1)S(1)} %reshape.7.refs_7_), channel_id=1, source_target_pairs={{0,6},{1,7},{2,4},{3,5},{4,2},{5,3},{6,0},{7,1},{8,14},{9,15},{10,... | collective-permute-start | bytes 393224 | tf_op jit(solution)/shard_map/ppermute | solution.py:27
  5.2 10.3 %load_weights.1.held_ref.refs_5_ = bf16[3,16,28,128,128]{4,3,2,1,0:T(8,128)(2,1)S(1)} custom-call(s32[2]{0:T(128)} %pad_add_fusion.info_ref.refs_0_, bf16[16,28,128,128]{3,2,1,0:T(8,128)(2,1)} %bitcast.10, bf16[16,28,128,128]{3,2,1,0:T(8,128)(2,1)} %bitcast.11), custom_call_target="tpu_custom_call" | custom-call | bytes 29360128 | tf_op jit(solution)/shard_map/load_weights/pallas_call | solution.py:84
  17.7 12.2 %layer_first.1 = (bf16[4,40,1024]{2,1,0:T(8,128)(2,1)S(1)}, bf16[4,40,1024]{2,1,0:T(8,128)(2,1)S(1)}, bf16[40,1024]{1,0:T(8,128)(2,1)S(1)}, bf16[3,16,28,128,128]{4,3,2,1,0:T(8,128)(2,1)S(1)}) custom-call(s32[2]{0:T(128)} %pad_add_fusion.info_ref.refs_0_, s32[4]{0:T(128)} %lengths_ref.1, s32[16,28]{1,0:T(8,128)} %bitcast.16, ...), custom_call_target="tpu_custom_call", output_to_operand_aliasing={{3}: (5, {})} | custom-call | flops 1761607680 | tf_op jit(solution)/shard_map/layer_first/pallas_call | solution.py:233
  30.2 1.3 collective-permute-done.7.came_ref
  31.6 1.5 %collective-permute-start.8 = (bf16[40,1024]{1,0:T(8,128)(2,1)S(1)}, bf16[40,1024]{1,0:T(8,128)(2,1)S(1)}, u32[]{:S(2)}, u32[]{:S(2)}) collective-permute-start(bf16[40,1024]{1,0:T(8,128)(2,1)S(1)} %get-tuple-element.49), channel_id=1, source_target_pairs={{0,2},{1,3},{2,0},{3,1},{4,6},{5,7},{6,4},{7,5},{8,10},{9,11},{10,... | collective-permute-start | bytes 245768 | tf_op jit(solution)/shard_map/ppermute | solution.py:27
  33.2 1.5 %collective-permute-start.9 = (bf16[40,1024]{1,0:T(8,128)(2,1)S(1)}, bf16[40,1024]{1,0:T(8,128)(2,1)S(1)}, u32[]{:S(2)}, u32[]{:S(2)}) collective-permute-start(bf16[40,1024]{1,0:T(8,128)(2,1)S(1)} %get-tuple-element.50), channel_id=1, source_target_pairs={{0,4},{1,5},{2,6},{3,7},{4,0},{5,1},{6,2},{7,3},{8,12},{9,13},{10,... | collective-permute-start | bytes 245768 | tf_op jit(solution)/shard_map/ppermute | solution.py:27
  36.3 2.1 %collective-permute-done.9.refs_1_ = bf16[40,1024]{1,0:T(8,128)(2,1)S(1)} collective-permute-done((bf16[40,1024]{1,0:T(8,128)(2,1)S(1)}, bf16[40,1024]{1,0:T(8,128)(2,1)S(1)}, u32[]{:S(2)}, u32[]{:S(2)}) %collective-permute-start.9) | collective-permute-done | bytes 81952 | tf_op jit(solution)/shard_map/ppermute | solution.py:27
  38.4 1.6 %collective-permute-done.10.refs_2_ = bf16[40,1024]{1,0:T(8,128)(2,1)S(1)} collective-permute-done((bf16[40,1024]{1,0:T(8,128)(2,1)S(1)}, bf16[40,1024]{1,0:T(8,128)(2,1)S(1)}, u32[]{:S(2)}, u32[]{:S(2)}) %collective-permute-start.10) | collective-permute-done | bytes 81952 | tf_op jit(solution)/shard_map/ppermute | solution.py:27
  45.5 10.2 %layer.3 = (bf16[4,40,1024]{2,1,0:T(8,128)(2,1)S(1)}, bf16[4,40,1024]{2,1,0:T(8,128)(2,1)S(1)}) custom-call(s32[2]{0:T(128)} %pad_add_fusion.info_ref.refs_0_, s32[4]{0:T(128)} %lengths_ref.1, s32[16,28]{1,0:T(8,128)} %bitcast.17, s32[16,28]{1,0:T(8,128)} %bitcast.21, f32[64,128]{1,0:T(8,128)} %bitcast.13, ...), custom_call_target="tpu_custom_call" | custom-call | flops 1761607680 | tf_op jit(solution)/shard_map/layer/pallas_call | solution.py:233
  56.0 1.3 collective-permute-done.19.came_ref
  58.9 2.0 %collective-permute-start.22 = (bf16[40,1024]{1,0:T(8,128)(2,1)S(1)}, bf16[40,1024]{1,0:T(8,128)(2,1)S(1)}, u32[]{:S(2)}, u32[]{:S(2)}) collective-permute-start(bf16[40,1024]{1,0:T(8,128)(2,1)S(1)} %get-tuple-element.58), channel_id=1, source_target_pairs={{0,6},{1,7},{2,4},{3,5},{4,2},{5,3},{6,0},{7,1},{8,14},{9,15},{10,... | collective-permute-start | bytes 245768 | tf_op jit(solution)/shard_map/ppermute | solution.py:27
  61.0 1.5 %collective-permute-done.20.refs_0_ = bf16[40,1024]{1,0:T(8,128)(2,1)S(1)} collective-permute-done((bf16[40,1024]{1,0:T(8,128)(2,1)S(1)}, bf16[40,1024]{1,0:T(8,128)(2,1)S(1)}, u32[]{:S(2)}, u32[]{:S(2)}) %collective-permute-start.20) | collective-permute-done | bytes 81952 | tf_op jit(solution)/shard_map/ppermute | solution.py:27
  63.0 1.3 collective-permute-done.22.refs_2_
  69.7 10.2 %layer.4 = (bf16[4,40,1024]{2,1,0:T(8,128)(2,1)S(1)}, bf16[4,40,1024]{2,1,0:T(8,128)(2,1)S(1)}) custom-call(s32[2]{0:T(128)} %pad_add_fusion.info_ref.refs_0_, s32[4]{0:T(128)} %lengths_ref.1, s32[16,28]{1,0:T(8,128)} %bitcast.18, s32[16,28]{1,0:T(8,128)} %bitcast.22, f32[64,128]{1,0:T(8,128)} %bitcast.14, ...), custom_call_target="tpu_custom_call" | custom-call | flops 1761607680 | tf_op jit(solution)/shard_map/layer/pallas_call | solution.py:233
  80.3 1.3 collective-permute-done.31.came_ref
  81.7 1.5 %collective-permute-start.32 = (bf16[40,1024]{1,0:T(8,128)(2,1)S(1)}, bf16[40,1024]{1,0:T(8,128)(2,1)S(1)}, u32[]{:S(2)}, u32[]{:S(2)}) collective-permute-start(bf16[40,1024]{1,0:T(8,128)(2,1)S(1)} %get-tuple-element.64), channel_id=1, source_target_pairs={{0,2},{1,3},{2,0},{3,1},{4,6},{5,7},{6,4},{7,5},{8,10},{9,11},{10,... | collective-permute-start | bytes 245768 | tf_op jit(solution)/shard_map/ppermute | solution.py:27
  86.4 1.2 collective-permute-done.33.refs_1_
  87.6 2.1 %collective-permute-done.34.refs_2_ = bf16[40,1024]{1,0:T(8,128)(2,1)S(1)} collective-permute-done((bf16[40,1024]{1,0:T(8,128)(2,1)S(1)}, bf16[40,1024]{1,0:T(8,128)(2,1)S(1)}, u32[]{:S(2)}, u32[]{:S(2)}) %collective-permute-start.34) | collective-permute-done | bytes 81952 | tf_op jit(solution)/shard_map/ppermute | solution.py:27
  90.5 1.3 collective-permute-start.41
  91.8 1.3 collective-permute-start.39
  93.1 1.3 collective-permute-start.37
  94.4 1.5 %collective-permute-start.35 = (bf16[40,1024]{1,0:T(8,128)(2,1)S(1)}, bf16[40,1024]{1,0:T(8,128)(2,1)S(1)}, u32[]{:S(2)}, u32[]{:S(2)}) collective-permute-start(bf16[40,1024]{1,0:T(8,128)(2,1)S(1)} %get-tuple-element.68), channel_id=1, source_target_pairs={{16,24},{17,25},{18,26},{19,27},{20,28},{21,29},{22,30},{23,31}} | collective-permute-start | bytes 245768 | tf_op jit(solution)/shard_map/ppermute | solution.py:39
  95.8 13.6 %collective-permute-done.41.refs_12_ = bf16[40,1024]{1,0:T(8,128)(2,1)S(1)} collective-permute-done((bf16[40,1024]{1,0:T(8,128)(2,1)S(1)}, bf16[40,1024]{1,0:T(8,128)(2,1)S(1)}, u32[]{:S(2)}, u32[]{:S(2)}) %collective-permute-start.41) | collective-permute-done | bytes 81952 | tf_op jit(solution)/shard_map/ppermute | solution.py:39
  110.6 1.2 collective-permute-done.37.refs_8_
  113.4 10.2 %layer.5 = (bf16[4,40,1024]{2,1,0:T(8,128)(2,1)S(1)}, bf16[4,40,1024]{2,1,0:T(8,128)(2,1)S(1)}) custom-call(s32[2]{0:T(128)} %pad_add_fusion.info_ref.refs_0_, s32[4]{0:T(128)} %lengths_ref.1, s32[16,28]{1,0:T(8,128)} %bitcast.19, s32[16,28]{1,0:T(8,128)} %bitcast.23, f32[64,128]{1,0:T(8,128)} %bitcast.15, ...), custom_call_target="tpu_custom_call" | custom-call | flops 1761607680 | tf_op jit(solution)/shard_map/layer/pallas_call | solution.py:233
  123.9 1.5 %collective-permute-done.43.came_ref = bf16[4,40,1024]{2,1,0:T(8,128)(2,1)S(1)} collective-permute-done((bf16[4,40,1024]{2,1,0:T(8,128)(2,1)S(1)}, bf16[4,40,1024]{2,1,0:T(8,128)(2,1)S(1)}, u32[]{:S(2)}, u32[]{:S(2)}) %collective-permute-start.43) | collective-permute-done | bytes 327712 | tf_op jit(solution)/shard_map/ppermute | solution.py:27
  127.8 1.2 collective-permute-start.46
  130.0 1.9 %collective-permute-done.45.refs_1_ = bf16[40,1024]{1,0:T(8,128)(2,1)S(1)} collective-permute-done((bf16[40,1024]{1,0:T(8,128)(2,1)S(1)}, bf16[40,1024]{1,0:T(8,128)(2,1)S(1)}, u32[]{:S(2)}, u32[]{:S(2)}) %collective-permute-start.45) | collective-permute-done | bytes 81952 | tf_op jit(solution)/shard_map/ppermute | solution.py:27
  133.1 1.5 %finish_sum.7 = (bf16[40,1024]{1,0:T(8,128)(2,1)}, bf16[40,1024]{1,0:T(8,128)(2,1)S(1)}) custom-call(s32[2]{0:T(128)} %pad_add_fusion.info_ref.refs_0_, bf16[3,16,28,128,128]{4,3,2,1,0:T(8,128)(2,1)S(1)} %get-tuple-element.44.held_ref.refs_5_, bf16[40,1024]{1,0:T(8,128)(2,1)S(1)} %collective-permute-done.35.refs_6_.x_ref, ...), custom_call_target="tpu_custom_call" | custom-call | tf_op jit(solution)/shard_map/finish_sum/pallas_call | solution.py:287
  134.6 1.2 collective-permute-start.52
  138.1 1.9 %collective-permute-done.52.refs_6_ = bf16[40,1024]{1,0:T(8,128)(2,1)S(1)} collective-permute-done((bf16[40,1024]{1,0:T(8,128)(2,1)S(1)}, bf16[40,1024]{1,0:T(8,128)(2,1)S(1)}, u32[]{:S(2)}, u32[]{:S(2)}) %collective-permute-start.52) | collective-permute-done | bytes 81952 | tf_op jit(solution)/shard_map/ppermute | solution.py:27
  142.7 1.4 %result_rows.1 = bf16[4,2,8192]{2,1,0:T(2,128)(2,1)} custom-call(s32[2]{0:T(128)S(1)} %copy-done, s32[4]{0:T(128)S(1)} %copy-done.1, bf16[40,1024]{1,0:T(8,128)(2,1)S(1)} %get-tuple-element.76.refs_0_, bf16[40,1024]{1,0:T(8,128)(2,1)S(1)} %collective-permute-done.47.refs_1_, bf16[40,1024]{1,0:T(8,128)(2,1)S(1)} %collective-permute-done.48.refs_2_, ...), custom_call_target="tpu_custom_call" | custom-call | tf_op jit(solution)/shard_map/result_rows/pallas_call | solution.py:322
  (97 shorter events, 37.2 us)
Async XLA Ops:
  1.0 14.5 %collective-permute-start.3 = (bf16[8,8192]{1,0:T(8,128)(2,1)S(1)}, bf16[8,8192]{1,0:T(8,128)(2,1)S(1)}, u32[]{:S(2)}, u32[]{:S(2)}) collective-permute-start(bf16[8,8192]{1,0:T(8,128)(2,1)S(1)} %reshape.7.refs_7_), channel_id=1, source_target_pairs={{0,6},{1,7},{2,4},{3,5},{4,2},{5,3},{6,0},{7,1},{8,14},{9,15},{10,... | collective-permute-start | bytes 393224 | tf_op jit(solution)/shard_map/ppermute | solution.py:27
  3.5 12.0 %collective-permute-start.2 = (bf16[8,8192]{1,0:T(8,128)(2,1)S(1)}, bf16[8,8192]{1,0:T(8,128)(2,1)S(1)}, u32[]{:S(2)}, u32[]{:S(2)}) collective-permute-start(bf16[8,8192]{1,0:T(8,128)(2,1)S(1)} %reshape.7.refs_7_), channel_id=1, source_target_pairs={{0,4},{1,5},{2,6},{3,7},{4,0},{5,1},{6,2},{7,3},{8,12},{9,13},{10,... | collective-permute-start | bytes 393224 | tf_op jit(solution)/shard_map/ppermute | solution.py:27
  4.0 11.5 %collective-permute-start.1 = (bf16[8,8192]{1,0:T(8,128)(2,1)S(1)}, bf16[8,8192]{1,0:T(8,128)(2,1)S(1)}, u32[]{:S(2)}, u32[]{:S(2)}) collective-permute-start(bf16[8,8192]{1,0:T(8,128)(2,1)S(1)} %reshape.7.refs_7_), channel_id=1, source_target_pairs={{0,2},{1,3},{2,0},{3,1},{4,6},{5,7},{6,4},{7,5},{8,10},{9,11},{10,... | collective-permute-start | bytes 393224 | tf_op jit(solution)/shard_map/ppermute | solution.py:27
  4.5 12.1 %collective-permute-start = (bf16[8,8192]{1,0:T(8,128)(2,1)S(1)}, bf16[8,8192]{1,0:T(8,128)(2,1)S(1)}, u32[]{:S(2)}, u32[]{:S(2)}) collective-permute-start(bf16[8,8192]{1,0:T(8,128)(2,1)S(1)} %reshape.7.refs_7_), channel_id=1, source_target_pairs={{0,1},{1,0},{2,3},{3,2},{4,5},{5,4},{6,7},{7,6},{8,9},{9,8},{10,11... | collective-permute-start | bytes 393224 | tf_op jit(solution)/shard_map/ppermute | solution.py:27
  31.6 4.7 %collective-permute-start.8 = (bf16[40,1024]{1,0:T(8,128)(2,1)S(1)}, bf16[40,1024]{1,0:T(8,128)(2,1)S(1)}, u32[]{:S(2)}, u32[]{:S(2)}) collective-permute-start(bf16[40,1024]{1,0:T(8,128)(2,1)S(1)} %get-tuple-element.49), channel_id=1, source_target_pairs={{0,2},{1,3},{2,0},{3,1},{4,6},{5,7},{6,4},{7,5},{8,10},{9,11},{10,... | collective-permute-start | bytes 245768 | tf_op jit(solution)/shard_map/ppermute | solution.py:27
  33.2 5.3 %collective-permute-start.9 = (bf16[40,1024]{1,0:T(8,128)(2,1)S(1)}, bf16[40,1024]{1,0:T(8,128)(2,1)S(1)}, u32[]{:S(2)}, u32[]{:S(2)}) collective-permute-start(bf16[40,1024]{1,0:T(8,128)(2,1)S(1)} %get-tuple-element.50), channel_id=1, source_target_pairs={{0,4},{1,5},{2,6},{3,7},{4,0},{5,1},{6,2},{7,3},{8,12},{9,13},{10,... | collective-permute-start | bytes 245768 | tf_op jit(solution)/shard_map/ppermute | solution.py:27
  34.7 5.3 %collective-permute-start.10 = (bf16[40,1024]{1,0:T(8,128)(2,1)S(1)}, bf16[40,1024]{1,0:T(8,128)(2,1)S(1)}, u32[]{:S(2)}, u32[]{:S(2)}) collective-permute-start(bf16[40,1024]{1,0:T(8,128)(2,1)S(1)} %get-tuple-element.51), channel_id=1, source_target_pairs={{0,6},{1,7},{2,4},{3,5},{4,2},{5,3},{6,0},{7,1},{8,14},{9,15},{10,... | collective-permute-start | bytes 245768 | tf_op jit(solution)/shard_map/ppermute | solution.py:27
  40.7 2.7 %collective-permute-start.17 = (bf16[40,1024]{1,0:T(8,128)(2,1)S(1)}, bf16[40,1024]{1,0:T(8,128)(2,1)S(1)}, u32[]{:S(2)}, u32[]{:S(2)}) collective-permute-start(bf16[40,1024]{1,0:T(8,128)(2,1)S(1)} %get-tuple-element.52), channel_id=1, source_target_pairs={{0,14},{1,15},{2,12},{3,13},{4,10},{5,11},{6,8},{7,9}} | collective-permute-start | bytes 245768 | tf_op jit(solution)/shard_map/ppermute | solution.py:39
  41.4 2.1 %collective-permute-start.15 = (bf16[40,1024]{1,0:T(8,128)(2,1)S(1)}, bf16[40,1024]{1,0:T(8,128)(2,1)S(1)}, u32[]{:S(2)}, u32[]{:S(2)}) collective-permute-start(bf16[40,1024]{1,0:T(8,128)(2,1)S(1)} %get-tuple-element.52), channel_id=1, source_target_pairs={{0,12},{1,13},{2,14},{3,15},{4,8},{5,9},{6,10},{7,11}} | collective-permute-start | bytes 245768 | tf_op jit(solution)/shard_map/ppermute | solution.py:39
  42.1 1.9 %collective-permute-start.13 = (bf16[40,1024]{1,0:T(8,128)(2,1)S(1)}, bf16[40,1024]{1,0:T(8,128)(2,1)S(1)}, u32[]{:S(2)}, u32[]{:S(2)}) collective-permute-start(bf16[40,1024]{1,0:T(8,128)(2,1)S(1)} %get-tuple-element.52), channel_id=1, source_target_pairs={{0,10},{1,11},{2,8},{3,9},{4,14},{5,15},{6,12},{7,13}} | collective-permute-start | bytes 245768 | tf_op jit(solution)/shard_map/ppermute | solution.py:39
  57.4 5.0 %collective-permute-start.20 = (bf16[40,1024]{1,0:T(8,128)(2,1)S(1)}, bf16[40,1024]{1,0:T(8,128)(2,1)S(1)}, u32[]{:S(2)}, u32[]{:S(2)}) collective-permute-start(bf16[40,1024]{1,0:T(8,128)(2,1)S(1)} %get-tuple-element.56), channel_id=1, source_target_pairs={{0,2},{1,3},{2,0},{3,1},{4,6},{5,7},{6,4},{7,5},{8,10},{9,11},{10,... | collective-permute-start | bytes 245768 | tf_op jit(solution)/shard_map/ppermute | solution.py:27
  58.1 4.9 %collective-permute-start.21 = (bf16[40,1024]{1,0:T(8,128)(2,1)S(1)}, bf16[40,1024]{1,0:T(8,128)(2,1)S(1)}, u32[]{:S(2)}, u32[]{:S(2)}) collective-permute-start(bf16[40,1024]{1,0:T(8,128)(2,1)S(1)} %get-tuple-element.57), channel_id=1, source_target_pairs={{0,4},{1,5},{2,6},{3,7},{4,0},{5,1},{6,2},{7,3},{8,12},{9,13},{10,... | collective-permute-start | bytes 245768 | tf_op jit(solution)/shard_map/ppermute | solution.py:27
  58.9 5.3 %collective-permute-start.22 = (bf16[40,1024]{1,0:T(8,128)(2,1)S(1)}, bf16[40,1024]{1,0:T(8,128)(2,1)S(1)}, u32[]{:S(2)}, u32[]{:S(2)}) collective-permute-start(bf16[40,1024]{1,0:T(8,128)(2,1)S(1)} %get-tuple-element.58), channel_id=1, source_target_pairs={{0,6},{1,7},{2,4},{3,5},{4,2},{5,3},{6,0},{7,1},{8,14},{9,15},{10,... | collective-permute-start | bytes 245768 | tf_op jit(solution)/shard_map/ppermute | solution.py:27
  65.0 2.7 %collective-permute-start.29 = (bf16[40,1024]{1,0:T(8,128)(2,1)S(1)}, bf16[40,1024]{1,0:T(8,128)(2,1)S(1)}, u32[]{:S(2)}, u32[]{:S(2)}) collective-permute-start(bf16[40,1024]{1,0:T(8,128)(2,1)S(1)} %get-tuple-element.60), channel_id=1, source_target_pairs={{8,22},{9,23},{10,20},{11,21},{12,18},{13,19},{14,16},{15,17}} | collective-permute-start | bytes 245768 | tf_op jit(solution)/shard_map/ppermute | solution.py:39
  65.7 2.1 %collective-permute-start.27 = (bf16[40,1024]{1,0:T(8,128)(2,1)S(1)}, bf16[40,1024]{1,0:T(8,128)(2,1)S(1)}, u32[]{:S(2)}, u32[]{:S(2)}) collective-permute-start(bf16[40,1024]{1,0:T(8,128)(2,1)S(1)} %get-tuple-element.60), channel_id=1, source_target_pairs={{8,20},{9,21},{10,22},{11,23},{12,16},{13,17},{14,18},{15,19}} | collective-permute-start | bytes 245768 | tf_op jit(solution)/shard_map/ppermute | solution.py:39
  66.4 1.9 %collective-permute-start.25 = (bf16[40,1024]{1,0:T(8,128)(2,1)S(1)}, bf16[40,1024]{1,0:T(8,128)(2,1)S(1)}, u32[]{:S(2)}, u32[]{:S(2)}) collective-permute-start(bf16[40,1024]{1,0:T(8,128)(2,1)S(1)} %get-tuple-element.60), channel_id=1, source_target_pairs={{8,18},{9,19},{10,16},{11,17},{12,22},{13,23},{14,20},{15,21}} | collective-permute-start | bytes 245768 | tf_op jit(solution)/shard_map/ppermute | solution.py:39
  81.7 4.7 %collective-permute-start.32 = (bf16[40,1024]{1,0:T(8,128)(2,1)S(1)}, bf16[40,1024]{1,0:T(8,128)(2,1)S(1)}, u32[]{:S(2)}, u32[]{:S(2)}) collective-permute-start(bf16[40,1024]{1,0:T(8,128)(2,1)S(1)} %get-tuple-element.64), channel_id=1, source_target_pairs={{0,2},{1,3},{2,0},{3,1},{4,6},{5,7},{6,4},{7,5},{8,10},{9,11},{10,... | collective-permute-start | bytes 245768 | tf_op jit(solution)/shard_map/ppermute | solution.py:27
  83.2 4.4 %collective-permute-start.33 = (bf16[40,1024]{1,0:T(8,128)(2,1)S(1)}, bf16[40,1024]{1,0:T(8,128)(2,1)S(1)}, u32[]{:S(2)}, u32[]{:S(2)}) collective-permute-start(bf16[40,1024]{1,0:T(8,128)(2,1)S(1)} %get-tuple-element.65), channel_id=1, source_target_pairs={{0,4},{1,5},{2,6},{3,7},{4,0},{5,1},{6,2},{7,3},{8,12},{9,13},{10,... | collective-permute-start | bytes 245768 | tf_op jit(solution)/shard_map/ppermute | solution.py:27
  84.4 5.3 %collective-permute-start.34 = (bf16[40,1024]{1,0:T(8,128)(2,1)S(1)}, bf16[40,1024]{1,0:T(8,128)(2,1)S(1)}, u32[]{:S(2)}, u32[]{:S(2)}) collective-permute-start(bf16[40,1024]{1,0:T(8,128)(2,1)S(1)} %get-tuple-element.66), channel_id=1, source_target_pairs={{0,6},{1,7},{2,4},{3,5},{4,2},{5,3},{6,0},{7,1},{8,14},{9,15},{10,... | collective-permute-start | bytes 245768 | tf_op jit(solution)/shard_map/ppermute | solution.py:27
  90.5 19.0 %collective-permute-start.41 = (bf16[40,1024]{1,0:T(8,128)(2,1)S(1)}, bf16[40,1024]{1,0:T(8,128)(2,1)S(1)}, u32[]{:S(2)}, u32[]{:S(2)}) collective-permute-start(bf16[40,1024]{1,0:T(8,128)(2,1)S(1)} %get-tuple-element.68), channel_id=1, source_target_pairs={{16,30},{17,31},{18,28},{19,29},{20,26},{21,27},{22,24},{23,25}} | collective-permute-start | bytes 245768 | tf_op jit(solution)/shard_map/ppermute | solution.py:39
  91.8 18.9 %collective-permute-start.39 = (bf16[40,1024]{1,0:T(8,128)(2,1)S(1)}, bf16[40,1024]{1,0:T(8,128)(2,1)S(1)}, u32[]{:S(2)}, u32[]{:S(2)}) collective-permute-start(bf16[40,1024]{1,0:T(8,128)(2,1)S(1)} %get-tuple-element.68), channel_id=1, source_target_pairs={{16,28},{17,29},{18,30},{19,31},{20,24},{21,25},{22,26},{23,27}} | collective-permute-start | bytes 245768 | tf_op jit(solution)/shard_map/ppermute | solution.py:39
  93.1 18.8 %collective-permute-start.37 = (bf16[40,1024]{1,0:T(8,128)(2,1)S(1)}, bf16[40,1024]{1,0:T(8,128)(2,1)S(1)}, u32[]{:S(2)}, u32[]{:S(2)}) collective-permute-start(bf16[40,1024]{1,0:T(8,128)(2,1)S(1)} %get-tuple-element.68), channel_id=1, source_target_pairs={{16,26},{17,27},{18,24},{19,25},{20,30},{21,31},{22,28},{23,29}} | collective-permute-start | bytes 245768 | tf_op jit(solution)/shard_map/ppermute | solution.py:39
  94.4 17.8 %collective-permute-start.35 = (bf16[40,1024]{1,0:T(8,128)(2,1)S(1)}, bf16[40,1024]{1,0:T(8,128)(2,1)S(1)}, u32[]{:S(2)}, u32[]{:S(2)}) collective-permute-start(bf16[40,1024]{1,0:T(8,128)(2,1)S(1)} %get-tuple-element.68), channel_id=1, source_target_pairs={{16,24},{17,25},{18,26},{19,27},{20,28},{21,29},{22,30},{23,31}} | collective-permute-start | bytes 245768 | tf_op jit(solution)/shard_map/ppermute | solution.py:39
  109.5 2.9 %collective-permute-start.42 = (bf16[40,1024]{1,0:T(8,128)(2,1)S(1)}, bf16[40,1024]{1,0:T(8,128)(2,1)S(1)}, u32[]{:S(2)}, u32[]{:S(2)}) collective-permute-start(bf16[40,1024]{1,0:T(8,128)(2,1)S(1)} %collective-permute-done.41.refs_12_), channel_id=1, source_target_pairs={{0,1},{1,0},{2,3},{3,2},{4,5},{5,4},{6,7},{7,6},{8,9},{9,8},{10,11... | collective-permute-start | bytes 245768 | tf_op jit(solution)/shard_map/ppermute | solution.py:27
  110.6 1.7 %collective-permute-start.40 = (bf16[40,1024]{1,0:T(8,128)(2,1)S(1)}, bf16[40,1024]{1,0:T(8,128)(2,1)S(1)}, u32[]{:S(2)}, u32[]{:S(2)}) collective-permute-start(bf16[40,1024]{1,0:T(8,128)(2,1)S(1)} %collective-permute-done.39.refs_10_), channel_id=1, source_target_pairs={{0,1},{1,0},{2,3},{3,2},{4,5},{5,4},{6,7},{7,6},{8,9},{9,8},{10,11... | collective-permute-start | bytes 245768 | tf_op jit(solution)/shard_map/ppermute | solution.py:27
  125.4 4.6 %collective-permute-start.44 = (bf16[40,1024]{1,0:T(8,128)(2,1)S(1)}, bf16[40,1024]{1,0:T(8,128)(2,1)S(1)}, u32[]{:S(2)}, u32[]{:S(2)}) collective-permute-start(bf16[40,1024]{1,0:T(8,128)(2,1)S(1)} %get-tuple-element.72), channel_id=1, source_target_pairs={{0,2},{1,3},{2,0},{3,1},{4,6},{5,7},{6,4},{7,5},{8,10},{9,11},{10,... | collective-permute-start | bytes 245768 | tf_op jit(solution)/shard_map/ppermute | solution.py:27
  126.6 5.3 %collective-permute-start.45 = (bf16[40,1024]{1,0:T(8,128)(2,1)S(1)}, bf16[40,1024]{1,0:T(8,128)(2,1)S(1)}, u32[]{:S(2)}, u32[]{:S(2)}) collective-permute-start(bf16[40,1024]{1,0:T(8,128)(2,1)S(1)} %get-tuple-element.73), channel_id=1, source_target_pairs={{0,4},{1,5},{2,6},{3,7},{4,0},{5,1},{6,2},{7,3},{8,12},{9,13},{10,... | collective-permute-start | bytes 245768 | tf_op jit(solution)/shard_map/ppermute | solution.py:27
  127.8 5.3 %collective-permute-start.46 = (bf16[40,1024]{1,0:T(8,128)(2,1)S(1)}, bf16[40,1024]{1,0:T(8,128)(2,1)S(1)}, u32[]{:S(2)}, u32[]{:S(2)}) collective-permute-start(bf16[40,1024]{1,0:T(8,128)(2,1)S(1)} %get-tuple-element.74), channel_id=1, source_target_pairs={{0,6},{1,7},{2,4},{3,5},{4,2},{5,3},{6,0},{7,1},{8,14},{9,15},{10,... | collective-permute-start | bytes 245768 | tf_op jit(solution)/shard_map/ppermute | solution.py:27
  134.6 5.4 %collective-permute-start.52 = (bf16[40,1024]{1,0:T(8,128)(2,1)S(1)}, bf16[40,1024]{1,0:T(8,128)(2,1)S(1)}, u32[]{:S(2)}, u32[]{:S(2)}) collective-permute-start(bf16[40,1024]{1,0:T(8,128)(2,1)S(1)} %get-tuple-element.76.refs_0_), channel_id=1, source_target_pairs={{0,6},{1,7},{2,4},{3,5},{4,2},{5,3},{6,0},{7,1},{8,14},{9,15},{10,... | collective-permute-start | bytes 245768 | tf_op jit(solution)/shard_map/ppermute | solution.py:27
  135.8 5.0 %collective-permute-start.50 = (bf16[40,1024]{1,0:T(8,128)(2,1)S(1)}, bf16[40,1024]{1,0:T(8,128)(2,1)S(1)}, u32[]{:S(2)}, u32[]{:S(2)}) collective-permute-start(bf16[40,1024]{1,0:T(8,128)(2,1)S(1)} %get-tuple-element.76.refs_0_), channel_id=1, source_target_pairs={{0,4},{1,5},{2,6},{3,7},{4,0},{5,1},{6,2},{7,3},{8,12},{9,13},{10,... | collective-permute-start | bytes 245768 | tf_op jit(solution)/shard_map/ppermute | solution.py:27
  136.9 4.4 %collective-permute-start.48 = (bf16[40,1024]{1,0:T(8,128)(2,1)S(1)}, bf16[40,1024]{1,0:T(8,128)(2,1)S(1)}, u32[]{:S(2)}, u32[]{:S(2)}) collective-permute-start(bf16[40,1024]{1,0:T(8,128)(2,1)S(1)} %get-tuple-element.76.refs_0_), channel_id=1, source_target_pairs={{0,2},{1,3},{2,0},{3,1},{4,6},{5,7},{6,4},{7,5},{8,10},{9,11},{10,... | collective-permute-start | bytes 245768 | tf_op jit(solution)/shard_map/ppermute | solution.py:27
  138.1 3.3 %collective-permute-start.47 = (bf16[40,1024]{1,0:T(8,128)(2,1)S(1)}, bf16[40,1024]{1,0:T(8,128)(2,1)S(1)}, u32[]{:S(2)}, u32[]{:S(2)}) collective-permute-start(bf16[40,1024]{1,0:T(8,128)(2,1)S(1)} %get-tuple-element.76.refs_0_), channel_id=1, source_target_pairs={{0,1},{1,0},{2,3},{3,2},{4,5},{5,4},{6,7},{7,6},{8,9},{9,8},{10,11... | collective-permute-start | bytes 245768 | tf_op jit(solution)/shard_map/ppermute | solution.py:27
  (24 other events, 50.3 us)

commit v3 on v2

v3 whole, which is shorter than its diff:
```python
import functools

import jax
import jax.numpy as jnp
from jax import lax
from jax.experimental import pallas as pl
from jax.experimental.pallas import tpu as pltpu
from jax.sharding import PartitionSpec as P

norm_eps = 1e-05
f32 = jnp.float32
bf16 = jnp.bfloat16
MIB = 2**20
VMEM_SPEC = pl.BlockSpec(memory_space=pltpu.VMEM)
SMEM_SPEC = pl.BlockSpec(memory_space=pltpu.SMEM)
ANY_SPEC = pl.BlockSpec(memory_space=pl.ANY)


def live_total(tokens_shape, shard_total):
    micro_count, own_count, _ = tokens_shape
    return micro_count * own_count * shard_total * 5 // 8


def xor_shard(value, mask):
    size = lax.axis_size("shard")
    return lax.ppermute(value, "shard", [(i, i ^ mask) for i in range(size)])


def same_core(value):
    size = lax.axis_size("shard")
    return [value] + [xor_shard(value, mask) for mask in range(2, size, 2)]


def next_section(value, turn):
    size = lax.axis_size("shard")
    start = turn * size
    return [
        lax.ppermute(
            value,
            ("section", "shard"),
            [(start + i, start + size + (i ^ mask)) for i in range(size)],
        )
        for mask in range(0, size, 2)
    ]


def both_cores(parts):
    other_core = [xor_shard(part, 1) for part in parts]
    return [part for pair in zip(parts, other_core) for part in pair]


def vmem_limit(rows):
    return (12 if rows <= 64 else 32) * MIB


def in_vmem(value):
    return pltpu.with_memory_space_constraint(value, pltpu.VMEM)


def preloaded(blocks):
    return blocks // 2


def load_kernel(gate_ref, up_ref, held_ref, sems):
    early = preloaded(gate_ref.shape[0])

    def copies(h):
        return [
            pltpu.make_async_copy(ref.at[h], held_ref.at[i, h], sems.at[i, h])
            for i, ref in enumerate((gate_ref, up_ref))
        ]

    @pl.loop(0, early)
    def _(h):
        for copy in copies(h):
            copy.start()

    @pl.loop(0, early)
    def _(h):
        for copy in copies(h):
            copy.wait()


def load_weights(gate, up, rows):
    early = preloaded(gate.shape[0])
    return pl.pallas_call(
        load_kernel,
        out_shape=pltpu.VMEM((3,) + gate.shape, bf16),
        in_specs=[ANY_SPEC] * 2,
        out_specs=VMEM_SPEC,
        scratch_shapes=[pltpu.SemaphoreType.DMA((2, early))],
        compiler_params=pltpu.CompilerParams(vmem_limit_bytes=vmem_limit(rows)),
        cost_estimate=pl.CostEstimate(
            flops=0,
            bytes_accessed=4 * gate.size,
            transcendentals=0,
        ),
        name="load_weights",
    )(gate, up)


def relay_kernel(held_ref, *refs):
    half = len(refs) // 2
    for source, target in zip(refs[:half], refs[half:]):
        target[...] = source[...]


def relay(held, parts, rows):
    return pl.pallas_call(
        relay_kernel,
        out_shape=[pltpu.VMEM(part.shape, part.dtype) for part in parts],
        in_specs=[VMEM_SPEC] * (1 + len(parts)),
        out_specs=[VMEM_SPEC] * len(parts),
        compiler_params=pltpu.CompilerParams(vmem_limit_bytes=vmem_limit(rows)),
        name="relay",
    )(held, *map(in_vmem, parts))


def row_starts(lengths_ref, micro_count):
    starts = [jnp.int32(0)]
    for m in range(micro_count):
        starts.append(starts[-1] + lengths_ref[m])
    return starts


def own_rows(device, lengths_ref, rows, micro_count, own_count):
    starts = row_starts(lengths_ref, micro_count)
    group = micro_count * own_count
    place = lax.broadcasted_iota(jnp.int32, (group, rows), 1)
    local = lax.broadcasted_iota(jnp.int32, (group, rows), 0)
    target = jnp.full((group, rows), -1, jnp.int32)
    for m in range(micro_count):
        for q in range(own_count):
            row = device * own_count + q
            to = jnp.where(row < lengths_ref[m], starts[m] + row, -1)
            target = jnp.where(local == m * own_count + q, to, target)
    return (target == place).astype(f32)


def layer_kernel(turn, last, rows, unroll, shard_total, micro_count, own_count, *refs):
    first = turn == 0
    lengths_ref, in_ref, out_ref, gain_ref, held_ref = refs[:5]
    rest = list(refs[5:])
    sources = [rest.pop(0) for _ in range(3)] if first else None
    shard_id = lax.axis_index("shard")
    active = lax.axis_index("section") == turn
    blocks, slots, block = held_ref.shape[1], held_ref.shape[2], held_ref.shape[4]
    block_total = gain_ref.shape[0]
    chunk_blocks = block_total // shard_total
    chunks = [rest.pop(0) for _ in range(shard_total)]
    back_in_ref = None if first else rest.pop(0)
    even_ref, odd_ref = rest.pop(0), rest.pop(0)
    back_ref = None if first else rest.pop(0)
    if first:
        own_ref, filled_ref = rest.pop(0), rest.pop(0)
        sems = rest.pop()

        early = preloaded(blocks)

        def copy_in(i, h):
            return pltpu.make_async_copy(sources[i].at[h], filled_ref.at[i, h], sems.at[i, h])

        @pl.loop(early, blocks)
        def _(h):
            copy_in(0, h).start()
            copy_in(1, h).start()

        @pl.loop(0, blocks)
        def _(h):
            copy_in(2, h).start()
    else:
        filled_ref = held_ref
    normed, hidden, total = rest

    @pl.when(active)
    def _():
        squares = jnp.zeros((rows, block), f32)
        if first:
            starts = row_starts(lengths_ref, micro_count)
            group = micro_count * own_count
            place = lax.broadcasted_iota(jnp.int32, (rows, group), 0)
            local = lax.broadcasted_iota(jnp.int32, (rows, group), 1)
            picks = []
            for j in range(shard_total):
                device = shard_id ^ j
                target = jnp.full((rows, group), -1, jnp.int32)
                for m in range(micro_count):
                    for q in range(own_count):
                        row = device * own_count + q
                        to = jnp.where(row < lengths_ref[m], starts[m] + row, -1)
                        target = jnp.where(local == m * own_count + q, to, target)
                picks.append((target == place).astype(f32))
            pick = jnp.concatenate(picks, axis=1).astype(bf16)
            for c in range(shard_total):
                columns = pl.ds(c * chunk_blocks * block, chunk_blocks * block)
                spans = jnp.concatenate([ref[:, columns].astype(f32) for ref in chunks], axis=0)
                raw = jnp.dot(pick, spans.astype(bf16), preferred_element_type=f32)
                for i in range(chunk_blocks):
                    piece = raw[:, i * block : (i + 1) * block]
                    squares += piece * piece
                    normed[c * chunk_blocks + i] = piece.astype(bf16)
            for i in range(chunk_blocks):
                own_ref[:, i * block : (i + 1) * block] = normed[shard_id * chunk_blocks + i]
        else:
            for j in range(shard_total):
                base = (shard_id ^ j) * chunk_blocks
                for i in range(chunk_blocks):
                    piece = chunks[j][:, i * block : (i + 1) * block]
                    normed[base + i] = piece
                    wide = piece.astype(f32)
                    squares += wide * wide
        mean = jnp.sum(squares, axis=1, keepdims=True) / (block_total * block)
        scale = lax.rsqrt(mean + norm_eps)
        for b in range(block_total):
            normed[b] = (normed[b].astype(f32) * scale * gain_ref[b : b + 1, :]).astype(bf16)
        normed[block_total] = jnp.zeros((rows, block), bf16)
        total[...] = jnp.zeros_like(total)

        def at(ref, h, k):
            index = ref[h, k]
            return jnp.where(index < 0, block_total, index)

        @pl.loop(0, blocks // unroll)
        def _(step):
            if first:

                @pl.when(step * unroll >= early)
                def _():
                    for q in range(unroll):
                        copy_in(0, step * unroll + q).wait()
                        copy_in(1, step * unroll + q).wait()

            for q in range(unroll):
                h = step * unroll + q
                picked = jnp.concatenate([normed[at(in_ref, h, k)] for k in range(slots)], axis=1)
                gate = jnp.dot(
                    picked, filled_ref[0, h].reshape(slots * block, block), preferred_element_type=f32
                )
                up = jnp.dot(
                    picked, filled_ref[1, h].reshape(slots * block, block), preferred_element_type=f32
                )
                hidden[h] = (gate / (1.0 + jnp.exp(-gate)) * up).astype(bf16)

        @pl.loop(0, blocks // unroll)
        def _(step):
            if first:
                for q in range(unroll):
                    copy_in(2, step * unroll + q).wait()
            for q in range(unroll):
                h = step * unroll + q
                rows_in = hidden[h]
                for k in range(0, slots, 2):
                    pair = jnp.concatenate([filled_ref[2, h, k], filled_ref[2, h, k + 1]], axis=1)
                    product = jnp.dot(rows_in, pair, preferred_element_type=f32)
                    for p in range(2):
                        total[at(out_ref, h, k + p)] += product[:, p * block : (p + 1) * block]

        if not first:
            pick = own_rows(shard_id, lengths_ref, rows, micro_count, own_count).astype(bf16)
            for j in range(shard_total):
                width = chunk_blocks * block
                columns = pl.ds(pl.multiple_of((shard_id ^ j) * width, width), width)
                value = jnp.dot(pick, chunks[j][...], preferred_element_type=f32)
                back_ref[:, columns] = value.astype(bf16)
        if last:
            group = micro_count * own_count
            picks = [
                own_rows(shard_id ^ j, lengths_ref, rows, micro_count, own_count)
                for j in (*range(0, shard_total, 2), *range(1, shard_total, 2))
            ]
            pick = jnp.concatenate(picks, axis=0).astype(bf16)
            span = chunk_blocks
            for b in range(0, block_total, span):
                part = jnp.concatenate([total[b + i].astype(bf16) for i in range(span)], axis=1)
                value = jnp.dot(pick, part, preferred_element_type=f32)
                columns = slice(b * block, (b + span) * block)
                for j in range(shard_total):
                    target = even_ref if j < shard_total // 2 else odd_ref
                    piece = value[j * group : (j + 1) * group]
                    target[j % (shard_total // 2), :, columns] = piece.astype(bf16)
        else:
            for j in range(shard_total):
                base = (shard_id ^ j) * chunk_blocks
                target = (odd_ref if j % 2 else even_ref).at[j // 2]
                for i in range(chunk_blocks):
                    target[:, i * block : (i + 1) * block] = total[base + i].astype(bf16)

    if not first:

        @pl.when(jnp.logical_not(active))
        def _():
            back_ref[...] = back_in_ref[...]

    if first:

        @pl.when(jnp.logical_not(active))
        def _():
            @pl.loop(early, blocks)
            def _(h):
                copy_in(0, h).wait()
                copy_in(1, h).wait()

            @pl.loop(0, blocks)
            def _(h):
                copy_in(2, h).wait()


def layer_step(turn, last, rows, lengths, in_index, out_index, gain, held, tiles, chunks, back, micro_count, own_count):
    first = turn == 0
    shard_total = len(chunks)
    _, blocks, slots, block, _ = held.shape
    block_total = gain.shape[0]
    width = block_total * block // shard_total
    unroll = max(u for u in (1, 2, 4) if blocks % u == 0 and preloaded(blocks) % u == 0)
    group = micro_count * own_count
    part = (group, block_total * block) if last else (rows, width)
    outs = [pltpu.VMEM((shard_total // 2,) + part, bf16)] * 2
    if not first:
        outs.append(pltpu.VMEM(back.shape, bf16))
    if first:
        outs.append(pltpu.VMEM((rows, width), bf16))
        outs.append(pltpu.VMEM(held.shape, bf16))
    return pl.pallas_call(
        functools.partial(layer_kernel, turn, last, rows, unroll, shard_total, micro_count, own_count),
        out_shape=outs,
        in_specs=[SMEM_SPEC] * 3
        + [VMEM_SPEC] * 2
        + [ANY_SPEC] * (3 * first)
        + [VMEM_SPEC] * (shard_total + (not first)),
        out_specs=[VMEM_SPEC] * len(outs),
        scratch_shapes=[
            pltpu.VMEM((block_total + 1, rows, block), bf16),
            pltpu.VMEM((blocks, rows, block), bf16),
            pltpu.VMEM((block_total + 1, rows, block), f32),
        ]
        + ([pltpu.SemaphoreType.DMA((3, blocks))] if first else []),
        compiler_params=pltpu.CompilerParams(vmem_limit_bytes=vmem_limit(rows)),
        cost_estimate=pl.CostEstimate(
            flops=2 * rows * held.size, bytes_accessed=0, transcendentals=0
        ),
        input_output_aliases={4: 3} if first else {},
        name=f"layer_{turn}",
    )(lengths, in_index, out_index, gain, held, *(tiles if first else ()), *map(in_vmem, chunks), *(() if first else (in_vmem(back),)))


def pair_kernel(held_ref, even_ref, came_ref, own_ref, *send_refs):
    own_ref[...] = even_ref[0].astype(f32) + came_ref[0].astype(f32)
    for i, ref in enumerate(send_refs):
        ref[...] = (even_ref[i + 1].astype(f32) + came_ref[i + 1].astype(f32)).astype(bf16)


def pair_sum(held, even, came):
    parts, rows, width = even.shape
    return pl.pallas_call(
        pair_kernel,
        out_shape=[pltpu.VMEM((rows, width), f32)] + [pltpu.VMEM((rows, width), bf16)] * (parts - 1),
        in_specs=[VMEM_SPEC] * 3,
        out_specs=[VMEM_SPEC] * parts,
        compiler_params=pltpu.CompilerParams(vmem_limit_bytes=vmem_limit(rows)),
        name="pair_sum",
    )(held, in_vmem(even), in_vmem(came))


def finish_kernel(held_ref, x_ref, own_ref, *refs):
    sum_value = own_ref[...]
    for ref in refs[:-1]:
        sum_value = sum_value + ref[...].astype(f32)
    refs[-1][...] = (x_ref[...].astype(f32) + sum_value).astype(bf16)


def finish_sum(held, x_own, own, came):
    rows, width = x_own.shape
    return pl.pallas_call(
        finish_kernel,
        out_shape=pltpu.VMEM((rows, width), bf16),
        in_specs=[VMEM_SPEC] * (3 + len(came)),
        out_specs=VMEM_SPEC,
        compiler_params=pltpu.CompilerParams(vmem_limit_bytes=vmem_limit(rows)),
        name="finish_sum",
    )(held, *map(in_vmem, (x_own, own, *came)))


def result_kernel(last_turn, later_ref, x_ref, own_ref, *refs):
    out_ref = refs[-1]
    micro_count, own_count, _ = out_ref.shape
    sum_value = own_ref[...]
    for ref in refs[:-1]:
        sum_value = sum_value + ref[...].astype(f32)
    fresh = x_ref[...].astype(f32) + sum_value
    mine = lax.axis_index("section") == last_turn
    value = jnp.where(mine, fresh, later_ref[...].astype(f32))
    for m in range(micro_count):
        out_ref[m] = value[m * own_count : (m + 1) * own_count].astype(bf16)


def result_rows(last_turn, later, x_own, own, came, shape):
    return pl.pallas_call(
        functools.partial(result_kernel, last_turn),
        out_shape=jax.ShapeDtypeStruct(shape, bf16),
        in_specs=[VMEM_SPEC] * (3 + len(came)),
        out_specs=VMEM_SPEC,
        compiler_params=pltpu.CompilerParams(vmem_limit_bytes=vmem_limit(x_own.shape[0])),
        name="result_rows",
    )(*map(in_vmem, (later, x_own, own, *came)))


def body(tokens, lengths, norm_gain, gate_tiles, up_tiles, in_index, down_tiles, out_index):
    micro_count, own_count, model_width = tokens.shape
    block = gate_tiles.shape[-1]
    section_total = lax.axis_size("section")
    shard_total = lax.axis_size("shard")
    rows = live_total(tokens.shape, shard_total)
    gain = in_vmem(norm_gain.reshape(model_width // block, block))
    in_index, out_index, lengths = [
        pltpu.with_memory_space_constraint(value, pltpu.SMEM) for value in (in_index[0], out_index[0], lengths)
    ]
    tiles = (gate_tiles[0], up_tiles[0], down_tiles[0])
    held = in_vmem(load_weights(*tiles[:2], rows))
    own_tokens = tokens.reshape(micro_count * own_count, model_width)
    came = same_core(own_tokens)[1:]
    chunks = both_cores([own_tokens, *relay(held, came, rows)])
    back = own_tokens
    for turn in range(section_total):
        first, last = turn == 0, turn + 1 == section_total
        parts = layer_step(
            turn, last, rows, lengths, in_index, out_index, gain, held, tiles, chunks, back, micro_count, own_count
        )
        if first:
            x_own, held = parts[2], in_vmem(parts[3])
        else:
            x_own, back = chunks[0], parts[2]
        sums = pair_sum(held, parts[0], xor_shard(parts[1], 1))
        came = [xor_shard(part, 2 * i + 2) for i, part in enumerate(sums[1:])]
        if not last:
            fresh = finish_sum(held, x_own, sums[0], came)
            chunks = both_cores(next_section(fresh, turn))
    later = lax.ppermute(back, "section", [(i + 1, i) for i in range(section_total - 1)])
    return result_rows(section_total - 1, later, back, sums[0], came, tokens.shape)[None]


def solution(mesh):
    placed = (
        P(None, "shard", None),
        P(),
        P("section", None),
        P("section", "shard", None, None, None),
        P("section", "shard", None, None, None),
        P("section", "shard", None),
        P("section", "shard", None, None, None),
        P("section", "shard", None),
    )
    return jax.shard_map(
        body,
        mesh=mesh,
        in_specs=placed,
        out_specs=P("section", None, "shard", None),
        check_vma=False,
    )
```

time: 145 us -> 128 us (0.88)
  Pallas kernels: 58.5 us -> 30.3 us
  waiting for transfers between devices: 47 us -> 62 us
  starting transfers between devices: 36.7 us -> 34.4 us
    pallas_call x10 -> x9, Pallas kernels: 58.2 us -> 29.9 us  [the longest x4 23.7 us: layer_step(): pl.pallas_call(functools.partial(layer_kernel, turn, last, rows, unroll,...]
    ppermute x12, waiting for transfers between devices: 16.3 us -> 35.2 us  [next_section(): lax.ppermute(value, ('section', 'shard'), [(start + i, start + size + (i...]
    ppermute x42 -> x35, waiting for transfers between devices: 30.7 us -> 26.8 us  [xor_shard(): return lax.ppermute(value, 'shard', [(i, i ^ mask) for i in range(size)])]
    ppermute x42 -> x35, starting transfers between devices: 26 us -> 22.4 us  [xor_shard(): return lax.ppermute(value, 'shard', [(i, i ^ mask) for i in range(size)])]
  transfers between devices with their start and end apart: 54 -> 48, of which waited for: 38 -> 34; matrix products, arithmetic and copies ran while one was open for 0% -> 0% of each run, Pallas kernels for 7% -> 4%
where the time goes in v3:
time: 128 us
  waiting for transfers between devices  62 us (48%)
  starting transfers between devices  34.4 us (27%)
  Pallas kernels  30.3 us (24%)
    ppermute x12, waiting for transfers between devices, next_section(): lax.ppermute(value, ('section', 'shard'), [(start + i, start + size + (i...  35.2 us
    ppermute x35, waiting for transfers between devices, xor_shard(): return lax.ppermute(value, 'shard', [(i, i ^ mask) for i in range(size)])  26.8 us
    pallas_call x4, Pallas kernels, layer_step(): pl.pallas_call(functools.partial(layer_kernel, turn, last, rows, unroll,...  23.7 us
    ppermute x35, starting transfers between devices, xor_shard(): return lax.ppermute(value, 'shard', [(i, i ^ mask) for i in range(size)])  22.4 us
    ppermute x12, starting transfers between devices, next_section(): lax.ppermute(value, ('section', 'shard'), [(start + i, start + size + (i...  10.7 us
    pallas_call x1, Pallas kernels, load_weights(): pl.pallas_call(load_kernel, out_shape=pltpu.VMEM((3,) + gate.shape, bf16)...  5.33 us
  transfers between devices with their start and end apart: 48, of which 34 were waited for; matrix products, arithmetic and copies ran while one was open for 0% of the time, Pallas kernels for 4%

profile of v3, /device:TPU:24, one launch (start us, length us, event | category | flops | bytes accessed | tf_op | source)
XLA Modules:
  0.0 127.9 jit_solution(12552285711505926227)
XLA Ops:
  1.0 2.5 %collective-permute-start.3 = (bf16[8,8192]{1,0:T(8,128)(2,1)S(1)}, bf16[8,8192]{1,0:T(8,128)(2,1)S(1)}, u32[]{:S(2)}, u32[]{:S(2)}) collective-permute-start(bf16[8,8192]{1,0:T(8,128)(2,1)S(1)} %reshape.7.refs_8_.refs_13_), channel_id=1, source_target_pairs={{0,6},{1,7},{2,4},{3,5},{4,2},{5,3},{6,0},{7,1},{8,14},{9,15},{10,... | collective-permute-start | bytes 393224 | tf_op jit(solution)/shard_map/ppermute | solution.py:26
  4.5 5.3 %load_weights.1.held_ref.refs_4_ = bf16[3,16,28,128,128]{4,3,2,1,0:T(8,128)(2,1)S(1)} custom-call(bf16[16,28,128,128]{3,2,1,0:T(8,128)(2,1)} %bitcast.11, bf16[16,28,128,128]{3,2,1,0:T(8,128)(2,1)} %bitcast.13), custom_call_target="tpu_custom_call" | custom-call | bytes 29360128 | tf_op jit(solution)/shard_map/load_weights/pallas_call | solution.py:86
  12.0 11.1 %layer_0.1 = (bf16[4,40,1024]{2,1,0:T(8,128)(2,1)S(1)}, bf16[4,40,1024]{2,1,0:T(8,128)(2,1)S(1)}, bf16[40,1024]{1,0:T(8,128)(2,1)S(1)}, bf16[3,16,28,128,128]{4,3,2,1,0:T(8,128)(2,1)S(1)}) custom-call(s32[4]{0:T(128)} %refs_0_.7, s32[16,28]{1,0:T(8,128)} %bitcast.16, s32[16,28]{1,0:T(8,128)} %bitcast.20, ...), custom_call_target="tpu_custom_call", output_to_operand_aliasing={{3}: (4, {})} | custom-call | flops 1761607680 | tf_op jit(solution)/shard_map/layer_0/pallas_call | solution.py:323
  23.5 1.3 %collective-permute-done.7.came_ref = bf16[4,40,1024]{2,1,0:T(8,128)(2,1)S(1)} collective-permute-done((bf16[4,40,1024]{2,1,0:T(8,128)(2,1)S(1)}, bf16[4,40,1024]{2,1,0:T(8,128)(2,1)S(1)}, u32[]{:S(2)}, u32[]{:S(2)}) %collective-permute-start.7) | collective-permute-done | bytes 327712 | tf_op jit(solution)/shard_map/ppermute | solution.py:26
  24.9 1.6 %collective-permute-start.8 = (bf16[40,1024]{1,0:T(8,128)(2,1)S(1)}, bf16[40,1024]{1,0:T(8,128)(2,1)S(1)}, u32[]{:S(2)}, u32[]{:S(2)}) collective-permute-start(bf16[40,1024]{1,0:T(8,128)(2,1)S(1)} %get-tuple-element.45), channel_id=1, source_target_pairs={{0,2},{1,3},{2,0},{3,1},{4,6},{5,7},{6,4},{7,5},{8,10},{9,11},{10,... | collective-permute-start | bytes 245768 | tf_op jit(solution)/shard_map/ppermute | solution.py:26
  26.5 1.5 %collective-permute-start.9 = (bf16[40,1024]{1,0:T(8,128)(2,1)S(1)}, bf16[40,1024]{1,0:T(8,128)(2,1)S(1)}, u32[]{:S(2)}, u32[]{:S(2)}) collective-permute-start(bf16[40,1024]{1,0:T(8,128)(2,1)S(1)} %get-tuple-element.46), channel_id=1, source_target_pairs={{0,4},{1,5},{2,6},{3,7},{4,0},{5,1},{6,2},{7,3},{8,12},{9,13},{10,... | collective-permute-start | bytes 245768 | tf_op jit(solution)/shard_map/ppermute | solution.py:26
  28.5 1.2 collective-permute-done.8.refs_0_
  29.7 2.1 %collective-permute-done.9.refs_1_ = bf16[40,1024]{1,0:T(8,128)(2,1)S(1)} collective-permute-done((bf16[40,1024]{1,0:T(8,128)(2,1)S(1)}, bf16[40,1024]{1,0:T(8,128)(2,1)S(1)}, u32[]{:S(2)}, u32[]{:S(2)}) %collective-permute-start.9) | collective-permute-done | bytes 81952 | tf_op jit(solution)/shard_map/ppermute | solution.py:26
  31.7 1.6 %collective-permute-done.10.refs_2_ = bf16[40,1024]{1,0:T(8,128)(2,1)S(1)} collective-permute-done((bf16[40,1024]{1,0:T(8,128)(2,1)S(1)}, bf16[40,1024]{1,0:T(8,128)(2,1)S(1)}, u32[]{:S(2)}, u32[]{:S(2)}) %collective-permute-start.10) | collective-permute-done | bytes 81952 | tf_op jit(solution)/shard_map/ppermute | solution.py:26
  39.5 1.3 collective-permute-done.19.came_ref
  42.3 2.1 %collective-permute-start.22 = (bf16[40,1024]{1,0:T(8,128)(2,1)S(1)}, bf16[40,1024]{1,0:T(8,128)(2,1)S(1)}, u32[]{:S(2)}, u32[]{:S(2)}) collective-permute-start(bf16[40,1024]{1,0:T(8,128)(2,1)S(1)} %get-tuple-element.53), channel_id=1, source_target_pairs={{0,6},{1,7},{2,4},{3,5},{4,2},{5,3},{6,0},{7,1},{8,14},{9,15},{10,... | collective-permute-start | bytes 245768 | tf_op jit(solution)/shard_map/ppermute | solution.py:26
  44.4 1.6 %collective-permute-done.20.refs_0_ = bf16[40,1024]{1,0:T(8,128)(2,1)S(1)} collective-permute-done((bf16[40,1024]{1,0:T(8,128)(2,1)S(1)}, bf16[40,1024]{1,0:T(8,128)(2,1)S(1)}, u32[]{:S(2)}, u32[]{:S(2)}) %collective-permute-start.20) | collective-permute-done | bytes 81952 | tf_op jit(solution)/shard_map/ppermute | solution.py:26
  46.2 1.5 %collective-permute-done.22.refs_2_ = bf16[40,1024]{1,0:T(8,128)(2,1)S(1)} collective-permute-done((bf16[40,1024]{1,0:T(8,128)(2,1)S(1)}, bf16[40,1024]{1,0:T(8,128)(2,1)S(1)}, u32[]{:S(2)}, u32[]{:S(2)}) %collective-permute-start.22) | collective-permute-done | bytes 81952 | tf_op jit(solution)/shard_map/ppermute | solution.py:26
  53.9 1.3 collective-permute-done.31.came_ref
  55.2 1.5 %collective-permute-start.32 = (bf16[40,1024]{1,0:T(8,128)(2,1)S(1)}, bf16[40,1024]{1,0:T(8,128)(2,1)S(1)}, u32[]{:S(2)}, u32[]{:S(2)}) collective-permute-start(bf16[40,1024]{1,0:T(8,128)(2,1)S(1)} %get-tuple-element.58), channel_id=1, source_target_pairs={{0,2},{1,3},{2,0},{3,1},{4,6},{5,7},{6,4},{7,5},{8,10},{9,11},{10,... | collective-permute-start | bytes 245768 | tf_op jit(solution)/shard_map/ppermute | solution.py:26
  56.7 1.2 collective-permute-start.33
  58.8 1.2 collective-permute-done.32.refs_0_
  60.0 1.2 collective-permute-done.33.refs_1_
  61.2 2.1 %collective-permute-done.34.refs_2_ = bf16[40,1024]{1,0:T(8,128)(2,1)S(1)} collective-permute-done((bf16[40,1024]{1,0:T(8,128)(2,1)S(1)}, bf16[40,1024]{1,0:T(8,128)(2,1)S(1)}, u32[]{:S(2)}, u32[]{:S(2)}) %collective-permute-start.34) | collective-permute-done | bytes 81952 | tf_op jit(solution)/shard_map/ppermute | solution.py:26
  63.3 1.3 %collective-permute-start.41 = (bf16[40,1024]{1,0:T(8,128)(2,1)S(1)}, bf16[40,1024]{1,0:T(8,128)(2,1)S(1)}, u32[]{:S(2)}, u32[]{:S(2)}) collective-permute-start(bf16[40,1024]{1,0:T(8,128)(2,1)S(1)} %finish_sum.5), channel_id=1, source_target_pairs={{16,30},{17,31},{18,28},{19,29},{20,26},{21,27},{22,24},{23,25}} | collective-permute-start | bytes 245768 | tf_op jit(solution)/shard_map/ppermute | solution.py:38
  64.6 1.3 %collective-permute-start.39 = (bf16[40,1024]{1,0:T(8,128)(2,1)S(1)}, bf16[40,1024]{1,0:T(8,128)(2,1)S(1)}, u32[]{:S(2)}, u32[]{:S(2)}) collective-permute-start(bf16[40,1024]{1,0:T(8,128)(2,1)S(1)} %finish_sum.5), channel_id=1, source_target_pairs={{16,28},{17,29},{18,30},{19,31},{20,24},{21,25},{22,26},{23,27}} | collective-permute-start | bytes 245768 | tf_op jit(solution)/shard_map/ppermute | solution.py:38
  65.9 1.3 %collective-permute-start.37 = (bf16[40,1024]{1,0:T(8,128)(2,1)S(1)}, bf16[40,1024]{1,0:T(8,128)(2,1)S(1)}, u32[]{:S(2)}, u32[]{:S(2)}) collective-permute-start(bf16[40,1024]{1,0:T(8,128)(2,1)S(1)} %finish_sum.5), channel_id=1, source_target_pairs={{16,26},{17,27},{18,24},{19,25},{20,30},{21,31},{22,28},{23,29}} | collective-permute-start | bytes 245768 | tf_op jit(solution)/shard_map/ppermute | solution.py:38
  67.2 1.5 %collective-permute-start.35 = (bf16[40,1024]{1,0:T(8,128)(2,1)S(1)}, bf16[40,1024]{1,0:T(8,128)(2,1)S(1)}, u32[]{:S(2)}, u32[]{:S(2)}) collective-permute-start(bf16[40,1024]{1,0:T(8,128)(2,1)S(1)} %finish_sum.5), channel_id=1, source_target_pairs={{16,24},{17,25},{18,26},{19,27},{20,28},{21,29},{22,30},{23,31}} | collective-permute-start | bytes 245768 | tf_op jit(solution)/shard_map/ppermute | solution.py:38
  68.7 32.4 %collective-permute-done.41.refs_11_ = bf16[40,1024]{1,0:T(8,128)(2,1)S(1)} collective-permute-done((bf16[40,1024]{1,0:T(8,128)(2,1)S(1)}, bf16[40,1024]{1,0:T(8,128)(2,1)S(1)}, u32[]{:S(2)}, u32[]{:S(2)}) %collective-permute-start.41) | collective-permute-done | bytes 81952 | tf_op jit(solution)/shard_map/ppermute | solution.py:38
  101.1 1.3 collective-permute-done.39.refs_9_
  102.3 1.1 collective-permute-done.37.refs_7_
  105.2 10.6 %layer_3.1 = (bf16[4,8,8192]{2,1,0:T(8,128)(2,1)S(1)}, bf16[4,8,8192]{2,1,0:T(8,128)(2,1)S(1)}, bf16[8,8192]{1,0:T(8,128)(2,1)S(1)}) custom-call(s32[4]{0:T(128)} %refs_0_.7, s32[16,28]{1,0:T(8,128)} %bitcast.19, s32[16,28]{1,0:T(8,128)} %bitcast.23, f32[64,128]{1,0:T(8,128)S(1)} %bitcast.10, ...), custom_call_target="tpu_custom_call" | custom-call | flops 1761607680 | tf_op jit(solution)/shard_map/layer_3/pallas_call | solution.py:323
  116.1 1.3 %collective-permute-start.43 = (bf16[8,8192]{1,0:T(8,128)(2,1)S(1)}, bf16[8,8192]{1,0:T(8,128)(2,1)S(1)}, u32[]{:S(2)}, u32[]{:S(2)}) collective-permute-start(bf16[8,8192]{1,0:T(8,128)(2,1)S(1)} %get-tuple-element.62.x_ref), channel_id=1, source_target_pairs={{8,0},{16,8},{24,16},{9,1},{17,9},{25,17},{10,2},{18,10},{26,18},{... | collective-permute-start | bytes 393224 | tf_op jit(solution)/shard_map/ppermute | solution.py:437
  119.0 1.2 collective-permute-start.46
  120.2 1.3 %collective-permute-start.47 = (bf16[8,8192]{1,0:T(8,128)(2,1)S(1)}, bf16[8,8192]{1,0:T(8,128)(2,1)S(1)}, u32[]{:S(2)}, u32[]{:S(2)}) collective-permute-start(bf16[8,8192]{1,0:T(8,128)(2,1)S(1)} %get-tuple-element.68), channel_id=1, source_target_pairs={{0,6},{1,7},{2,4},{3,5},{4,2},{5,3},{6,0},{7,1},{8,14},{9,15},{10,... | collective-permute-start | bytes 393224 | tf_op jit(solution)/shard_map/ppermute | solution.py:26
  121.5 2.8 %collective-permute-done.45.refs_0_ = bf16[8,8192]{1,0:T(8,128)(2,1)S(1)} collective-permute-done((bf16[8,8192]{1,0:T(8,128)(2,1)S(1)}, bf16[8,8192]{1,0:T(8,128)(2,1)S(1)}, u32[]{:S(2)}, u32[]{:S(2)}) %collective-permute-start.45) | collective-permute-done | bytes 131104 | tf_op jit(solution)/shard_map/ppermute | solution.py:26
  124.3 2.8 %collective-permute-done.46.refs_1_ = bf16[8,8192]{1,0:T(8,128)(2,1)S(1)} collective-permute-done((bf16[8,8192]{1,0:T(8,128)(2,1)S(1)}, bf16[8,8192]{1,0:T(8,128)(2,1)S(1)}, u32[]{:S(2)}, u32[]{:S(2)}) %collective-permute-start.46) | collective-permute-done | bytes 131104 | tf_op jit(solution)/shard_map/ppermute | solution.py:26
  (81 shorter events, 24.5 us)
Async XLA Ops:
  1.0 8.9 %collective-permute-start.3 = (bf16[8,8192]{1,0:T(8,128)(2,1)S(1)}, bf16[8,8192]{1,0:T(8,128)(2,1)S(1)}, u32[]{:S(2)}, u32[]{:S(2)}) collective-permute-start(bf16[8,8192]{1,0:T(8,128)(2,1)S(1)} %reshape.7.refs_8_.refs_13_), channel_id=1, source_target_pairs={{0,6},{1,7},{2,4},{3,5},{4,2},{5,3},{6,0},{7,1},{8,14},{9,15},{10,... | collective-permute-start | bytes 393224 | tf_op jit(solution)/shard_map/ppermute | solution.py:26
  3.5 6.5 %collective-permute-start.2 = (bf16[8,8192]{1,0:T(8,128)(2,1)S(1)}, bf16[8,8192]{1,0:T(8,128)(2,1)S(1)}, u32[]{:S(2)}, u32[]{:S(2)}) collective-permute-start(bf16[8,8192]{1,0:T(8,128)(2,1)S(1)} %reshape.7.refs_8_.refs_13_), channel_id=1, source_target_pairs={{0,4},{1,5},{2,6},{3,7},{4,0},{5,1},{6,2},{7,3},{8,12},{9,13},{10,... | collective-permute-start | bytes 393224 | tf_op jit(solution)/shard_map/ppermute | solution.py:26
  4.0 6.0 %collective-permute-start.1 = (bf16[8,8192]{1,0:T(8,128)(2,1)S(1)}, bf16[8,8192]{1,0:T(8,128)(2,1)S(1)}, u32[]{:S(2)}, u32[]{:S(2)}) collective-permute-start(bf16[8,8192]{1,0:T(8,128)(2,1)S(1)} %reshape.7.refs_8_.refs_13_), channel_id=1, source_target_pairs={{0,2},{1,3},{2,0},{3,1},{4,6},{5,7},{6,4},{7,5},{8,10},{9,11},{10,... | collective-permute-start | bytes 393224 | tf_op jit(solution)/shard_map/ppermute | solution.py:26
  4.5 6.5 %collective-permute-start = (bf16[8,8192]{1,0:T(8,128)(2,1)S(1)}, bf16[8,8192]{1,0:T(8,128)(2,1)S(1)}, u32[]{:S(2)}, u32[]{:S(2)}) collective-permute-start(bf16[8,8192]{1,0:T(8,128)(2,1)S(1)} %reshape.7.refs_8_.refs_13_), channel_id=1, source_target_pairs={{0,1},{1,0},{2,3},{3,2},{4,5},{5,4},{6,7},{7,6},{8,9},{9,8},{10,11... | collective-permute-start | bytes 393224 | tf_op jit(solution)/shard_map/ppermute | solution.py:26
  23.1 1.7 %collective-permute-start.7 = (bf16[4,40,1024]{2,1,0:T(8,128)(2,1)S(1)}, bf16[4,40,1024]{2,1,0:T(8,128)(2,1)S(1)}, u32[]{:S(2)}, u32[]{:S(2)}) collective-permute-start(bf16[4,40,1024]{2,1,0:T(8,128)(2,1)S(1)} %get-tuple-element.43), channel_id=1, source_target_pairs={{0,1},{1,0},{2,3},{3,2},{4,5},{5,4},{6,7},{7,6},{8,9},{9,8},{10,11... | collective-permute-start | bytes 983048 | tf_op jit(solution)/shard_map/ppermute | solution.py:26
  24.9 4.7 %collective-permute-start.8 = (bf16[40,1024]{1,0:T(8,128)(2,1)S(1)}, bf16[40,1024]{1,0:T(8,128)(2,1)S(1)}, u32[]{:S(2)}, u32[]{:S(2)}) collective-permute-start(bf16[40,1024]{1,0:T(8,128)(2,1)S(1)} %get-tuple-element.45), channel_id=1, source_target_pairs={{0,2},{1,3},{2,0},{3,1},{4,6},{5,7},{6,4},{7,5},{8,10},{9,11},{10,... | collective-permute-start | bytes 245768 | tf_op jit(solution)/shard_map/ppermute | solution.py:26
  26.5 5.3 %collective-permute-start.9 = (bf16[40,1024]{1,0:T(8,128)(2,1)S(1)}, bf16[40,1024]{1,0:T(8,128)(2,1)S(1)}, u32[]{:S(2)}, u32[]{:S(2)}) collective-permute-start(bf16[40,1024]{1,0:T(8,128)(2,1)S(1)} %get-tuple-element.46), channel_id=1, source_target_pairs={{0,4},{1,5},{2,6},{3,7},{4,0},{5,1},{6,2},{7,3},{8,12},{9,13},{10,... | collective-permute-start | bytes 245768 | tf_op jit(solution)/shard_map/ppermute | solution.py:26
  28.0 5.3 %collective-permute-start.10 = (bf16[40,1024]{1,0:T(8,128)(2,1)S(1)}, bf16[40,1024]{1,0:T(8,128)(2,1)S(1)}, u32[]{:S(2)}, u32[]{:S(2)}) collective-permute-start(bf16[40,1024]{1,0:T(8,128)(2,1)S(1)} %get-tuple-element.47), channel_id=1, source_target_pairs={{0,6},{1,7},{2,4},{3,5},{4,2},{5,3},{6,0},{7,1},{8,14},{9,15},{10,... | collective-permute-start | bytes 245768 | tf_op jit(solution)/shard_map/ppermute | solution.py:26
  33.4 2.7 %collective-permute-start.17 = (bf16[40,1024]{1,0:T(8,128)(2,1)S(1)}, bf16[40,1024]{1,0:T(8,128)(2,1)S(1)}, u32[]{:S(2)}, u32[]{:S(2)}) collective-permute-start(bf16[40,1024]{1,0:T(8,128)(2,1)S(1)} %finish_sum.3), channel_id=1, source_target_pairs={{0,14},{1,15},{2,12},{3,13},{4,10},{5,11},{6,8},{7,9}} | collective-permute-start | bytes 245768 | tf_op jit(solution)/shard_map/ppermute | solution.py:38
  34.1 2.1 %collective-permute-start.15 = (bf16[40,1024]{1,0:T(8,128)(2,1)S(1)}, bf16[40,1024]{1,0:T(8,128)(2,1)S(1)}, u32[]{:S(2)}, u32[]{:S(2)}) collective-permute-start(bf16[40,1024]{1,0:T(8,128)(2,1)S(1)} %finish_sum.3), channel_id=1, source_target_pairs={{0,12},{1,13},{2,14},{3,15},{4,8},{5,9},{6,10},{7,11}} | collective-permute-start | bytes 245768 | tf_op jit(solution)/shard_map/ppermute | solution.py:38
  34.7 1.9 %collective-permute-start.13 = (bf16[40,1024]{1,0:T(8,128)(2,1)S(1)}, bf16[40,1024]{1,0:T(8,128)(2,1)S(1)}, u32[]{:S(2)}, u32[]{:S(2)}) collective-permute-start(bf16[40,1024]{1,0:T(8,128)(2,1)S(1)} %finish_sum.3), channel_id=1, source_target_pairs={{0,10},{1,11},{2,8},{3,9},{4,14},{5,15},{6,12},{7,13}} | collective-permute-start | bytes 245768 | tf_op jit(solution)/shard_map/ppermute | solution.py:38
  39.1 1.7 %collective-permute-start.19 = (bf16[4,40,1024]{2,1,0:T(8,128)(2,1)S(1)}, bf16[4,40,1024]{2,1,0:T(8,128)(2,1)S(1)}, u32[]{:S(2)}, u32[]{:S(2)}) collective-permute-start(bf16[4,40,1024]{2,1,0:T(8,128)(2,1)S(1)} %get-tuple-element.49), channel_id=1, source_target_pairs={{0,1},{1,0},{2,3},{3,2},{4,5},{5,4},{6,7},{7,6},{8,9},{9,8},{10,11... | collective-permute-start | bytes 983048 | tf_op jit(solution)/shard_map/ppermute | solution.py:26
  40.9 5.1 %collective-permute-start.20 = (bf16[40,1024]{1,0:T(8,128)(2,1)S(1)}, bf16[40,1024]{1,0:T(8,128)(2,1)S(1)}, u32[]{:S(2)}, u32[]{:S(2)}) collective-permute-start(bf16[40,1024]{1,0:T(8,128)(2,1)S(1)} %get-tuple-element.51), channel_id=1, source_target_pairs={{0,2},{1,3},{2,0},{3,1},{4,6},{5,7},{6,4},{7,5},{8,10},{9,11},{10,... | collective-permute-start | bytes 245768 | tf_op jit(solution)/shard_map/ppermute | solution.py:26
  41.5 4.8 %collective-permute-start.21 = (bf16[40,1024]{1,0:T(8,128)(2,1)S(1)}, bf16[40,1024]{1,0:T(8,128)(2,1)S(1)}, u32[]{:S(2)}, u32[]{:S(2)}) collective-permute-start(bf16[40,1024]{1,0:T(8,128)(2,1)S(1)} %get-tuple-element.52), channel_id=1, source_target_pairs={{0,4},{1,5},{2,6},{3,7},{4,0},{5,1},{6,2},{7,3},{8,12},{9,13},{10,... | collective-permute-start | bytes 245768 | tf_op jit(solution)/shard_map/ppermute | solution.py:26
  42.3 5.4 %collective-permute-start.22 = (bf16[40,1024]{1,0:T(8,128)(2,1)S(1)}, bf16[40,1024]{1,0:T(8,128)(2,1)S(1)}, u32[]{:S(2)}, u32[]{:S(2)}) collective-permute-start(bf16[40,1024]{1,0:T(8,128)(2,1)S(1)} %get-tuple-element.53), channel_id=1, source_target_pairs={{0,6},{1,7},{2,4},{3,5},{4,2},{5,3},{6,0},{7,1},{8,14},{9,15},{10,... | collective-permute-start | bytes 245768 | tf_op jit(solution)/shard_map/ppermute | solution.py:26
  47.7 2.7 %collective-permute-start.29 = (bf16[40,1024]{1,0:T(8,128)(2,1)S(1)}, bf16[40,1024]{1,0:T(8,128)(2,1)S(1)}, u32[]{:S(2)}, u32[]{:S(2)}) collective-permute-start(bf16[40,1024]{1,0:T(8,128)(2,1)S(1)} %finish_sum.4), channel_id=1, source_target_pairs={{8,22},{9,23},{10,20},{11,21},{12,18},{13,19},{14,16},{15,17}} | collective-permute-start | bytes 245768 | tf_op jit(solution)/shard_map/ppermute | solution.py:38
  48.4 2.1 %collective-permute-start.27 = (bf16[40,1024]{1,0:T(8,128)(2,1)S(1)}, bf16[40,1024]{1,0:T(8,128)(2,1)S(1)}, u32[]{:S(2)}, u32[]{:S(2)}) collective-permute-start(bf16[40,1024]{1,0:T(8,128)(2,1)S(1)} %finish_sum.4), channel_id=1, source_target_pairs={{8,20},{9,21},{10,22},{11,23},{12,16},{13,17},{14,18},{15,19}} | collective-permute-start | bytes 245768 | tf_op jit(solution)/shard_map/ppermute | solution.py:38
  49.1 1.9 %collective-permute-start.25 = (bf16[40,1024]{1,0:T(8,128)(2,1)S(1)}, bf16[40,1024]{1,0:T(8,128)(2,1)S(1)}, u32[]{:S(2)}, u32[]{:S(2)}) collective-permute-start(bf16[40,1024]{1,0:T(8,128)(2,1)S(1)} %finish_sum.4), channel_id=1, source_target_pairs={{8,18},{9,19},{10,16},{11,17},{12,22},{13,23},{14,20},{15,21}} | collective-permute-start | bytes 245768 | tf_op jit(solution)/shard_map/ppermute | solution.py:38
  53.4 1.7 %collective-permute-start.31 = (bf16[4,40,1024]{2,1,0:T(8,128)(2,1)S(1)}, bf16[4,40,1024]{2,1,0:T(8,128)(2,1)S(1)}, u32[]{:S(2)}, u32[]{:S(2)}) collective-permute-start(bf16[4,40,1024]{2,1,0:T(8,128)(2,1)S(1)} %get-tuple-element.56), channel_id=1, source_target_pairs={{0,1},{1,0},{2,3},{3,2},{4,5},{5,4},{6,7},{7,6},{8,9},{9,8},{10,11... | collective-permute-start | bytes 983048 | tf_op jit(solution)/shard_map/ppermute | solution.py:26
  55.2 4.8 %collective-permute-start.32 = (bf16[40,1024]{1,0:T(8,128)(2,1)S(1)}, bf16[40,1024]{1,0:T(8,128)(2,1)S(1)}, u32[]{:S(2)}, u32[]{:S(2)}) collective-permute-start(bf16[40,1024]{1,0:T(8,128)(2,1)S(1)} %get-tuple-element.58), channel_id=1, source_target_pairs={{0,2},{1,3},{2,0},{3,1},{4,6},{5,7},{6,4},{7,5},{8,10},{9,11},{10,... | collective-permute-start | bytes 245768 | tf_op jit(solution)/shard_map/ppermute | solution.py:26
  56.7 4.4 %collective-permute-start.33 = (bf16[40,1024]{1,0:T(8,128)(2,1)S(1)}, bf16[40,1024]{1,0:T(8,128)(2,1)S(1)}, u32[]{:S(2)}, u32[]{:S(2)}) collective-permute-start(bf16[40,1024]{1,0:T(8,128)(2,1)S(1)} %get-tuple-element.59), channel_id=1, source_target_pairs={{0,4},{1,5},{2,6},{3,7},{4,0},{5,1},{6,2},{7,3},{8,12},{9,13},{10,... | collective-permute-start | bytes 245768 | tf_op jit(solution)/shard_map/ppermute | solution.py:26
  57.9 5.3 %collective-permute-start.34 = (bf16[40,1024]{1,0:T(8,128)(2,1)S(1)}, bf16[40,1024]{1,0:T(8,128)(2,1)S(1)}, u32[]{:S(2)}, u32[]{:S(2)}) collective-permute-start(bf16[40,1024]{1,0:T(8,128)(2,1)S(1)} %get-tuple-element.60), channel_id=1, source_target_pairs={{0,6},{1,7},{2,4},{3,5},{4,2},{5,3},{6,0},{7,1},{8,14},{9,15},{10,... | collective-permute-start | bytes 245768 | tf_op jit(solution)/shard_map/ppermute | solution.py:26
  63.3 37.8 %collective-permute-start.41 = (bf16[40,1024]{1,0:T(8,128)(2,1)S(1)}, bf16[40,1024]{1,0:T(8,128)(2,1)S(1)}, u32[]{:S(2)}, u32[]{:S(2)}) collective-permute-start(bf16[40,1024]{1,0:T(8,128)(2,1)S(1)} %finish_sum.5), channel_id=1, source_target_pairs={{16,30},{17,31},{18,28},{19,29},{20,26},{21,27},{22,24},{23,25}} | collective-permute-start | bytes 245768 | tf_op jit(solution)/shard_map/ppermute | solution.py:38
  64.6 37.7 %collective-permute-start.39 = (bf16[40,1024]{1,0:T(8,128)(2,1)S(1)}, bf16[40,1024]{1,0:T(8,128)(2,1)S(1)}, u32[]{:S(2)}, u32[]{:S(2)}) collective-permute-start(bf16[40,1024]{1,0:T(8,128)(2,1)S(1)} %finish_sum.5), channel_id=1, source_target_pairs={{16,28},{17,29},{18,30},{19,31},{20,24},{21,25},{22,26},{23,27}} | collective-permute-start | bytes 245768 | tf_op jit(solution)/shard_map/ppermute | solution.py:38
  65.9 37.5 %collective-permute-start.37 = (bf16[40,1024]{1,0:T(8,128)(2,1)S(1)}, bf16[40,1024]{1,0:T(8,128)(2,1)S(1)}, u32[]{:S(2)}, u32[]{:S(2)}) collective-permute-start(bf16[40,1024]{1,0:T(8,128)(2,1)S(1)} %finish_sum.5), channel_id=1, source_target_pairs={{16,26},{17,27},{18,24},{19,25},{20,30},{21,31},{22,28},{23,29}} | collective-permute-start | bytes 245768 | tf_op jit(solution)/shard_map/ppermute | solution.py:38
  67.2 36.7 %collective-permute-start.35 = (bf16[40,1024]{1,0:T(8,128)(2,1)S(1)}, bf16[40,1024]{1,0:T(8,128)(2,1)S(1)}, u32[]{:S(2)}, u32[]{:S(2)}) collective-permute-start(bf16[40,1024]{1,0:T(8,128)(2,1)S(1)} %finish_sum.5), channel_id=1, source_target_pairs={{16,24},{17,25},{18,26},{19,27},{20,28},{21,29},{22,30},{23,31}} | collective-permute-start | bytes 245768 | tf_op jit(solution)/shard_map/ppermute | solution.py:38
  101.1 2.9 %collective-permute-start.42 = (bf16[40,1024]{1,0:T(8,128)(2,1)S(1)}, bf16[40,1024]{1,0:T(8,128)(2,1)S(1)}, u32[]{:S(2)}, u32[]{:S(2)}) collective-permute-start(bf16[40,1024]{1,0:T(8,128)(2,1)S(1)} %collective-permute-done.41.refs_11_), channel_id=1, source_target_pairs={{0,1},{1,0},{2,3},{3,2},{4,5},{5,4},{6,7},{7,6},{8,9},{9,8},{10,11... | collective-permute-start | bytes 245768 | tf_op jit(solution)/shard_map/ppermute | solution.py:26
  115.8 2.0 %collective-permute-start.44 = (bf16[4,8,8192]{2,1,0:T(8,128)(2,1)S(1)}, bf16[4,8,8192]{2,1,0:T(8,128)(2,1)S(1)}, u32[]{:S(2)}, u32[]{:S(2)}) collective-permute-start(bf16[4,8,8192]{2,1,0:T(8,128)(2,1)S(1)} %get-tuple-element.64), channel_id=1, source_target_pairs={{0,1},{1,0},{2,3},{3,2},{4,5},{5,4},{6,7},{7,6},{8,9},{9,8},{10,11... | collective-permute-start | bytes 1572872 | tf_op jit(solution)/shard_map/ppermute | solution.py:26
  116.1 5.4 %collective-permute-start.43 = (bf16[8,8192]{1,0:T(8,128)(2,1)S(1)}, bf16[8,8192]{1,0:T(8,128)(2,1)S(1)}, u32[]{:S(2)}, u32[]{:S(2)}) collective-permute-start(bf16[8,8192]{1,0:T(8,128)(2,1)S(1)} %get-tuple-element.62.x_ref), channel_id=1, source_target_pairs={{8,0},{16,8},{24,16},{9,1},{17,9},{25,17},{10,2},{18,10},{26,18},{... | collective-permute-start | bytes 393224 | tf_op jit(solution)/shard_map/ppermute | solution.py:437
  117.9 6.4 %collective-permute-start.45 = (bf16[8,8192]{1,0:T(8,128)(2,1)S(1)}, bf16[8,8192]{1,0:T(8,128)(2,1)S(1)}, u32[]{:S(2)}, u32[]{:S(2)}) collective-permute-start(bf16[8,8192]{1,0:T(8,128)(2,1)S(1)} %get-tuple-element.66), channel_id=1, source_target_pairs={{0,2},{1,3},{2,0},{3,1},{4,6},{5,7},{6,4},{7,5},{8,10},{9,11},{10,... | collective-permute-start | bytes 393224 | tf_op jit(solution)/shard_map/ppermute | solution.py:26
  119.0 8.1 %collective-permute-start.46 = (bf16[8,8192]{1,0:T(8,128)(2,1)S(1)}, bf16[8,8192]{1,0:T(8,128)(2,1)S(1)}, u32[]{:S(2)}, u32[]{:S(2)}) collective-permute-start(bf16[8,8192]{1,0:T(8,128)(2,1)S(1)} %get-tuple-element.67), channel_id=1, source_target_pairs={{0,4},{1,5},{2,6},{3,7},{4,0},{5,1},{6,2},{7,3},{8,12},{9,13},{10,... | collective-permute-start | bytes 393224 | tf_op jit(solution)/shard_map/ppermute | solution.py:26
  120.2 6.9 %collective-permute-start.47 = (bf16[8,8192]{1,0:T(8,128)(2,1)S(1)}, bf16[8,8192]{1,0:T(8,128)(2,1)S(1)}, u32[]{:S(2)}, u32[]{:S(2)}) collective-permute-start(bf16[8,8192]{1,0:T(8,128)(2,1)S(1)} %get-tuple-element.68), channel_id=1, source_target_pairs={{0,6},{1,7},{2,4},{3,5},{4,2},{5,3},{6,0},{7,1},{8,14},{9,15},{10,... | collective-permute-start | bytes 393224 | tf_op jit(solution)/shard_map/ppermute | solution.py:26
  (17 other events, 24.0 us)

commit v4 on v3

--- a/solution.py
+++ b/solution.py
@@ -12,7 +12,6 @@
 bf16 = jnp.bfloat16
 MIB = 2**20
 VMEM_SPEC = pl.BlockSpec(memory_space=pltpu.VMEM)
-SMEM_SPEC = pl.BlockSpec(memory_space=pltpu.SMEM)
 ANY_SPEC = pl.BlockSpec(memory_space=pl.ANY)
 
 
@@ -139,7 +138,7 @@
 
 def layer_kernel(turn, last, rows, unroll, shard_total, micro_count, own_count, *refs):
     first = turn == 0
-    lengths_ref, in_ref, out_ref, gain_ref, held_ref = refs[:5]
+    scalars, (gain_ref, held_ref) = refs[:3], refs[3:5]
     rest = list(refs[5:])
     sources = [rest.pop(0) for _ in range(3)] if first else None
     shard_id = lax.axis_index("shard")
@@ -151,10 +150,16 @@
     back_in_ref = None if first else rest.pop(0)
     even_ref, odd_ref = rest.pop(0), rest.pop(0)
     back_ref = None if first else rest.pop(0)
+    own_ref, filled_ref = (rest.pop(0), rest.pop(0)) if first else (None, held_ref)
+    sems = rest.pop() if first else None
+    normed, hidden, total, lengths_ref, in_ref, out_ref, scalar_sems = rest
+    places = (lengths_ref, in_ref, out_ref)
+    lengths_copy, in_copy, out_copy = [
+        pltpu.make_async_copy(scalars[i], places[i], scalar_sems.at[i]) for i in range(3)
+    ]
+    for copy in (lengths_copy, in_copy, out_copy):
+        copy.start()
     if first:
-        own_ref, filled_ref = rest.pop(0), rest.pop(0)
-        sems = rest.pop()
-
         early = preloaded(blocks)
 
         def copy_in(i, h):
@@ -168,14 +173,12 @@
         @pl.loop(0, blocks)
         def _(h):
             copy_in(2, h).start()
-    else:
-        filled_ref = held_ref
-    normed, hidden, total = rest
 
     @pl.when(active)
     def _():
         squares = jnp.zeros((rows, block), f32)
         if first:
+            lengths_copy.wait()
             starts = row_starts(lengths_ref, micro_count)
             group = micro_count * own_count
             place = lax.broadcasted_iota(jnp.int32, (rows, group), 0)
@@ -220,6 +223,8 @@
             index = ref[h, k]
             return jnp.where(index < 0, block_total, index)
 
+        in_copy.wait()
+
         @pl.loop(0, blocks // unroll)
         def _(step):
             if first:
@@ -240,6 +245,8 @@
                     picked, filled_ref[1, h].reshape(slots * block, block), preferred_element_type=f32
                 )
                 hidden[h] = (gate / (1.0 + jnp.exp(-gate)) * up).astype(bf16)
+
+        out_copy.wait()
 
         @pl.loop(0, blocks // unroll)
         def _(step):
@@ -256,6 +263,7 @@
                         total[at(out_ref, h, k + p)] += product[:, p * block : (p + 1) * block]
 
         if not first:
+            lengths_copy.wait()
             pick = own_rows(shard_id, lengths_ref, rows, micro_count, own_count).astype(bf16)
             for j in range(shard_total):
                 width = chunk_blocks * block
@@ -285,16 +293,12 @@
                 for i in range(chunk_blocks):
                     target[:, i * block : (i + 1) * block] = total[base + i].astype(bf16)
 
-    if not first:
-
-        @pl.when(jnp.logical_not(active))
-        def _():
-            back_ref[...] = back_in_ref[...]
-
-    if first:
-
-        @pl.when(jnp.logical_not(active))
-        def _():
+    @pl.when(jnp.logical_not(active))
+    def _():
+        for copy in (lengths_copy, in_copy, out_copy):
+            copy.wait()
+        if first:
+
             @pl.loop(early, blocks)
             def _(h):
                 copy_in(0, h).wait()
@@ -303,6 +307,9 @@
             @pl.loop(0, blocks)
             def _(h):
                 copy_in(2, h).wait()
+
+        else:
+            back_ref[...] = back_in_ref[...]
 
 
 def layer_step(turn, last, rows, lengths, in_index, out_index, gain, held, tiles, chunks, back, micro_count, own_count):
@@ -311,7 +318,8 @@
     _, blocks, slots, block, _ = held.shape
     block_total = gain.shape[0]
     width = block_total * block // shard_total
-    unroll = max(u for u in (1, 2, 4) if blocks % u == 0 and preloaded(blocks) % u == 0)
+    whole = preloaded(blocks) if first else blocks
+    unroll = max(u for u in ((1, 2, 4) if first else (1, 2, 4, 8)) if blocks % u == 0 and whole % u == 0)
     group = micro_count * own_count
     part = (group, block_total * block) if last else (rows, width)
     outs = [pltpu.VMEM((shard_total // 2,) + part, bf16)] * 2
@@ -323,7 +331,7 @@
     return pl.pallas_call(
         functools.partial(layer_kernel, turn, last, rows, unroll, shard_total, micro_count, own_count),
         out_shape=outs,
-        in_specs=[SMEM_SPEC] * 3
+        in_specs=[ANY_SPEC] * 3
         + [VMEM_SPEC] * 2
         + [ANY_SPEC] * (3 * first)
         + [VMEM_SPEC] * (shard_total + (not first)),
@@ -332,6 +340,10 @@
             pltpu.VMEM((block_total + 1, rows, block), bf16),
             pltpu.VMEM((blocks, rows, block), bf16),
             pltpu.VMEM((block_total + 1, rows, block), f32),
+            pltpu.SMEM(lengths.shape, jnp.int32),
+            pltpu.SMEM(in_index.shape, jnp.int32),
+            pltpu.SMEM(out_index.shape, jnp.int32),
+            pltpu.SemaphoreType.DMA((3,)),
         ]
         + ([pltpu.SemaphoreType.DMA((3, blocks))] if first else []),
         compiler_params=pltpu.CompilerParams(vmem_limit_bytes=vmem_limit(rows)),
@@ -411,9 +423,7 @@
     shard_total = lax.axis_size("shard")
     rows = live_total(tokens.shape, shard_total)
     gain = in_vmem(norm_gain.reshape(model_width // block, block))
-    in_index, out_index, lengths = [
-        pltpu.with_memory_space_constraint(value, pltpu.SMEM) for value in (in_index[0], out_index[0], lengths)
-    ]
+    in_index, out_index = in_index[0], out_index[0]
     tiles = (gate_tiles[0], up_tiles[0], down_tiles[0])
     held = in_vmem(load_weights(*tiles[:2], rows))
     own_tokens = tokens.reshape(micro_count * own_count, model_width)

time: 128 us -> 124 us (0.969)
  Pallas kernels: 30.3 us -> 28.2 us
  waiting for transfers between devices: 62 us -> 59.9 us
    ppermute x12, waiting for transfers between devices: 35.2 us -> 33.1 us  [next_section(): lax.ppermute(value, ('section', 'shard'), [(start + i, start + size + (i...]
    pallas_call x4, Pallas kernels: 23.7 us -> 21.6 us  [layer_step(): pl.pallas_call(functools.partial(layer_kernel, turn, last, rows, unroll,...]
where the time goes in v4:
time: 124 us
  waiting for transfers between devices  59.9 us (48%)
  starting transfers between devices  34.3 us (28%)
  Pallas kernels  28.2 us (23%)
    ppermute x12, waiting for transfers between devices, next_section(): lax.ppermute(value, ('section', 'shard'), [(start + i, start + size + (i...  33.1 us
    ppermute x35, waiting for transfers between devices, xor_shard(): return lax.ppermute(value, 'shard', [(i, i ^ mask) for i in range(size)])  26.8 us
    ppermute x35, starting transfers between devices, xor_shard(): return lax.ppermute(value, 'shard', [(i, i ^ mask) for i in range(size)])  22.5 us
    pallas_call x4, Pallas kernels, layer_step(): pl.pallas_call(functools.partial(layer_kernel, turn, last, rows, unroll,...  21.6 us
    ppermute x12, starting transfers between devices, next_section(): lax.ppermute(value, ('section', 'shard'), [(start + i, start + size + (i...  10.5 us
    pallas_call x1, Pallas kernels, load_weights(): pl.pallas_call(load_kernel, out_shape=pltpu.VMEM((3,) + gate.shape, bf16)...  5.33 us
  transfers between devices with their start and end apart: 48, of which 34 were waited for; matrix products, arithmetic and copies ran while one was open for 0% of the time, Pallas kernels for 4%

profile of v4, /device:TPU:24, one launch (start us, length us, event | category | flops | bytes accessed | tf_op | source)
XLA Modules:
  0.0 123.6 jit_solution(10010729178961105957)
XLA Ops:
  1.0 2.5 %collective-permute-start.3 = (bf16[8,8192]{1,0:T(8,128)(2,1)S(1)}, bf16[8,8192]{1,0:T(8,128)(2,1)S(1)}, u32[]{:S(2)}, u32[]{:S(2)}) collective-permute-start(bf16[8,8192]{1,0:T(8,128)(2,1)S(1)} %reshape.7.refs_8_.refs_13_), channel_id=1, source_target_pairs={{0,6},{1,7},{2,4},{3,5},{4,2},{5,3},{6,0},{7,1},{8,14},{9,15},{10,... | collective-permute-start | bytes 393224 | tf_op jit(solution)/shard_map/ppermute | solution.py:25
  4.5 5.3 %load_weights.1.held_ref.refs_4_ = bf16[3,16,28,128,128]{4,3,2,1,0:T(8,128)(2,1)S(1)} custom-call(bf16[16,28,128,128]{3,2,1,0:T(8,128)(2,1)} %bitcast.11, bf16[16,28,128,128]{3,2,1,0:T(8,128)(2,1)} %bitcast.13), custom_call_target="tpu_custom_call" | custom-call | bytes 29360128 | tf_op jit(solution)/shard_map/load_weights/pallas_call | solution.py:85
  12.0 10.2 %layer_0.1 = (bf16[4,40,1024]{2,1,0:T(8,128)(2,1)S(1)}, bf16[4,40,1024]{2,1,0:T(8,128)(2,1)S(1)}, bf16[40,1024]{1,0:T(8,128)(2,1)S(1)}, bf16[3,16,28,128,128]{4,3,2,1,0:T(8,128)(2,1)S(1)}) custom-call(s32[4]{0:T(128)} %refs_0_.7, s32[16,28]{1,0:T(8,128)} %bitcast.16, s32[16,28]{1,0:T(8,128)} %bitcast.20, ...), custom_call_target="tpu_custom_call", output_to_operand_aliasing={{3}: (4, {})} | custom-call | flops 1761607680 | tf_op jit(solution)/shard_map/layer_0/pallas_call | solution.py:331
  22.6 1.3 %collective-permute-done.7.came_ref = bf16[4,40,1024]{2,1,0:T(8,128)(2,1)S(1)} collective-permute-done((bf16[4,40,1024]{2,1,0:T(8,128)(2,1)S(1)}, bf16[4,40,1024]{2,1,0:T(8,128)(2,1)S(1)}, u32[]{:S(2)}, u32[]{:S(2)}) %collective-permute-start.7) | collective-permute-done | bytes 327712 | tf_op jit(solution)/shard_map/ppermute | solution.py:25
  24.0 1.6 %collective-permute-start.8 = (bf16[40,1024]{1,0:T(8,128)(2,1)S(1)}, bf16[40,1024]{1,0:T(8,128)(2,1)S(1)}, u32[]{:S(2)}, u32[]{:S(2)}) collective-permute-start(bf16[40,1024]{1,0:T(8,128)(2,1)S(1)} %get-tuple-element.45), channel_id=1, source_target_pairs={{0,2},{1,3},{2,0},{3,1},{4,6},{5,7},{6,4},{7,5},{8,10},{9,11},{10,... | collective-permute-start | bytes 245768 | tf_op jit(solution)/shard_map/ppermute | solution.py:25
  25.6 1.5 %collective-permute-start.9 = (bf16[40,1024]{1,0:T(8,128)(2,1)S(1)}, bf16[40,1024]{1,0:T(8,128)(2,1)S(1)}, u32[]{:S(2)}, u32[]{:S(2)}) collective-permute-start(bf16[40,1024]{1,0:T(8,128)(2,1)S(1)} %get-tuple-element.46), channel_id=1, source_target_pairs={{0,4},{1,5},{2,6},{3,7},{4,0},{5,1},{6,2},{7,3},{8,12},{9,13},{10,... | collective-permute-start | bytes 245768 | tf_op jit(solution)/shard_map/ppermute | solution.py:25
  27.6 1.2 collective-permute-done.8.refs_0_
  28.7 2.1 %collective-permute-done.9.refs_1_ = bf16[40,1024]{1,0:T(8,128)(2,1)S(1)} collective-permute-done((bf16[40,1024]{1,0:T(8,128)(2,1)S(1)}, bf16[40,1024]{1,0:T(8,128)(2,1)S(1)}, u32[]{:S(2)}, u32[]{:S(2)}) %collective-permute-start.9) | collective-permute-done | bytes 81952 | tf_op jit(solution)/shard_map/ppermute | solution.py:25
  30.8 1.6 %collective-permute-done.10.refs_2_ = bf16[40,1024]{1,0:T(8,128)(2,1)S(1)} collective-permute-done((bf16[40,1024]{1,0:T(8,128)(2,1)S(1)}, bf16[40,1024]{1,0:T(8,128)(2,1)S(1)}, u32[]{:S(2)}, u32[]{:S(2)}) %collective-permute-start.10) | collective-permute-done | bytes 81952 | tf_op jit(solution)/shard_map/ppermute | solution.py:25
  38.6 1.3 %collective-permute-done.19.came_ref = bf16[4,40,1024]{2,1,0:T(8,128)(2,1)S(1)} collective-permute-done((bf16[4,40,1024]{2,1,0:T(8,128)(2,1)S(1)}, bf16[4,40,1024]{2,1,0:T(8,128)(2,1)S(1)}, u32[]{:S(2)}, u32[]{:S(2)}) %collective-permute-start.19) | collective-permute-done | bytes 327712 | tf_op jit(solution)/shard_map/ppermute | solution.py:25
  41.4 2.1 %collective-permute-start.22 = (bf16[40,1024]{1,0:T(8,128)(2,1)S(1)}, bf16[40,1024]{1,0:T(8,128)(2,1)S(1)}, u32[]{:S(2)}, u32[]{:S(2)}) collective-permute-start(bf16[40,1024]{1,0:T(8,128)(2,1)S(1)} %get-tuple-element.53), channel_id=1, source_target_pairs={{0,6},{1,7},{2,4},{3,5},{4,2},{5,3},{6,0},{7,1},{8,14},{9,15},{10,... | collective-permute-start | bytes 245768 | tf_op jit(solution)/shard_map/ppermute | solution.py:25
  43.5 1.6 %collective-permute-done.20.refs_0_ = bf16[40,1024]{1,0:T(8,128)(2,1)S(1)} collective-permute-done((bf16[40,1024]{1,0:T(8,128)(2,1)S(1)}, bf16[40,1024]{1,0:T(8,128)(2,1)S(1)}, u32[]{:S(2)}, u32[]{:S(2)}) %collective-permute-start.20) | collective-permute-done | bytes 81952 | tf_op jit(solution)/shard_map/ppermute | solution.py:25
  45.3 1.5 %collective-permute-done.22.refs_2_ = bf16[40,1024]{1,0:T(8,128)(2,1)S(1)} collective-permute-done((bf16[40,1024]{1,0:T(8,128)(2,1)S(1)}, bf16[40,1024]{1,0:T(8,128)(2,1)S(1)}, u32[]{:S(2)}, u32[]{:S(2)}) %collective-permute-start.22) | collective-permute-done | bytes 81952 | tf_op jit(solution)/shard_map/ppermute | solution.py:25
  52.9 1.3 %collective-permute-done.31.came_ref = bf16[4,40,1024]{2,1,0:T(8,128)(2,1)S(1)} collective-permute-done((bf16[4,40,1024]{2,1,0:T(8,128)(2,1)S(1)}, bf16[4,40,1024]{2,1,0:T(8,128)(2,1)S(1)}, u32[]{:S(2)}, u32[]{:S(2)}) %collective-permute-start.31) | collective-permute-done | bytes 327712 | tf_op jit(solution)/shard_map/ppermute | solution.py:25
  54.3 1.5 %collective-permute-start.32 = (bf16[40,1024]{1,0:T(8,128)(2,1)S(1)}, bf16[40,1024]{1,0:T(8,128)(2,1)S(1)}, u32[]{:S(2)}, u32[]{:S(2)}) collective-permute-start(bf16[40,1024]{1,0:T(8,128)(2,1)S(1)} %get-tuple-element.58), channel_id=1, source_target_pairs={{0,2},{1,3},{2,0},{3,1},{4,6},{5,7},{6,4},{7,5},{8,10},{9,11},{10,... | collective-permute-start | bytes 245768 | tf_op jit(solution)/shard_map/ppermute | solution.py:25
  55.8 1.2 collective-permute-start.33
  57.8 1.2 collective-permute-done.32.refs_0_
  59.1 1.2 collective-permute-done.33.refs_1_
  60.3 2.1 %collective-permute-done.34.refs_2_ = bf16[40,1024]{1,0:T(8,128)(2,1)S(1)} collective-permute-done((bf16[40,1024]{1,0:T(8,128)(2,1)S(1)}, bf16[40,1024]{1,0:T(8,128)(2,1)S(1)}, u32[]{:S(2)}, u32[]{:S(2)}) %collective-permute-start.34) | collective-permute-done | bytes 81952 | tf_op jit(solution)/shard_map/ppermute | solution.py:25
  62.4 1.3 %collective-permute-start.41 = (bf16[40,1024]{1,0:T(8,128)(2,1)S(1)}, bf16[40,1024]{1,0:T(8,128)(2,1)S(1)}, u32[]{:S(2)}, u32[]{:S(2)}) collective-permute-start(bf16[40,1024]{1,0:T(8,128)(2,1)S(1)} %finish_sum.5), channel_id=1, source_target_pairs={{16,30},{17,31},{18,28},{19,29},{20,26},{21,27},{22,24},{23,25}} | collective-permute-start | bytes 245768 | tf_op jit(solution)/shard_map/ppermute | solution.py:37
  63.7 1.3 %collective-permute-start.39 = (bf16[40,1024]{1,0:T(8,128)(2,1)S(1)}, bf16[40,1024]{1,0:T(8,128)(2,1)S(1)}, u32[]{:S(2)}, u32[]{:S(2)}) collective-permute-start(bf16[40,1024]{1,0:T(8,128)(2,1)S(1)} %finish_sum.5), channel_id=1, source_target_pairs={{16,28},{17,29},{18,30},{19,31},{20,24},{21,25},{22,26},{23,27}} | collective-permute-start | bytes 245768 | tf_op jit(solution)/shard_map/ppermute | solution.py:37
  65.0 1.3 %collective-permute-start.37 = (bf16[40,1024]{1,0:T(8,128)(2,1)S(1)}, bf16[40,1024]{1,0:T(8,128)(2,1)S(1)}, u32[]{:S(2)}, u32[]{:S(2)}) collective-permute-start(bf16[40,1024]{1,0:T(8,128)(2,1)S(1)} %finish_sum.5), channel_id=1, source_target_pairs={{16,26},{17,27},{18,24},{19,25},{20,30},{21,31},{22,28},{23,29}} | collective-permute-start | bytes 245768 | tf_op jit(solution)/shard_map/ppermute | solution.py:37
  66.3 1.3 %collective-permute-start.35 = (bf16[40,1024]{1,0:T(8,128)(2,1)S(1)}, bf16[40,1024]{1,0:T(8,128)(2,1)S(1)}, u32[]{:S(2)}, u32[]{:S(2)}) collective-permute-start(bf16[40,1024]{1,0:T(8,128)(2,1)S(1)} %finish_sum.5), channel_id=1, source_target_pairs={{16,24},{17,25},{18,26},{19,27},{20,28},{21,29},{22,30},{23,31}} | collective-permute-start | bytes 245768 | tf_op jit(solution)/shard_map/ppermute | solution.py:37
  67.6 30.3 %collective-permute-done.41.refs_11_ = bf16[40,1024]{1,0:T(8,128)(2,1)S(1)} collective-permute-done((bf16[40,1024]{1,0:T(8,128)(2,1)S(1)}, bf16[40,1024]{1,0:T(8,128)(2,1)S(1)}, u32[]{:S(2)}, u32[]{:S(2)}) %collective-permute-start.41) | collective-permute-done | bytes 81952 | tf_op jit(solution)/shard_map/ppermute | solution.py:37
  97.9 1.2 collective-permute-done.39.refs_9_
  99.1 1.2 collective-permute-done.37.refs_7_
  101.9 9.5 %layer_3.1 = (bf16[4,8,8192]{2,1,0:T(8,128)(2,1)S(1)}, bf16[4,8,8192]{2,1,0:T(8,128)(2,1)S(1)}, bf16[8,8192]{1,0:T(8,128)(2,1)S(1)}) custom-call(s32[4]{0:T(128)} %refs_0_.7, s32[16,28]{1,0:T(8,128)} %bitcast.19, s32[16,28]{1,0:T(8,128)} %bitcast.23, f32[64,128]{1,0:T(8,128)S(1)} %bitcast.10, ...), custom_call_target="tpu_custom_call" | custom-call | flops 1761607680 | tf_op jit(solution)/shard_map/layer_3/pallas_call | solution.py:331
  111.7 1.3 %collective-permute-start.43 = (bf16[8,8192]{1,0:T(8,128)(2,1)S(1)}, bf16[8,8192]{1,0:T(8,128)(2,1)S(1)}, u32[]{:S(2)}, u32[]{:S(2)}) collective-permute-start(bf16[8,8192]{1,0:T(8,128)(2,1)S(1)} %get-tuple-element.62.x_ref), channel_id=1, source_target_pairs={{8,0},{16,8},{24,16},{9,1},{17,9},{25,17},{10,2},{18,10},{26,18},{... | collective-permute-start | bytes 393224 | tf_op jit(solution)/shard_map/ppermute | solution.py:447
  113.6 1.2 collective-permute-start.45
  115.9 1.3 %collective-permute-start.47 = (bf16[8,8192]{1,0:T(8,128)(2,1)S(1)}, bf16[8,8192]{1,0:T(8,128)(2,1)S(1)}, u32[]{:S(2)}, u32[]{:S(2)}) collective-permute-start(bf16[8,8192]{1,0:T(8,128)(2,1)S(1)} %get-tuple-element.68), channel_id=1, source_target_pairs={{0,6},{1,7},{2,4},{3,5},{4,2},{5,3},{6,0},{7,1},{8,14},{9,15},{10,... | collective-permute-start | bytes 393224 | tf_op jit(solution)/shard_map/ppermute | solution.py:25
  117.1 2.8 %collective-permute-done.45.refs_0_ = bf16[8,8192]{1,0:T(8,128)(2,1)S(1)} collective-permute-done((bf16[8,8192]{1,0:T(8,128)(2,1)S(1)}, bf16[8,8192]{1,0:T(8,128)(2,1)S(1)}, u32[]{:S(2)}, u32[]{:S(2)}) %collective-permute-start.45) | collective-permute-done | bytes 131104 | tf_op jit(solution)/shard_map/ppermute | solution.py:25
  120.0 2.9 %collective-permute-done.46.refs_1_ = bf16[8,8192]{1,0:T(8,128)(2,1)S(1)} collective-permute-done((bf16[8,8192]{1,0:T(8,128)(2,1)S(1)}, bf16[8,8192]{1,0:T(8,128)(2,1)S(1)}, u32[]{:S(2)}, u32[]{:S(2)}) %collective-permute-start.46) | collective-permute-done | bytes 131104 | tf_op jit(solution)/shard_map/ppermute | solution.py:25
  (81 shorter events, 24.4 us)
Async XLA Ops:
  1.0 8.9 %collective-permute-start.3 = (bf16[8,8192]{1,0:T(8,128)(2,1)S(1)}, bf16[8,8192]{1,0:T(8,128)(2,1)S(1)}, u32[]{:S(2)}, u32[]{:S(2)}) collective-permute-start(bf16[8,8192]{1,0:T(8,128)(2,1)S(1)} %reshape.7.refs_8_.refs_13_), channel_id=1, source_target_pairs={{0,6},{1,7},{2,4},{3,5},{4,2},{5,3},{6,0},{7,1},{8,14},{9,15},{10,... | collective-permute-start | bytes 393224 | tf_op jit(solution)/shard_map/ppermute | solution.py:25
  3.5 6.5 %collective-permute-start.2 = (bf16[8,8192]{1,0:T(8,128)(2,1)S(1)}, bf16[8,8192]{1,0:T(8,128)(2,1)S(1)}, u32[]{:S(2)}, u32[]{:S(2)}) collective-permute-start(bf16[8,8192]{1,0:T(8,128)(2,1)S(1)} %reshape.7.refs_8_.refs_13_), channel_id=1, source_target_pairs={{0,4},{1,5},{2,6},{3,7},{4,0},{5,1},{6,2},{7,3},{8,12},{9,13},{10,... | collective-permute-start | bytes 393224 | tf_op jit(solution)/shard_map/ppermute | solution.py:25
  4.0 6.0 %collective-permute-start.1 = (bf16[8,8192]{1,0:T(8,128)(2,1)S(1)}, bf16[8,8192]{1,0:T(8,128)(2,1)S(1)}, u32[]{:S(2)}, u32[]{:S(2)}) collective-permute-start(bf16[8,8192]{1,0:T(8,128)(2,1)S(1)} %reshape.7.refs_8_.refs_13_), channel_id=1, source_target_pairs={{0,2},{1,3},{2,0},{3,1},{4,6},{5,7},{6,4},{7,5},{8,10},{9,11},{10,... | collective-permute-start | bytes 393224 | tf_op jit(solution)/shard_map/ppermute | solution.py:25
  4.5 6.5 %collective-permute-start = (bf16[8,8192]{1,0:T(8,128)(2,1)S(1)}, bf16[8,8192]{1,0:T(8,128)(2,1)S(1)}, u32[]{:S(2)}, u32[]{:S(2)}) collective-permute-start(bf16[8,8192]{1,0:T(8,128)(2,1)S(1)} %reshape.7.refs_8_.refs_13_), channel_id=1, source_target_pairs={{0,1},{1,0},{2,3},{3,2},{4,5},{5,4},{6,7},{7,6},{8,9},{9,8},{10,11... | collective-permute-start | bytes 393224 | tf_op jit(solution)/shard_map/ppermute | solution.py:25
  22.2 1.7 %collective-permute-start.7 = (bf16[4,40,1024]{2,1,0:T(8,128)(2,1)S(1)}, bf16[4,40,1024]{2,1,0:T(8,128)(2,1)S(1)}, u32[]{:S(2)}, u32[]{:S(2)}) collective-permute-start(bf16[4,40,1024]{2,1,0:T(8,128)(2,1)S(1)} %get-tuple-element.43), channel_id=1, source_target_pairs={{0,1},{1,0},{2,3},{3,2},{4,5},{5,4},{6,7},{7,6},{8,9},{9,8},{10,11... | collective-permute-start | bytes 983048 | tf_op jit(solution)/shard_map/ppermute | solution.py:25
  24.0 4.7 %collective-permute-start.8 = (bf16[40,1024]{1,0:T(8,128)(2,1)S(1)}, bf16[40,1024]{1,0:T(8,128)(2,1)S(1)}, u32[]{:S(2)}, u32[]{:S(2)}) collective-permute-start(bf16[40,1024]{1,0:T(8,128)(2,1)S(1)} %get-tuple-element.45), channel_id=1, source_target_pairs={{0,2},{1,3},{2,0},{3,1},{4,6},{5,7},{6,4},{7,5},{8,10},{9,11},{10,... | collective-permute-start | bytes 245768 | tf_op jit(solution)/shard_map/ppermute | solution.py:25
  25.6 5.3 %collective-permute-start.9 = (bf16[40,1024]{1,0:T(8,128)(2,1)S(1)}, bf16[40,1024]{1,0:T(8,128)(2,1)S(1)}, u32[]{:S(2)}, u32[]{:S(2)}) collective-permute-start(bf16[40,1024]{1,0:T(8,128)(2,1)S(1)} %get-tuple-element.46), channel_id=1, source_target_pairs={{0,4},{1,5},{2,6},{3,7},{4,0},{5,1},{6,2},{7,3},{8,12},{9,13},{10,... | collective-permute-start | bytes 245768 | tf_op jit(solution)/shard_map/ppermute | solution.py:25
  27.1 5.3 %collective-permute-start.10 = (bf16[40,1024]{1,0:T(8,128)(2,1)S(1)}, bf16[40,1024]{1,0:T(8,128)(2,1)S(1)}, u32[]{:S(2)}, u32[]{:S(2)}) collective-permute-start(bf16[40,1024]{1,0:T(8,128)(2,1)S(1)} %get-tuple-element.47), channel_id=1, source_target_pairs={{0,6},{1,7},{2,4},{3,5},{4,2},{5,3},{6,0},{7,1},{8,14},{9,15},{10,... | collective-permute-start | bytes 245768 | tf_op jit(solution)/shard_map/ppermute | solution.py:25
  32.5 2.7 %collective-permute-start.17 = (bf16[40,1024]{1,0:T(8,128)(2,1)S(1)}, bf16[40,1024]{1,0:T(8,128)(2,1)S(1)}, u32[]{:S(2)}, u32[]{:S(2)}) collective-permute-start(bf16[40,1024]{1,0:T(8,128)(2,1)S(1)} %finish_sum.3), channel_id=1, source_target_pairs={{0,14},{1,15},{2,12},{3,13},{4,10},{5,11},{6,8},{7,9}} | collective-permute-start | bytes 245768 | tf_op jit(solution)/shard_map/ppermute | solution.py:37
  33.1 2.1 %collective-permute-start.15 = (bf16[40,1024]{1,0:T(8,128)(2,1)S(1)}, bf16[40,1024]{1,0:T(8,128)(2,1)S(1)}, u32[]{:S(2)}, u32[]{:S(2)}) collective-permute-start(bf16[40,1024]{1,0:T(8,128)(2,1)S(1)} %finish_sum.3), channel_id=1, source_target_pairs={{0,12},{1,13},{2,14},{3,15},{4,8},{5,9},{6,10},{7,11}} | collective-permute-start | bytes 245768 | tf_op jit(solution)/shard_map/ppermute | solution.py:37
  33.8 1.9 %collective-permute-start.13 = (bf16[40,1024]{1,0:T(8,128)(2,1)S(1)}, bf16[40,1024]{1,0:T(8,128)(2,1)S(1)}, u32[]{:S(2)}, u32[]{:S(2)}) collective-permute-start(bf16[40,1024]{1,0:T(8,128)(2,1)S(1)} %finish_sum.3), channel_id=1, source_target_pairs={{0,10},{1,11},{2,8},{3,9},{4,14},{5,15},{6,12},{7,13}} | collective-permute-start | bytes 245768 | tf_op jit(solution)/shard_map/ppermute | solution.py:37
  38.2 1.7 %collective-permute-start.19 = (bf16[4,40,1024]{2,1,0:T(8,128)(2,1)S(1)}, bf16[4,40,1024]{2,1,0:T(8,128)(2,1)S(1)}, u32[]{:S(2)}, u32[]{:S(2)}) collective-permute-start(bf16[4,40,1024]{2,1,0:T(8,128)(2,1)S(1)} %get-tuple-element.49), channel_id=1, source_target_pairs={{0,1},{1,0},{2,3},{3,2},{4,5},{5,4},{6,7},{7,6},{8,9},{9,8},{10,11... | collective-permute-start | bytes 983048 | tf_op jit(solution)/shard_map/ppermute | solution.py:25
  39.9 5.1 %collective-permute-start.20 = (bf16[40,1024]{1,0:T(8,128)(2,1)S(1)}, bf16[40,1024]{1,0:T(8,128)(2,1)S(1)}, u32[]{:S(2)}, u32[]{:S(2)}) collective-permute-start(bf16[40,1024]{1,0:T(8,128)(2,1)S(1)} %get-tuple-element.51), channel_id=1, source_target_pairs={{0,2},{1,3},{2,0},{3,1},{4,6},{5,7},{6,4},{7,5},{8,10},{9,11},{10,... | collective-permute-start | bytes 245768 | tf_op jit(solution)/shard_map/ppermute | solution.py:25
  40.5 4.8 %collective-permute-start.21 = (bf16[40,1024]{1,0:T(8,128)(2,1)S(1)}, bf16[40,1024]{1,0:T(8,128)(2,1)S(1)}, u32[]{:S(2)}, u32[]{:S(2)}) collective-permute-start(bf16[40,1024]{1,0:T(8,128)(2,1)S(1)} %get-tuple-element.52), channel_id=1, source_target_pairs={{0,4},{1,5},{2,6},{3,7},{4,0},{5,1},{6,2},{7,3},{8,12},{9,13},{10,... | collective-permute-start | bytes 245768 | tf_op jit(solution)/shard_map/ppermute | solution.py:25
  41.4 5.4 %collective-permute-start.22 = (bf16[40,1024]{1,0:T(8,128)(2,1)S(1)}, bf16[40,1024]{1,0:T(8,128)(2,1)S(1)}, u32[]{:S(2)}, u32[]{:S(2)}) collective-permute-start(bf16[40,1024]{1,0:T(8,128)(2,1)S(1)} %get-tuple-element.53), channel_id=1, source_target_pairs={{0,6},{1,7},{2,4},{3,5},{4,2},{5,3},{6,0},{7,1},{8,14},{9,15},{10,... | collective-permute-start | bytes 245768 | tf_op jit(solution)/shard_map/ppermute | solution.py:25
  46.8 2.7 %collective-permute-start.29 = (bf16[40,1024]{1,0:T(8,128)(2,1)S(1)}, bf16[40,1024]{1,0:T(8,128)(2,1)S(1)}, u32[]{:S(2)}, u32[]{:S(2)}) collective-permute-start(bf16[40,1024]{1,0:T(8,128)(2,1)S(1)} %finish_sum.4), channel_id=1, source_target_pairs={{8,22},{9,23},{10,20},{11,21},{12,18},{13,19},{14,16},{15,17}} | collective-permute-start | bytes 245768 | tf_op jit(solution)/shard_map/ppermute | solution.py:37
  47.5 2.1 %collective-permute-start.27 = (bf16[40,1024]{1,0:T(8,128)(2,1)S(1)}, bf16[40,1024]{1,0:T(8,128)(2,1)S(1)}, u32[]{:S(2)}, u32[]{:S(2)}) collective-permute-start(bf16[40,1024]{1,0:T(8,128)(2,1)S(1)} %finish_sum.4), channel_id=1, source_target_pairs={{8,20},{9,21},{10,22},{11,23},{12,16},{13,17},{14,18},{15,19}} | collective-permute-start | bytes 245768 | tf_op jit(solution)/shard_map/ppermute | solution.py:37
  48.2 1.9 %collective-permute-start.25 = (bf16[40,1024]{1,0:T(8,128)(2,1)S(1)}, bf16[40,1024]{1,0:T(8,128)(2,1)S(1)}, u32[]{:S(2)}, u32[]{:S(2)}) collective-permute-start(bf16[40,1024]{1,0:T(8,128)(2,1)S(1)} %finish_sum.4), channel_id=1, source_target_pairs={{8,18},{9,19},{10,16},{11,17},{12,22},{13,23},{14,20},{15,21}} | collective-permute-start | bytes 245768 | tf_op jit(solution)/shard_map/ppermute | solution.py:37
  52.5 1.7 %collective-permute-start.31 = (bf16[4,40,1024]{2,1,0:T(8,128)(2,1)S(1)}, bf16[4,40,1024]{2,1,0:T(8,128)(2,1)S(1)}, u32[]{:S(2)}, u32[]{:S(2)}) collective-permute-start(bf16[4,40,1024]{2,1,0:T(8,128)(2,1)S(1)} %get-tuple-element.56), channel_id=1, source_target_pairs={{0,1},{1,0},{2,3},{3,2},{4,5},{5,4},{6,7},{7,6},{8,9},{9,8},{10,11... | collective-permute-start | bytes 983048 | tf_op jit(solution)/shard_map/ppermute | solution.py:25
  54.3 4.8 %collective-permute-start.32 = (bf16[40,1024]{1,0:T(8,128)(2,1)S(1)}, bf16[40,1024]{1,0:T(8,128)(2,1)S(1)}, u32[]{:S(2)}, u32[]{:S(2)}) collective-permute-start(bf16[40,1024]{1,0:T(8,128)(2,1)S(1)} %get-tuple-element.58), channel_id=1, source_target_pairs={{0,2},{1,3},{2,0},{3,1},{4,6},{5,7},{6,4},{7,5},{8,10},{9,11},{10,... | collective-permute-start | bytes 245768 | tf_op jit(solution)/shard_map/ppermute | solution.py:25
  55.8 4.4 %collective-permute-start.33 = (bf16[40,1024]{1,0:T(8,128)(2,1)S(1)}, bf16[40,1024]{1,0:T(8,128)(2,1)S(1)}, u32[]{:S(2)}, u32[]{:S(2)}) collective-permute-start(bf16[40,1024]{1,0:T(8,128)(2,1)S(1)} %get-tuple-element.59), channel_id=1, source_target_pairs={{0,4},{1,5},{2,6},{3,7},{4,0},{5,1},{6,2},{7,3},{8,12},{9,13},{10,... | collective-permute-start | bytes 245768 | tf_op jit(solution)/shard_map/ppermute | solution.py:25
  57.0 5.3 %collective-permute-start.34 = (bf16[40,1024]{1,0:T(8,128)(2,1)S(1)}, bf16[40,1024]{1,0:T(8,128)(2,1)S(1)}, u32[]{:S(2)}, u32[]{:S(2)}) collective-permute-start(bf16[40,1024]{1,0:T(8,128)(2,1)S(1)} %get-tuple-element.60), channel_id=1, source_target_pairs={{0,6},{1,7},{2,4},{3,5},{4,2},{5,3},{6,0},{7,1},{8,14},{9,15},{10,... | collective-permute-start | bytes 245768 | tf_op jit(solution)/shard_map/ppermute | solution.py:25
  62.4 35.5 %collective-permute-start.41 = (bf16[40,1024]{1,0:T(8,128)(2,1)S(1)}, bf16[40,1024]{1,0:T(8,128)(2,1)S(1)}, u32[]{:S(2)}, u32[]{:S(2)}) collective-permute-start(bf16[40,1024]{1,0:T(8,128)(2,1)S(1)} %finish_sum.5), channel_id=1, source_target_pairs={{16,30},{17,31},{18,28},{19,29},{20,26},{21,27},{22,24},{23,25}} | collective-permute-start | bytes 245768 | tf_op jit(solution)/shard_map/ppermute | solution.py:37
  63.7 35.4 %collective-permute-start.39 = (bf16[40,1024]{1,0:T(8,128)(2,1)S(1)}, bf16[40,1024]{1,0:T(8,128)(2,1)S(1)}, u32[]{:S(2)}, u32[]{:S(2)}) collective-permute-start(bf16[40,1024]{1,0:T(8,128)(2,1)S(1)} %finish_sum.5), channel_id=1, source_target_pairs={{16,28},{17,29},{18,30},{19,31},{20,24},{21,25},{22,26},{23,27}} | collective-permute-start | bytes 245768 | tf_op jit(solution)/shard_map/ppermute | solution.py:37
  65.0 35.3 %collective-permute-start.37 = (bf16[40,1024]{1,0:T(8,128)(2,1)S(1)}, bf16[40,1024]{1,0:T(8,128)(2,1)S(1)}, u32[]{:S(2)}, u32[]{:S(2)}) collective-permute-start(bf16[40,1024]{1,0:T(8,128)(2,1)S(1)} %finish_sum.5), channel_id=1, source_target_pairs={{16,26},{17,27},{18,24},{19,25},{20,30},{21,31},{22,28},{23,29}} | collective-permute-start | bytes 245768 | tf_op jit(solution)/shard_map/ppermute | solution.py:37
  66.3 34.4 %collective-permute-start.35 = (bf16[40,1024]{1,0:T(8,128)(2,1)S(1)}, bf16[40,1024]{1,0:T(8,128)(2,1)S(1)}, u32[]{:S(2)}, u32[]{:S(2)}) collective-permute-start(bf16[40,1024]{1,0:T(8,128)(2,1)S(1)} %finish_sum.5), channel_id=1, source_target_pairs={{16,24},{17,25},{18,26},{19,27},{20,28},{21,29},{22,30},{23,31}} | collective-permute-start | bytes 245768 | tf_op jit(solution)/shard_map/ppermute | solution.py:37
  97.9 2.9 %collective-permute-start.42 = (bf16[40,1024]{1,0:T(8,128)(2,1)S(1)}, bf16[40,1024]{1,0:T(8,128)(2,1)S(1)}, u32[]{:S(2)}, u32[]{:S(2)}) collective-permute-start(bf16[40,1024]{1,0:T(8,128)(2,1)S(1)} %collective-permute-done.41.refs_11_), channel_id=1, source_target_pairs={{0,1},{1,0},{2,3},{3,2},{4,5},{5,4},{6,7},{7,6},{8,9},{9,8},{10,11... | collective-permute-start | bytes 245768 | tf_op jit(solution)/shard_map/ppermute | solution.py:25
  111.5 2.0 %collective-permute-start.44 = (bf16[4,8,8192]{2,1,0:T(8,128)(2,1)S(1)}, bf16[4,8,8192]{2,1,0:T(8,128)(2,1)S(1)}, u32[]{:S(2)}, u32[]{:S(2)}) collective-permute-start(bf16[4,8,8192]{2,1,0:T(8,128)(2,1)S(1)} %get-tuple-element.64), channel_id=1, source_target_pairs={{0,1},{1,0},{2,3},{3,2},{4,5},{5,4},{6,7},{7,6},{8,9},{9,8},{10,11... | collective-permute-start | bytes 1572872 | tf_op jit(solution)/shard_map/ppermute | solution.py:25
  111.7 5.4 %collective-permute-start.43 = (bf16[8,8192]{1,0:T(8,128)(2,1)S(1)}, bf16[8,8192]{1,0:T(8,128)(2,1)S(1)}, u32[]{:S(2)}, u32[]{:S(2)}) collective-permute-start(bf16[8,8192]{1,0:T(8,128)(2,1)S(1)} %get-tuple-element.62.x_ref), channel_id=1, source_target_pairs={{8,0},{16,8},{24,16},{9,1},{17,9},{25,17},{10,2},{18,10},{26,18},{... | collective-permute-start | bytes 393224 | tf_op jit(solution)/shard_map/ppermute | solution.py:447
  113.6 6.4 %collective-permute-start.45 = (bf16[8,8192]{1,0:T(8,128)(2,1)S(1)}, bf16[8,8192]{1,0:T(8,128)(2,1)S(1)}, u32[]{:S(2)}, u32[]{:S(2)}) collective-permute-start(bf16[8,8192]{1,0:T(8,128)(2,1)S(1)} %get-tuple-element.66), channel_id=1, source_target_pairs={{0,2},{1,3},{2,0},{3,1},{4,6},{5,7},{6,4},{7,5},{8,10},{9,11},{10,... | collective-permute-start | bytes 393224 | tf_op jit(solution)/shard_map/ppermute | solution.py:25
  114.8 8.1 %collective-permute-start.46 = (bf16[8,8192]{1,0:T(8,128)(2,1)S(1)}, bf16[8,8192]{1,0:T(8,128)(2,1)S(1)}, u32[]{:S(2)}, u32[]{:S(2)}) collective-permute-start(bf16[8,8192]{1,0:T(8,128)(2,1)S(1)} %get-tuple-element.67), channel_id=1, source_target_pairs={{0,4},{1,5},{2,6},{3,7},{4,0},{5,1},{6,2},{7,3},{8,12},{9,13},{10,... | collective-permute-start | bytes 393224 | tf_op jit(solution)/shard_map/ppermute | solution.py:25
  115.9 7.0 %collective-permute-start.47 = (bf16[8,8192]{1,0:T(8,128)(2,1)S(1)}, bf16[8,8192]{1,0:T(8,128)(2,1)S(1)}, u32[]{:S(2)}, u32[]{:S(2)}) collective-permute-start(bf16[8,8192]{1,0:T(8,128)(2,1)S(1)} %get-tuple-element.68), channel_id=1, source_target_pairs={{0,6},{1,7},{2,4},{3,5},{4,2},{5,3},{6,0},{7,1},{8,14},{9,15},{10,... | collective-permute-start | bytes 393224 | tf_op jit(solution)/shard_map/ppermute | solution.py:25
  (17 other events, 24.1 us)

commit v5 on v4

--- a/solution.py
+++ b/solution.py
@@ -319,7 +319,7 @@
     block_total = gain.shape[0]
     width = block_total * block // shard_total
     whole = preloaded(blocks) if first else blocks
-    unroll = max(u for u in ((1, 2, 4) if first else (1, 2, 4, 8)) if blocks % u == 0 and whole % u == 0)
+    unroll = max(u for u in ((1, 2, 4) if first else (1, 2, 4, 8, 16)) if blocks % u == 0 and whole % u == 0)
     group = micro_count * own_count
     part = (group, block_total * block) if last else (rows, width)
     outs = [pltpu.VMEM((shard_total // 2,) + part, bf16)] * 2

time: 124 us -> 123 us (level)
  no operation moved by 1% of the time
where the time goes in v5:
time: 123 us
  waiting for transfers between devices  59.1 us (48%)
  starting transfers between devices  34.2 us (28%)
  Pallas kernels  28 us (23%)
    ppermute x12, waiting for transfers between devices, next_section(): lax.ppermute(value, ('section', 'shard'), [(start + i, start + size + (i...  32.4 us
    ppermute x35, waiting for transfers between devices, xor_shard(): return lax.ppermute(value, 'shard', [(i, i ^ mask) for i in range(size)])  26.7 us
    ppermute x35, starting transfers between devices, xor_shard(): return lax.ppermute(value, 'shard', [(i, i ^ mask) for i in range(size)])  22.5 us
    pallas_call x4, Pallas kernels, layer_step(): pl.pallas_call(functools.partial(layer_kernel, turn, last, rows, unroll,...  21.4 us
    ppermute x12, starting transfers between devices, next_section(): lax.ppermute(value, ('section', 'shard'), [(start + i, start + size + (i...  10.5 us
    pallas_call x1, Pallas kernels, load_weights(): pl.pallas_call(load_kernel, out_shape=pltpu.VMEM((3,) + gate.shape, bf16)...  5.33 us
  transfers between devices with their start and end apart: 48, of which 34 were waited for; matrix products, arithmetic and copies ran while one was open for 0% of the time, Pallas kernels for 4%

profile of v5, /device:TPU:24, one launch (start us, length us, event | category | flops | bytes accessed | tf_op | source)
XLA Modules:
  0.0 122.6 jit_solution(9289182822461517333)
XLA Ops:
  1.0 2.5 %collective-permute-start.3 = (bf16[8,8192]{1,0:T(8,128)(2,1)S(1)}, bf16[8,8192]{1,0:T(8,128)(2,1)S(1)}, u32[]{:S(2)}, u32[]{:S(2)}) collective-permute-start(bf16[8,8192]{1,0:T(8,128)(2,1)S(1)} %reshape.7.refs_8_.refs_13_), channel_id=1, source_target_pairs={{0,6},{1,7},{2,4},{3,5},{4,2},{5,3},{6,0},{7,1},{8,14},{9,15},{10,... | collective-permute-start | bytes 393224 | tf_op jit(solution)/shard_map/ppermute | solution.py:25
  4.5 5.3 %load_weights.1.held_ref.refs_4_ = bf16[3,16,28,128,128]{4,3,2,1,0:T(8,128)(2,1)S(1)} custom-call(bf16[16,28,128,128]{3,2,1,0:T(8,128)(2,1)} %bitcast.11, bf16[16,28,128,128]{3,2,1,0:T(8,128)(2,1)} %bitcast.13), custom_call_target="tpu_custom_call" | custom-call | bytes 29360128 | tf_op jit(solution)/shard_map/load_weights/pallas_call | solution.py:85
  12.0 10.2 %layer_0.1 = (bf16[4,40,1024]{2,1,0:T(8,128)(2,1)S(1)}, bf16[4,40,1024]{2,1,0:T(8,128)(2,1)S(1)}, bf16[40,1024]{1,0:T(8,128)(2,1)S(1)}, bf16[3,16,28,128,128]{4,3,2,1,0:T(8,128)(2,1)S(1)}) custom-call(s32[4]{0:T(128)} %refs_0_.7, s32[16,28]{1,0:T(8,128)} %bitcast.16, s32[16,28]{1,0:T(8,128)} %bitcast.20, ...), custom_call_target="tpu_custom_call", output_to_operand_aliasing={{3}: (4, {})} | custom-call | flops 1761607680 | tf_op jit(solution)/shard_map/layer_0/pallas_call | solution.py:331
  22.6 1.3 %collective-permute-done.7.came_ref = bf16[4,40,1024]{2,1,0:T(8,128)(2,1)S(1)} collective-permute-done((bf16[4,40,1024]{2,1,0:T(8,128)(2,1)S(1)}, bf16[4,40,1024]{2,1,0:T(8,128)(2,1)S(1)}, u32[]{:S(2)}, u32[]{:S(2)}) %collective-permute-start.7) | collective-permute-done | bytes 327712 | tf_op jit(solution)/shard_map/ppermute | solution.py:25
  24.0 1.6 %collective-permute-start.8 = (bf16[40,1024]{1,0:T(8,128)(2,1)S(1)}, bf16[40,1024]{1,0:T(8,128)(2,1)S(1)}, u32[]{:S(2)}, u32[]{:S(2)}) collective-permute-start(bf16[40,1024]{1,0:T(8,128)(2,1)S(1)} %get-tuple-element.45), channel_id=1, source_target_pairs={{0,2},{1,3},{2,0},{3,1},{4,6},{5,7},{6,4},{7,5},{8,10},{9,11},{10,... | collective-permute-start | bytes 245768 | tf_op jit(solution)/shard_map/ppermute | solution.py:25
  25.6 1.5 %collective-permute-start.9 = (bf16[40,1024]{1,0:T(8,128)(2,1)S(1)}, bf16[40,1024]{1,0:T(8,128)(2,1)S(1)}, u32[]{:S(2)}, u32[]{:S(2)}) collective-permute-start(bf16[40,1024]{1,0:T(8,128)(2,1)S(1)} %get-tuple-element.46), channel_id=1, source_target_pairs={{0,4},{1,5},{2,6},{3,7},{4,0},{5,1},{6,2},{7,3},{8,12},{9,13},{10,... | collective-permute-start | bytes 245768 | tf_op jit(solution)/shard_map/ppermute | solution.py:25
  27.6 1.2 collective-permute-done.8.refs_0_
  28.7 2.1 %collective-permute-done.9.refs_1_ = bf16[40,1024]{1,0:T(8,128)(2,1)S(1)} collective-permute-done((bf16[40,1024]{1,0:T(8,128)(2,1)S(1)}, bf16[40,1024]{1,0:T(8,128)(2,1)S(1)}, u32[]{:S(2)}, u32[]{:S(2)}) %collective-permute-start.9) | collective-permute-done | bytes 81952 | tf_op jit(solution)/shard_map/ppermute | solution.py:25
  30.8 1.6 %collective-permute-done.10.refs_2_ = bf16[40,1024]{1,0:T(8,128)(2,1)S(1)} collective-permute-done((bf16[40,1024]{1,0:T(8,128)(2,1)S(1)}, bf16[40,1024]{1,0:T(8,128)(2,1)S(1)}, u32[]{:S(2)}, u32[]{:S(2)}) %collective-permute-start.10) | collective-permute-done | bytes 81952 | tf_op jit(solution)/shard_map/ppermute | solution.py:25
  38.6 1.3 %collective-permute-done.19.came_ref = bf16[4,40,1024]{2,1,0:T(8,128)(2,1)S(1)} collective-permute-done((bf16[4,40,1024]{2,1,0:T(8,128)(2,1)S(1)}, bf16[4,40,1024]{2,1,0:T(8,128)(2,1)S(1)}, u32[]{:S(2)}, u32[]{:S(2)}) %collective-permute-start.19) | collective-permute-done | bytes 327712 | tf_op jit(solution)/shard_map/ppermute | solution.py:25
  41.4 2.1 %collective-permute-start.22 = (bf16[40,1024]{1,0:T(8,128)(2,1)S(1)}, bf16[40,1024]{1,0:T(8,128)(2,1)S(1)}, u32[]{:S(2)}, u32[]{:S(2)}) collective-permute-start(bf16[40,1024]{1,0:T(8,128)(2,1)S(1)} %get-tuple-element.53), channel_id=1, source_target_pairs={{0,6},{1,7},{2,4},{3,5},{4,2},{5,3},{6,0},{7,1},{8,14},{9,15},{10,... | collective-permute-start | bytes 245768 | tf_op jit(solution)/shard_map/ppermute | solution.py:25
  43.5 1.6 %collective-permute-done.20.refs_0_ = bf16[40,1024]{1,0:T(8,128)(2,1)S(1)} collective-permute-done((bf16[40,1024]{1,0:T(8,128)(2,1)S(1)}, bf16[40,1024]{1,0:T(8,128)(2,1)S(1)}, u32[]{:S(2)}, u32[]{:S(2)}) %collective-permute-start.20) | collective-permute-done | bytes 81952 | tf_op jit(solution)/shard_map/ppermute | solution.py:25
  45.3 1.5 %collective-permute-done.22.refs_2_ = bf16[40,1024]{1,0:T(8,128)(2,1)S(1)} collective-permute-done((bf16[40,1024]{1,0:T(8,128)(2,1)S(1)}, bf16[40,1024]{1,0:T(8,128)(2,1)S(1)}, u32[]{:S(2)}, u32[]{:S(2)}) %collective-permute-start.22) | collective-permute-done | bytes 81952 | tf_op jit(solution)/shard_map/ppermute | solution.py:25
  52.9 1.3 %collective-permute-done.31.came_ref = bf16[4,40,1024]{2,1,0:T(8,128)(2,1)S(1)} collective-permute-done((bf16[4,40,1024]{2,1,0:T(8,128)(2,1)S(1)}, bf16[4,40,1024]{2,1,0:T(8,128)(2,1)S(1)}, u32[]{:S(2)}, u32[]{:S(2)}) %collective-permute-start.31) | collective-permute-done | bytes 327712 | tf_op jit(solution)/shard_map/ppermute | solution.py:25
  54.3 1.5 %collective-permute-start.32 = (bf16[40,1024]{1,0:T(8,128)(2,1)S(1)}, bf16[40,1024]{1,0:T(8,128)(2,1)S(1)}, u32[]{:S(2)}, u32[]{:S(2)}) collective-permute-start(bf16[40,1024]{1,0:T(8,128)(2,1)S(1)} %get-tuple-element.58), channel_id=1, source_target_pairs={{0,2},{1,3},{2,0},{3,1},{4,6},{5,7},{6,4},{7,5},{8,10},{9,11},{10,... | collective-permute-start | bytes 245768 | tf_op jit(solution)/shard_map/ppermute | solution.py:25
  55.8 1.2 collective-permute-start.33
  57.8 1.2 collective-permute-done.32.refs_0_
  59.1 1.2 collective-permute-done.33.refs_1_
  60.3 2.1 %collective-permute-done.34.refs_2_ = bf16[40,1024]{1,0:T(8,128)(2,1)S(1)} collective-permute-done((bf16[40,1024]{1,0:T(8,128)(2,1)S(1)}, bf16[40,1024]{1,0:T(8,128)(2,1)S(1)}, u32[]{:S(2)}, u32[]{:S(2)}) %collective-permute-start.34) | collective-permute-done | bytes 81952 | tf_op jit(solution)/shard_map/ppermute | solution.py:25
  62.4 1.3 %collective-permute-start.41 = (bf16[40,1024]{1,0:T(8,128)(2,1)S(1)}, bf16[40,1024]{1,0:T(8,128)(2,1)S(1)}, u32[]{:S(2)}, u32[]{:S(2)}) collective-permute-start(bf16[40,1024]{1,0:T(8,128)(2,1)S(1)} %finish_sum.5), channel_id=1, source_target_pairs={{16,30},{17,31},{18,28},{19,29},{20,26},{21,27},{22,24},{23,25}} | collective-permute-start | bytes 245768 | tf_op jit(solution)/shard_map/ppermute | solution.py:37
  63.7 1.3 %collective-permute-start.39 = (bf16[40,1024]{1,0:T(8,128)(2,1)S(1)}, bf16[40,1024]{1,0:T(8,128)(2,1)S(1)}, u32[]{:S(2)}, u32[]{:S(2)}) collective-permute-start(bf16[40,1024]{1,0:T(8,128)(2,1)S(1)} %finish_sum.5), channel_id=1, source_target_pairs={{16,28},{17,29},{18,30},{19,31},{20,24},{21,25},{22,26},{23,27}} | collective-permute-start | bytes 245768 | tf_op jit(solution)/shard_map/ppermute | solution.py:37
  65.0 1.3 %collective-permute-start.37 = (bf16[40,1024]{1,0:T(8,128)(2,1)S(1)}, bf16[40,1024]{1,0:T(8,128)(2,1)S(1)}, u32[]{:S(2)}, u32[]{:S(2)}) collective-permute-start(bf16[40,1024]{1,0:T(8,128)(2,1)S(1)} %finish_sum.5), channel_id=1, source_target_pairs={{16,26},{17,27},{18,24},{19,25},{20,30},{21,31},{22,28},{23,29}} | collective-permute-start | bytes 245768 | tf_op jit(solution)/shard_map/ppermute | solution.py:37
  66.3 1.3 %collective-permute-start.35 = (bf16[40,1024]{1,0:T(8,128)(2,1)S(1)}, bf16[40,1024]{1,0:T(8,128)(2,1)S(1)}, u32[]{:S(2)}, u32[]{:S(2)}) collective-permute-start(bf16[40,1024]{1,0:T(8,128)(2,1)S(1)} %finish_sum.5), channel_id=1, source_target_pairs={{16,24},{17,25},{18,26},{19,27},{20,28},{21,29},{22,30},{23,31}} | collective-permute-start | bytes 245768 | tf_op jit(solution)/shard_map/ppermute | solution.py:37
  67.6 29.6 %collective-permute-done.41.refs_11_ = bf16[40,1024]{1,0:T(8,128)(2,1)S(1)} collective-permute-done((bf16[40,1024]{1,0:T(8,128)(2,1)S(1)}, bf16[40,1024]{1,0:T(8,128)(2,1)S(1)}, u32[]{:S(2)}, u32[]{:S(2)}) %collective-permute-start.41) | collective-permute-done | bytes 81952 | tf_op jit(solution)/shard_map/ppermute | solution.py:37
  97.2 1.3 %collective-permute-done.39.refs_9_ = bf16[40,1024]{1,0:T(8,128)(2,1)S(1)} collective-permute-done((bf16[40,1024]{1,0:T(8,128)(2,1)S(1)}, bf16[40,1024]{1,0:T(8,128)(2,1)S(1)}, u32[]{:S(2)}, u32[]{:S(2)}) %collective-permute-start.39) | collective-permute-done | bytes 81952 | tf_op jit(solution)/shard_map/ppermute | solution.py:37
  98.5 1.1 collective-permute-done.37.refs_7_
  101.3 9.3 %layer_3.1 = (bf16[4,8,8192]{2,1,0:T(8,128)(2,1)S(1)}, bf16[4,8,8192]{2,1,0:T(8,128)(2,1)S(1)}, bf16[8,8192]{1,0:T(8,128)(2,1)S(1)}) custom-call(s32[4]{0:T(128)} %refs_0_.7, s32[16,28]{1,0:T(8,128)} %bitcast.19, s32[16,28]{1,0:T(8,128)} %bitcast.23, f32[64,128]{1,0:T(8,128)S(1)} %bitcast.10, ...), custom_call_target="tpu_custom_call" | custom-call | flops 1761607680 | tf_op jit(solution)/shard_map/layer_3/pallas_call | solution.py:331
  110.8 1.3 %collective-permute-start.43 = (bf16[8,8192]{1,0:T(8,128)(2,1)S(1)}, bf16[8,8192]{1,0:T(8,128)(2,1)S(1)}, u32[]{:S(2)}, u32[]{:S(2)}) collective-permute-start(bf16[8,8192]{1,0:T(8,128)(2,1)S(1)} %get-tuple-element.62.x_ref), channel_id=1, source_target_pairs={{8,0},{16,8},{24,16},{9,1},{17,9},{25,17},{10,2},{18,10},{26,18},{... | collective-permute-start | bytes 393224 | tf_op jit(solution)/shard_map/ppermute | solution.py:447
  112.7 1.1 collective-permute-start.45
  114.9 1.3 %collective-permute-start.47 = (bf16[8,8192]{1,0:T(8,128)(2,1)S(1)}, bf16[8,8192]{1,0:T(8,128)(2,1)S(1)}, u32[]{:S(2)}, u32[]{:S(2)}) collective-permute-start(bf16[8,8192]{1,0:T(8,128)(2,1)S(1)} %get-tuple-element.68), channel_id=1, source_target_pairs={{0,6},{1,7},{2,4},{3,5},{4,2},{5,3},{6,0},{7,1},{8,14},{9,15},{10,... | collective-permute-start | bytes 393224 | tf_op jit(solution)/shard_map/ppermute | solution.py:25
  116.2 2.8 %collective-permute-done.45.refs_0_ = bf16[8,8192]{1,0:T(8,128)(2,1)S(1)} collective-permute-done((bf16[8,8192]{1,0:T(8,128)(2,1)S(1)}, bf16[8,8192]{1,0:T(8,128)(2,1)S(1)}, u32[]{:S(2)}, u32[]{:S(2)}) %collective-permute-start.45) | collective-permute-done | bytes 131104 | tf_op jit(solution)/shard_map/ppermute | solution.py:25
  119.1 2.8 %collective-permute-done.46.refs_1_ = bf16[8,8192]{1,0:T(8,128)(2,1)S(1)} collective-permute-done((bf16[8,8192]{1,0:T(8,128)(2,1)S(1)}, bf16[8,8192]{1,0:T(8,128)(2,1)S(1)}, u32[]{:S(2)}, u32[]{:S(2)}) %collective-permute-start.46) | collective-permute-done | bytes 131104 | tf_op jit(solution)/shard_map/ppermute | solution.py:25
  (81 shorter events, 24.4 us)
Async XLA Ops:
  1.0 8.9 %collective-permute-start.3 = (bf16[8,8192]{1,0:T(8,128)(2,1)S(1)}, bf16[8,8192]{1,0:T(8,128)(2,1)S(1)}, u32[]{:S(2)}, u32[]{:S(2)}) collective-permute-start(bf16[8,8192]{1,0:T(8,128)(2,1)S(1)} %reshape.7.refs_8_.refs_13_), channel_id=1, source_target_pairs={{0,6},{1,7},{2,4},{3,5},{4,2},{5,3},{6,0},{7,1},{8,14},{9,15},{10,... | collective-permute-start | bytes 393224 | tf_op jit(solution)/shard_map/ppermute | solution.py:25
  3.5 6.5 %collective-permute-start.2 = (bf16[8,8192]{1,0:T(8,128)(2,1)S(1)}, bf16[8,8192]{1,0:T(8,128)(2,1)S(1)}, u32[]{:S(2)}, u32[]{:S(2)}) collective-permute-start(bf16[8,8192]{1,0:T(8,128)(2,1)S(1)} %reshape.7.refs_8_.refs_13_), channel_id=1, source_target_pairs={{0,4},{1,5},{2,6},{3,7},{4,0},{5,1},{6,2},{7,3},{8,12},{9,13},{10,... | collective-permute-start | bytes 393224 | tf_op jit(solution)/shard_map/ppermute | solution.py:25
  4.0 6.0 %collective-permute-start.1 = (bf16[8,8192]{1,0:T(8,128)(2,1)S(1)}, bf16[8,8192]{1,0:T(8,128)(2,1)S(1)}, u32[]{:S(2)}, u32[]{:S(2)}) collective-permute-start(bf16[8,8192]{1,0:T(8,128)(2,1)S(1)} %reshape.7.refs_8_.refs_13_), channel_id=1, source_target_pairs={{0,2},{1,3},{2,0},{3,1},{4,6},{5,7},{6,4},{7,5},{8,10},{9,11},{10,... | collective-permute-start | bytes 393224 | tf_op jit(solution)/shard_map/ppermute | solution.py:25
  4.5 6.5 %collective-permute-start = (bf16[8,8192]{1,0:T(8,128)(2,1)S(1)}, bf16[8,8192]{1,0:T(8,128)(2,1)S(1)}, u32[]{:S(2)}, u32[]{:S(2)}) collective-permute-start(bf16[8,8192]{1,0:T(8,128)(2,1)S(1)} %reshape.7.refs_8_.refs_13_), channel_id=1, source_target_pairs={{0,1},{1,0},{2,3},{3,2},{4,5},{5,4},{6,7},{7,6},{8,9},{9,8},{10,11... | collective-permute-start | bytes 393224 | tf_op jit(solution)/shard_map/ppermute | solution.py:25
  22.2 1.7 %collective-permute-start.7 = (bf16[4,40,1024]{2,1,0:T(8,128)(2,1)S(1)}, bf16[4,40,1024]{2,1,0:T(8,128)(2,1)S(1)}, u32[]{:S(2)}, u32[]{:S(2)}) collective-permute-start(bf16[4,40,1024]{2,1,0:T(8,128)(2,1)S(1)} %get-tuple-element.43), channel_id=1, source_target_pairs={{0,1},{1,0},{2,3},{3,2},{4,5},{5,4},{6,7},{7,6},{8,9},{9,8},{10,11... | collective-permute-start | bytes 983048 | tf_op jit(solution)/shard_map/ppermute | solution.py:25
  24.0 4.7 %collective-permute-start.8 = (bf16[40,1024]{1,0:T(8,128)(2,1)S(1)}, bf16[40,1024]{1,0:T(8,128)(2,1)S(1)}, u32[]{:S(2)}, u32[]{:S(2)}) collective-permute-start(bf16[40,1024]{1,0:T(8,128)(2,1)S(1)} %get-tuple-element.45), channel_id=1, source_target_pairs={{0,2},{1,3},{2,0},{3,1},{4,6},{5,7},{6,4},{7,5},{8,10},{9,11},{10,... | collective-permute-start | bytes 245768 | tf_op jit(solution)/shard_map/ppermute | solution.py:25
  25.6 5.3 %collective-permute-start.9 = (bf16[40,1024]{1,0:T(8,128)(2,1)S(1)}, bf16[40,1024]{1,0:T(8,128)(2,1)S(1)}, u32[]{:S(2)}, u32[]{:S(2)}) collective-permute-start(bf16[40,1024]{1,0:T(8,128)(2,1)S(1)} %get-tuple-element.46), channel_id=1, source_target_pairs={{0,4},{1,5},{2,6},{3,7},{4,0},{5,1},{6,2},{7,3},{8,12},{9,13},{10,... | collective-permute-start | bytes 245768 | tf_op jit(solution)/shard_map/ppermute | solution.py:25
  27.1 5.3 %collective-permute-start.10 = (bf16[40,1024]{1,0:T(8,128)(2,1)S(1)}, bf16[40,1024]{1,0:T(8,128)(2,1)S(1)}, u32[]{:S(2)}, u32[]{:S(2)}) collective-permute-start(bf16[40,1024]{1,0:T(8,128)(2,1)S(1)} %get-tuple-element.47), channel_id=1, source_target_pairs={{0,6},{1,7},{2,4},{3,5},{4,2},{5,3},{6,0},{7,1},{8,14},{9,15},{10,... | collective-permute-start | bytes 245768 | tf_op jit(solution)/shard_map/ppermute | solution.py:25
  32.5 2.7 %collective-permute-start.17 = (bf16[40,1024]{1,0:T(8,128)(2,1)S(1)}, bf16[40,1024]{1,0:T(8,128)(2,1)S(1)}, u32[]{:S(2)}, u32[]{:S(2)}) collective-permute-start(bf16[40,1024]{1,0:T(8,128)(2,1)S(1)} %finish_sum.3), channel_id=1, source_target_pairs={{0,14},{1,15},{2,12},{3,13},{4,10},{5,11},{6,8},{7,9}} | collective-permute-start | bytes 245768 | tf_op jit(solution)/shard_map/ppermute | solution.py:37
  33.1 2.1 %collective-permute-start.15 = (bf16[40,1024]{1,0:T(8,128)(2,1)S(1)}, bf16[40,1024]{1,0:T(8,128)(2,1)S(1)}, u32[]{:S(2)}, u32[]{:S(2)}) collective-permute-start(bf16[40,1024]{1,0:T(8,128)(2,1)S(1)} %finish_sum.3), channel_id=1, source_target_pairs={{0,12},{1,13},{2,14},{3,15},{4,8},{5,9},{6,10},{7,11}} | collective-permute-start | bytes 245768 | tf_op jit(solution)/shard_map/ppermute | solution.py:37
  33.8 1.9 %collective-permute-start.13 = (bf16[40,1024]{1,0:T(8,128)(2,1)S(1)}, bf16[40,1024]{1,0:T(8,128)(2,1)S(1)}, u32[]{:S(2)}, u32[]{:S(2)}) collective-permute-start(bf16[40,1024]{1,0:T(8,128)(2,1)S(1)} %finish_sum.3), channel_id=1, source_target_pairs={{0,10},{1,11},{2,8},{3,9},{4,14},{5,15},{6,12},{7,13}} | collective-permute-start | bytes 245768 | tf_op jit(solution)/shard_map/ppermute | solution.py:37
  38.2 1.7 %collective-permute-start.19 = (bf16[4,40,1024]{2,1,0:T(8,128)(2,1)S(1)}, bf16[4,40,1024]{2,1,0:T(8,128)(2,1)S(1)}, u32[]{:S(2)}, u32[]{:S(2)}) collective-permute-start(bf16[4,40,1024]{2,1,0:T(8,128)(2,1)S(1)} %get-tuple-element.49), channel_id=1, source_target_pairs={{0,1},{1,0},{2,3},{3,2},{4,5},{5,4},{6,7},{7,6},{8,9},{9,8},{10,11... | collective-permute-start | bytes 983048 | tf_op jit(solution)/shard_map/ppermute | solution.py:25
  39.9 5.1 %collective-permute-start.20 = (bf16[40,1024]{1,0:T(8,128)(2,1)S(1)}, bf16[40,1024]{1,0:T(8,128)(2,1)S(1)}, u32[]{:S(2)}, u32[]{:S(2)}) collective-permute-start(bf16[40,1024]{1,0:T(8,128)(2,1)S(1)} %get-tuple-element.51), channel_id=1, source_target_pairs={{0,2},{1,3},{2,0},{3,1},{4,6},{5,7},{6,4},{7,5},{8,10},{9,11},{10,... | collective-permute-start | bytes 245768 | tf_op jit(solution)/shard_map/ppermute | solution.py:25
  40.5 4.8 %collective-permute-start.21 = (bf16[40,1024]{1,0:T(8,128)(2,1)S(1)}, bf16[40,1024]{1,0:T(8,128)(2,1)S(1)}, u32[]{:S(2)}, u32[]{:S(2)}) collective-permute-start(bf16[40,1024]{1,0:T(8,128)(2,1)S(1)} %get-tuple-element.52), channel_id=1, source_target_pairs={{0,4},{1,5},{2,6},{3,7},{4,0},{5,1},{6,2},{7,3},{8,12},{9,13},{10,... | collective-permute-start | bytes 245768 | tf_op jit(solution)/shard_map/ppermute | solution.py:25
  41.4 5.4 %collective-permute-start.22 = (bf16[40,1024]{1,0:T(8,128)(2,1)S(1)}, bf16[40,1024]{1,0:T(8,128)(2,1)S(1)}, u32[]{:S(2)}, u32[]{:S(2)}) collective-permute-start(bf16[40,1024]{1,0:T(8,128)(2,1)S(1)} %get-tuple-element.53), channel_id=1, source_target_pairs={{0,6},{1,7},{2,4},{3,5},{4,2},{5,3},{6,0},{7,1},{8,14},{9,15},{10,... | collective-permute-start | bytes 245768 | tf_op jit(solution)/shard_map/ppermute | solution.py:25
  46.8 2.7 %collective-permute-start.29 = (bf16[40,1024]{1,0:T(8,128)(2,1)S(1)}, bf16[40,1024]{1,0:T(8,128)(2,1)S(1)}, u32[]{:S(2)}, u32[]{:S(2)}) collective-permute-start(bf16[40,1024]{1,0:T(8,128)(2,1)S(1)} %finish_sum.4), channel_id=1, source_target_pairs={{8,22},{9,23},{10,20},{11,21},{12,18},{13,19},{14,16},{15,17}} | collective-permute-start | bytes 245768 | tf_op jit(solution)/shard_map/ppermute | solution.py:37
  47.5 2.1 %collective-permute-start.27 = (bf16[40,1024]{1,0:T(8,128)(2,1)S(1)}, bf16[40,1024]{1,0:T(8,128)(2,1)S(1)}, u32[]{:S(2)}, u32[]{:S(2)}) collective-permute-start(bf16[40,1024]{1,0:T(8,128)(2,1)S(1)} %finish_sum.4), channel_id=1, source_target_pairs={{8,20},{9,21},{10,22},{11,23},{12,16},{13,17},{14,18},{15,19}} | collective-permute-start | bytes 245768 | tf_op jit(solution)/shard_map/ppermute | solution.py:37
  48.2 1.9 %collective-permute-start.25 = (bf16[40,1024]{1,0:T(8,128)(2,1)S(1)}, bf16[40,1024]{1,0:T(8,128)(2,1)S(1)}, u32[]{:S(2)}, u32[]{:S(2)}) collective-permute-start(bf16[40,1024]{1,0:T(8,128)(2,1)S(1)} %finish_sum.4), channel_id=1, source_target_pairs={{8,18},{9,19},{10,16},{11,17},{12,22},{13,23},{14,20},{15,21}} | collective-permute-start | bytes 245768 | tf_op jit(solution)/shard_map/ppermute | solution.py:37
  52.5 1.7 %collective-permute-start.31 = (bf16[4,40,1024]{2,1,0:T(8,128)(2,1)S(1)}, bf16[4,40,1024]{2,1,0:T(8,128)(2,1)S(1)}, u32[]{:S(2)}, u32[]{:S(2)}) collective-permute-start(bf16[4,40,1024]{2,1,0:T(8,128)(2,1)S(1)} %get-tuple-element.56), channel_id=1, source_target_pairs={{0,1},{1,0},{2,3},{3,2},{4,5},{5,4},{6,7},{7,6},{8,9},{9,8},{10,11... | collective-permute-start | bytes 983048 | tf_op jit(solution)/shard_map/ppermute | solution.py:25
  54.3 4.8 %collective-permute-start.32 = (bf16[40,1024]{1,0:T(8,128)(2,1)S(1)}, bf16[40,1024]{1,0:T(8,128)(2,1)S(1)}, u32[]{:S(2)}, u32[]{:S(2)}) collective-permute-start(bf16[40,1024]{1,0:T(8,128)(2,1)S(1)} %get-tuple-element.58), channel_id=1, source_target_pairs={{0,2},{1,3},{2,0},{3,1},{4,6},{5,7},{6,4},{7,5},{8,10},{9,11},{10,... | collective-permute-start | bytes 245768 | tf_op jit(solution)/shard_map/ppermute | solution.py:25
  55.8 4.4 %collective-permute-start.33 = (bf16[40,1024]{1,0:T(8,128)(2,1)S(1)}, bf16[40,1024]{1,0:T(8,128)(2,1)S(1)}, u32[]{:S(2)}, u32[]{:S(2)}) collective-permute-start(bf16[40,1024]{1,0:T(8,128)(2,1)S(1)} %get-tuple-element.59), channel_id=1, source_target_pairs={{0,4},{1,5},{2,6},{3,7},{4,0},{5,1},{6,2},{7,3},{8,12},{9,13},{10,... | collective-permute-start | bytes 245768 | tf_op jit(solution)/shard_map/ppermute | solution.py:25
  57.0 5.3 %collective-permute-start.34 = (bf16[40,1024]{1,0:T(8,128)(2,1)S(1)}, bf16[40,1024]{1,0:T(8,128)(2,1)S(1)}, u32[]{:S(2)}, u32[]{:S(2)}) collective-permute-start(bf16[40,1024]{1,0:T(8,128)(2,1)S(1)} %get-tuple-element.60), channel_id=1, source_target_pairs={{0,6},{1,7},{2,4},{3,5},{4,2},{5,3},{6,0},{7,1},{8,14},{9,15},{10,... | collective-permute-start | bytes 245768 | tf_op jit(solution)/shard_map/ppermute | solution.py:25
  62.4 34.8 %collective-permute-start.41 = (bf16[40,1024]{1,0:T(8,128)(2,1)S(1)}, bf16[40,1024]{1,0:T(8,128)(2,1)S(1)}, u32[]{:S(2)}, u32[]{:S(2)}) collective-permute-start(bf16[40,1024]{1,0:T(8,128)(2,1)S(1)} %finish_sum.5), channel_id=1, source_target_pairs={{16,30},{17,31},{18,28},{19,29},{20,26},{21,27},{22,24},{23,25}} | collective-permute-start | bytes 245768 | tf_op jit(solution)/shard_map/ppermute | solution.py:37
  63.7 34.8 %collective-permute-start.39 = (bf16[40,1024]{1,0:T(8,128)(2,1)S(1)}, bf16[40,1024]{1,0:T(8,128)(2,1)S(1)}, u32[]{:S(2)}, u32[]{:S(2)}) collective-permute-start(bf16[40,1024]{1,0:T(8,128)(2,1)S(1)} %finish_sum.5), channel_id=1, source_target_pairs={{16,28},{17,29},{18,30},{19,31},{20,24},{21,25},{22,26},{23,27}} | collective-permute-start | bytes 245768 | tf_op jit(solution)/shard_map/ppermute | solution.py:37
  65.0 34.6 %collective-permute-start.37 = (bf16[40,1024]{1,0:T(8,128)(2,1)S(1)}, bf16[40,1024]{1,0:T(8,128)(2,1)S(1)}, u32[]{:S(2)}, u32[]{:S(2)}) collective-permute-start(bf16[40,1024]{1,0:T(8,128)(2,1)S(1)} %finish_sum.5), channel_id=1, source_target_pairs={{16,26},{17,27},{18,24},{19,25},{20,30},{21,31},{22,28},{23,29}} | collective-permute-start | bytes 245768 | tf_op jit(solution)/shard_map/ppermute | solution.py:37
  66.3 33.7 %collective-permute-start.35 = (bf16[40,1024]{1,0:T(8,128)(2,1)S(1)}, bf16[40,1024]{1,0:T(8,128)(2,1)S(1)}, u32[]{:S(2)}, u32[]{:S(2)}) collective-permute-start(bf16[40,1024]{1,0:T(8,128)(2,1)S(1)} %finish_sum.5), channel_id=1, source_target_pairs={{16,24},{17,25},{18,26},{19,27},{20,28},{21,29},{22,30},{23,31}} | collective-permute-start | bytes 245768 | tf_op jit(solution)/shard_map/ppermute | solution.py:37
  97.2 2.9 %collective-permute-start.42 = (bf16[40,1024]{1,0:T(8,128)(2,1)S(1)}, bf16[40,1024]{1,0:T(8,128)(2,1)S(1)}, u32[]{:S(2)}, u32[]{:S(2)}) collective-permute-start(bf16[40,1024]{1,0:T(8,128)(2,1)S(1)} %collective-permute-done.41.refs_11_), channel_id=1, source_target_pairs={{0,1},{1,0},{2,3},{3,2},{4,5},{5,4},{6,7},{7,6},{8,9},{9,8},{10,11... | collective-permute-start | bytes 245768 | tf_op jit(solution)/shard_map/ppermute | solution.py:25
  110.6 2.0 %collective-permute-start.44 = (bf16[4,8,8192]{2,1,0:T(8,128)(2,1)S(1)}, bf16[4,8,8192]{2,1,0:T(8,128)(2,1)S(1)}, u32[]{:S(2)}, u32[]{:S(2)}) collective-permute-start(bf16[4,8,8192]{2,1,0:T(8,128)(2,1)S(1)} %get-tuple-element.64), channel_id=1, source_target_pairs={{0,1},{1,0},{2,3},{3,2},{4,5},{5,4},{6,7},{7,6},{8,9},{9,8},{10,11... | collective-permute-start | bytes 1572872 | tf_op jit(solution)/shard_map/ppermute | solution.py:25
  110.8 5.4 %collective-permute-start.43 = (bf16[8,8192]{1,0:T(8,128)(2,1)S(1)}, bf16[8,8192]{1,0:T(8,128)(2,1)S(1)}, u32[]{:S(2)}, u32[]{:S(2)}) collective-permute-start(bf16[8,8192]{1,0:T(8,128)(2,1)S(1)} %get-tuple-element.62.x_ref), channel_id=1, source_target_pairs={{8,0},{16,8},{24,16},{9,1},{17,9},{25,17},{10,2},{18,10},{26,18},{... | collective-permute-start | bytes 393224 | tf_op jit(solution)/shard_map/ppermute | solution.py:447
  112.7 6.4 %collective-permute-start.45 = (bf16[8,8192]{1,0:T(8,128)(2,1)S(1)}, bf16[8,8192]{1,0:T(8,128)(2,1)S(1)}, u32[]{:S(2)}, u32[]{:S(2)}) collective-permute-start(bf16[8,8192]{1,0:T(8,128)(2,1)S(1)} %get-tuple-element.66), channel_id=1, source_target_pairs={{0,2},{1,3},{2,0},{3,1},{4,6},{5,7},{6,4},{7,5},{8,10},{9,11},{10,... | collective-permute-start | bytes 393224 | tf_op jit(solution)/shard_map/ppermute | solution.py:25
  113.8 8.1 %collective-permute-start.46 = (bf16[8,8192]{1,0:T(8,128)(2,1)S(1)}, bf16[8,8192]{1,0:T(8,128)(2,1)S(1)}, u32[]{:S(2)}, u32[]{:S(2)}) collective-permute-start(bf16[8,8192]{1,0:T(8,128)(2,1)S(1)} %get-tuple-element.67), channel_id=1, source_target_pairs={{0,4},{1,5},{2,6},{3,7},{4,0},{5,1},{6,2},{7,3},{8,12},{9,13},{10,... | collective-permute-start | bytes 393224 | tf_op jit(solution)/shard_map/ppermute | solution.py:25
  114.9 7.0 %collective-permute-start.47 = (bf16[8,8192]{1,0:T(8,128)(2,1)S(1)}, bf16[8,8192]{1,0:T(8,128)(2,1)S(1)}, u32[]{:S(2)}, u32[]{:S(2)}) collective-permute-start(bf16[8,8192]{1,0:T(8,128)(2,1)S(1)} %get-tuple-element.68), channel_id=1, source_target_pairs={{0,6},{1,7},{2,4},{3,5},{4,2},{5,3},{6,0},{7,1},{8,14},{9,15},{10,... | collective-permute-start | bytes 393224 | tf_op jit(solution)/shard_map/ppermute | solution.py:25
  (17 other events, 24.1 us)
